TPU v7x, 32 devices: a whole 2x2x4 slice. The times are simulated.
32 devices in a mesh: dp: 8 (over z, core), seq: 4 (over y, x).
Axes of the slice: x: 2, y: 2, z: 4, core: 2. Of those that a mesh axis runs over, the one named last changes fastest.
Arguments:
- tokens: bfloat16 [8, 1024, 2048], P('dp', 'seq'), may hold values from -6 to 6
- doc_ids: int32 [8, 1024], P('dp', 'seq'), may hold values from 0 to 1023, as said below
- pad_mask: int32 [8, 1024], P('dp', 'seq'), may hold values from 0 to 1, as said below
- attn_norm_gain: bfloat16 [2048], replicated, may hold values from 0.5 to 1.5
- attn_norm_bias: bfloat16 [2048], replicated, may hold values from -3 to 3
- qkv_weight: bfloat16 [2304, 2048], P(('dp', 'seq')), may hold values from -0.125 to 0.125
- query_bias: bfloat16 [2048], replicated, may hold values from -3 to 3
- value_bias: bfloat16 [128], replicated, may hold values from -3 to 3
- out_weight: bfloat16 [2048, 2048], P(('dp', 'seq')), may hold values from -2 to 2
- out_bias: bfloat16 [2048], replicated, may hold values from -3 to 3
- mlp_norm_gain: bfloat16 [2048], replicated, may hold values from 0.5 to 1.5
- mlp_norm_bias: bfloat16 [2048], replicated, may hold values from -3 to 3
- fc_weight: bfloat16 [8192, 2048], P(('dp', 'seq')), may hold values from -0.125 to 0.125
- fc_bias: bfloat16 [8192], replicated, may hold values from -3 to 3
- proj_weight: bfloat16 [8192, 2048], P(('dp', 'seq')), may hold values from -0.0625 to 0.0625
- proj_bias: bfloat16 [2048], replicated, may hold values from -3 to 3
- cotangent: bfloat16 [8, 1024, 2048], P('dp', 'seq'), may hold values from -6 to 6
Outputs:
- block_out: bfloat16 [8, 1024, 2048], P('dp', 'seq')
- tokens_grad: bfloat16 [8, 1024, 2048], P('dp', 'seq')
- attn_norm_gain_grad: float32 [2048], replicated
- attn_norm_bias_grad: float32 [2048], replicated
- qkv_weight_grad: float32 [2304, 2048], P(('dp', 'seq'))
- query_bias_grad: float32 [2048], replicated
- value_bias_grad: float32 [128], replicated
- out_weight_grad: float32 [2048, 2048], P(('dp', 'seq'))
- out_bias_grad: float32 [2048], replicated
- mlp_norm_gain_grad: float32 [2048], replicated
- mlp_norm_bias_grad: float32 [2048], replicated
- fc_weight_grad: float32 [8192, 2048], P(('dp', 'seq'))
- fc_bias_grad: float32 [8192], replicated
- proj_weight_grad: float32 [8192, 2048], P(('dp', 'seq'))
- proj_bias_grad: float32 [2048], replicated
Inputs may be any that keep to these rules, and one draw needn't show every extreme that they name: `doc_ids`: along each row the ids never fall. In every row one document begins within the first 256 positions and ends within the last 256. Padding positions carry the id 1024 - 1. `pad_mask`: every row ends with a run of zeros, 1 to 255 long, and all its other positions are 1.
All inputs are finite; a program needn't handle non-finite values.
Results may differ from a plain program's by a relative error of at most 0.015.
Values may be sent and summed in bfloat16 or wider, within the bound.
No kernel may reach another device: no remote copies, remote signals or barrier semaphores. Data moves between devices by JAX's collectives and lax.ppermute only.
A program may use at most 256 MiB of HBM per device.

v0:
```python
import math

import jax
import jax.numpy as jnp
from jax import lax
from jax.sharding import PartitionSpec as P

HEADS = 16
HDIM = 128


EPSILON = 1e-05
NEGATIVE = -1e30
PRECISE = lax.Precision.HIGHEST


def contract_rows(left, right):
    return lax.dot_general(
        left, right, (((1,), (1,)), ((), ())), preferred_element_type=jnp.float32
    )


def contract_cols(left, right):
    return lax.dot_general(
        left, right, (((0,), (0,)), ((), ())), preferred_element_type=jnp.float32
    )


def normalize(values):
    center = jnp.mean(values, -1, keepdims=True)
    shifted = values - center
    inverse = lax.rsqrt(jnp.mean(shifted * shifted, -1, keepdims=True) + EPSILON)
    return (shifted * inverse, inverse)


def norm_back(grad_normed, normed, inverse):
    first_mean = jnp.mean(grad_normed, -1, keepdims=True)
    second_mean = jnp.mean(grad_normed * normed, -1, keepdims=True)
    return inverse * (grad_normed - first_mean - normed * second_mean)


def gelu_tanh(values):
    return jax.nn.gelu(values, approximate=True)


def shards(
    tokens,
    doc_ids,
    pad_mask,
    attn_norm_gain,
    attn_norm_bias,
    qkv_weight,
    query_bias,
    value_bias,
    out_weight,
    out_bias,
    mlp_norm_gain,
    mlp_norm_bias,
    fc_weight,
    fc_bias,
    proj_weight,
    proj_bias,
    cotangent,
):
    row_count, tok_count, width = tokens.shape
    token_count = row_count * tok_count
    scale = HDIM ** (-0.5)
    seq_index = lax.axis_index("seq")
    seq_size = lax.axis_size("seq")
    dp_size = lax.axis_size("dp")
    seq_len = tok_count * seq_size
    block_len = math.gcd(seq_len, 512)
    block_count = seq_len // block_len
    query_first = seq_index * tok_count
    query_pos = query_first + jnp.arange(tok_count, dtype=jnp.int32)
    query_last = query_first + tok_count - 1
    gain_one = attn_norm_gain.astype(jnp.float32)
    shift_one = attn_norm_bias.astype(jnp.float32)
    query_shift = query_bias.astype(jnp.float32)
    value_shift = value_bias.astype(jnp.float32)
    out_shift = out_bias.astype(jnp.float32)
    gain_two = mlp_norm_gain.astype(jnp.float32)
    shift_two = mlp_norm_bias.astype(jnp.float32)
    fc_shift = fc_bias.astype(jnp.float32)
    proj_shift = proj_bias.astype(jnp.float32)

    def admitted(key_pos, key_doc, key_live):
        causal = key_pos[None, None, :] <= query_pos[None, :, None]
        same_doc = key_doc[:, None, :] == doc_ids[:, :, None]
        usable = (key_live[:, None, :] == 1) | (key_pos[None, None, :] == query_pos[None, :, None])
        return (causal & same_doc & usable)[:, :, None, :]

    flat = tokens.reshape(token_count, width).astype(jnp.float32)
    normed_one, inverse_one = normalize(flat)
    hidden_one = (normed_one * gain_one + shift_one).astype(jnp.bfloat16)
    qkv = contract_rows(hidden_one, lax.all_gather(qkv_weight, ("dp", "seq"), axis=0, tiled=True))
    query = (
        (qkv[:, :width] + query_shift)
        .astype(jnp.bfloat16)
        .reshape(row_count, tok_count, HEADS, HDIM)
    )
    keys = qkv[:, width : width + HDIM].astype(jnp.bfloat16).reshape(row_count, tok_count, HDIM)
    values = (
        (qkv[:, width + HDIM :] + value_shift)
        .astype(jnp.bfloat16)
        .reshape(row_count, tok_count, HDIM)
    )

    def key_scores(key_block):
        return (
            jnp.einsum("rthd,rpd->rthp", query, key_block, preferred_element_type=jnp.float32)
            * scale
        )

    start_state = (
        jnp.full((row_count, tok_count, HEADS), NEGATIVE, jnp.float32),
        jnp.zeros((row_count, tok_count, HEADS), jnp.float32),
        jnp.zeros((row_count, tok_count, HEADS, HDIM), jnp.float32),
    )
    key_block = lax.all_gather(keys, "seq", axis=1, tiled=True)
    value_block = lax.all_gather(values, "seq", axis=1, tiled=True)
    doc_block = lax.all_gather(doc_ids, "seq", axis=1, tiled=True)
    live_block = lax.all_gather(pad_mask, "seq", axis=1, tiled=True)
    key_pos = jnp.arange(key_block.shape[1], dtype=jnp.int32)

    def attend_visit(state):
        running_max, running_sum, weighted = state
        allowed = admitted(key_pos, doc_block, live_block)
        scores = jnp.where(allowed, key_scores(key_block), NEGATIVE)
        new_max = jnp.maximum(running_max, jnp.max(scores, -1))
        weights = jnp.where(allowed, jnp.exp(scores - new_max[..., None]), 0.0)
        running_sum = jnp.sum(weights, -1)
        weighted = jnp.einsum(
            "rthp,rpd->rthd", weights, value_block.astype(jnp.float32), precision=PRECISE
        )
        return (new_max, running_sum, weighted)

    final_state = lax.cond(
        jnp.int32(0) <= query_last, attend_visit, lambda state: state, start_state
    )
    running_max, running_sum, weighted = final_state
    attn = weighted / running_sum[..., None]
    log_total = running_max + jnp.log(running_sum)
    attn_low = attn.reshape(token_count, width).astype(jnp.bfloat16)
    branch = contract_rows(attn_low, lax.all_gather(out_weight, ("dp", "seq"), axis=0, tiled=True))
    middle = flat + branch + out_shift
    normed_two, inverse_two = normalize(middle)
    hidden_two = (normed_two * gain_two + shift_two).astype(jnp.bfloat16)
    grad_out = cotangent.reshape(token_count, width).astype(jnp.float32)
    grad_low = grad_out.astype(jnp.bfloat16)
    fc_block = lax.all_gather(fc_weight, ("dp", "seq"), axis=0, tiled=True)
    proj_block = lax.all_gather(proj_weight, ("dp", "seq"), axis=0, tiled=True)
    pre = contract_rows(hidden_two, fc_block) + fc_shift
    act = gelu_tanh(pre).astype(jnp.bfloat16)
    mlp = jnp.dot(act, proj_block, preferred_element_type=jnp.float32)

    def as_rows(member):
        return member.reshape(row_count, tok_count, width)

    row_hidden_one, row_attn, row_hidden_two, row_grad_low = (
        lax.all_gather(as_rows(hidden_one), "seq", axis=1, tiled=True),
        lax.all_gather(as_rows(attn_low), "seq", axis=1, tiled=True),
        lax.all_gather(as_rows(hidden_two), "seq", axis=1, tiled=True),
        lax.all_gather(as_rows(grad_low), "seq", axis=1, tiled=True),
    )
    fc_block = lax.all_gather(fc_weight, ("dp", "seq"), axis=0, tiled=True)
    proj_block = lax.all_gather(proj_weight, ("dp", "seq"), axis=0, tiled=True)
    pre = contract_rows(hidden_two, fc_block) + fc_shift
    act = gelu_tanh(pre).astype(jnp.bfloat16)
    grad_act = contract_rows(grad_low, proj_block)
    slope = jax.vjp(gelu_tanh, pre)[1]
    grad_pre = slope(grad_act)[0]
    grad_pre_low = grad_pre.astype(jnp.bfloat16)
    grad_hidden = jnp.dot(grad_pre_low, fc_block, preferred_element_type=jnp.float32)
    grad_pre_all = grad_pre_low
    act_all = act
    fc_bias_sum = jnp.sum(grad_pre, 0)
    grad_hidden_two, grad_pre_all, act_all, fc_bias_grad = (
        grad_hidden,
        grad_pre_all,
        act_all,
        fc_bias_sum,
    )
    block_out = (middle + mlp + proj_shift).astype(jnp.bfloat16).reshape(tokens.shape)
    grad_middle = grad_out + norm_back(grad_hidden_two * gain_two, normed_two, inverse_two)
    grad_middle_low = grad_middle.astype(jnp.bfloat16)
    columns = grad_middle_low
    grad_attn = jnp.dot(
        columns,
        lax.all_gather(out_weight, ("dp", "seq"), axis=0, tiled=True),
        preferred_element_type=jnp.float32,
    )
    grad_attn_low = grad_attn.astype(jnp.bfloat16).reshape(row_count, tok_count, HEADS, HDIM)
    grad_attn_wide = grad_attn_low.astype(jnp.float32)
    delta = jnp.sum(grad_attn_wide * attn, -1)
    all_keys, all_values, all_docs, all_live = (
        lax.all_gather(keys, "seq", axis=1, tiled=True),
        lax.all_gather(values, "seq", axis=1, tiled=True),
        lax.all_gather(doc_ids, "seq", axis=1, tiled=True),
        lax.all_gather(pad_mask, "seq", axis=1, tiled=True),
    )

    def back_step(state, block_index):
        grad_query, grad_keys_all, grad_values_all = state
        start = block_index * block_len
        key_block = lax.dynamic_slice_in_dim(all_keys, start, block_len, 1)
        value_block = lax.dynamic_slice_in_dim(all_values, start, block_len, 1)
        doc_block = lax.dynamic_slice_in_dim(all_docs, start, block_len, 1)
        live_block = lax.dynamic_slice_in_dim(all_live, start, block_len, 1)
        key_pos = start + jnp.arange(block_len, dtype=jnp.int32)

        def back_visit(grad_now):
            allowed = admitted(key_pos, doc_block, live_block)
            scores = jnp.where(allowed, key_scores(key_block), NEGATIVE)
            probs = jnp.where(allowed, jnp.exp(scores - log_total[..., None]), 0.0)
            grad_probs = jnp.einsum(
                "rthd,rpd->rthp", grad_attn_low, value_block, preferred_element_type=jnp.float32
            )
            grad_scores = (probs * (grad_probs - delta[..., None])).astype(jnp.bfloat16)
            new_grad = (
                grad_now
                + jnp.einsum(
                    "rthp,rpd->rthd", grad_scores, key_block, preferred_element_type=jnp.float32
                )
                * scale
            )
            key_part = (
                jnp.einsum("rthp,rthd->rpd", grad_scores, query, preferred_element_type=jnp.float32)
                * scale
            )
            value_part = jnp.einsum("rthp,rthd->rpd", probs, grad_attn_wide, precision=PRECISE)
            return (new_grad, key_part, value_part)

        def skip(grad_now):
            empty = jnp.zeros((row_count, block_len, HDIM), jnp.float32)
            return (grad_now, empty, empty)

        grad_query, key_part, value_part = lax.cond(
            start <= query_last, back_visit, skip, grad_query
        )
        grad_keys_all = lax.dynamic_update_slice_in_dim(grad_keys_all, key_part, start, 1)
        grad_values_all = lax.dynamic_update_slice_in_dim(grad_values_all, value_part, start, 1)
        return ((grad_query, grad_keys_all, grad_values_all), None)

    scan_start = (
        jnp.zeros((row_count, tok_count, HEADS, HDIM), jnp.float32),
        jnp.zeros((row_count, seq_len, HDIM), jnp.float32),
        jnp.zeros((row_count, seq_len, HDIM), jnp.float32),
    )
    (grad_query, grad_keys_all, grad_values_all), unused_back = lax.scan(
        back_step, scan_start, jnp.arange(block_count, dtype=jnp.int32)
    )
    grad_keys, grad_values = (
        lax.psum_scatter(
            grad_keys_all.astype(jnp.bfloat16), "seq", scatter_dimension=1, tiled=True
        ).astype(jnp.float32),
        lax.psum_scatter(
            grad_values_all.astype(jnp.bfloat16), "seq", scatter_dimension=1, tiled=True
        ).astype(jnp.float32),
    )
    grad_query_flat = grad_query.reshape(token_count, width)
    grad_values_flat = grad_values.reshape(token_count, HDIM)
    grad_qkv = jnp.concatenate(
        [grad_query_flat, grad_keys.reshape(token_count, HDIM), grad_values_flat], 1
    ).astype(jnp.bfloat16)
    columns = grad_qkv
    grad_hidden_one = jnp.dot(
        columns,
        lax.all_gather(qkv_weight, ("dp", "seq"), axis=0, tiled=True),
        preferred_element_type=jnp.float32,
    )

    def owner_columns(member):
        return member.reshape(row_count, tok_count, dp_size, seq_size, -1)

    received = (
        lax.all_to_all(
            owner_columns(grad_middle_low), "seq", split_axis=3, concat_axis=1, tiled=True
        ),
        lax.all_to_all(owner_columns(grad_qkv), "seq", split_axis=3, concat_axis=1, tiled=True),
        lax.all_to_all(owner_columns(grad_pre_all), "seq", split_axis=3, concat_axis=1, tiled=True),
        lax.all_to_all(owner_columns(act_all), "seq", split_axis=3, concat_axis=1, tiled=True),
    )
    column_sets = tuple((member.reshape(row_count * seq_len, -1) for member in received))
    partners = tuple(
        (
            member.reshape(row_count * seq_len, width)
            for member in (row_attn, row_hidden_one, row_hidden_two, row_grad_low)
        )
    )
    group_rows = tuple((member.shape[1] // dp_size for member in column_sets))
    rows_kept = sum(group_rows)
    blocks = rows_kept * lax.axis_size("dp") // rows_kept
    parts = []
    for columns, partner, group in zip(column_sets, partners, group_rows):
        parts.append(contract_cols(columns, partner).reshape(blocks, group, width))
    owned = lax.psum_scatter(
        jnp.concatenate(parts, 1)
        .reshape(rows_kept * lax.axis_size("dp"), width)
        .astype(jnp.bfloat16),
        "dp",
        scatter_dimension=0,
        tiled=True,
    ).astype(jnp.float32)
    out_end = group_rows[0]
    qkv_end = out_end + group_rows[1]
    fc_end = qkv_end + group_rows[2]
    out_grad = owned[:out_end]
    qkv_grad = owned[out_end:qkv_end]
    fc_grad = owned[qkv_end:fc_end]
    proj_grad = owned[fc_end:]
    tokens_grad = (
        (grad_middle + norm_back(grad_hidden_one * gain_one, normed_one, inverse_one))
        .astype(jnp.bfloat16)
        .reshape(tokens.shape)
    )
    sums = lax.psum(
        (
            jnp.sum(grad_hidden_one * normed_one, 0),
            jnp.sum(grad_hidden_one, 0),
            jnp.sum(grad_query_flat, 0),
            jnp.sum(grad_values_flat, 0),
            jnp.sum(grad_middle, 0),
            jnp.sum(grad_hidden_two * normed_two, 0),
            jnp.sum(grad_hidden_two, 0),
            fc_bias_grad,
            jnp.sum(grad_out, 0),
        ),
        ("dp", "seq"),
    )
    return (
        block_out,
        tokens_grad,
        sums[0],
        sums[1],
        qkv_grad,
        sums[2],
        sums[3],
        out_grad,
        sums[4],
        sums[5],
        sums[6],
        fc_grad,
        sums[7],
        proj_grad,
        sums[8],
    )


def solution(mesh):
    return jax.shard_map(
        shards,
        mesh=mesh,
        in_specs=(
            P("dp", "seq", None),
            P("dp", "seq"),
            P("dp", "seq"),
            P(),
            P(),
            P(("dp", "seq"), None),
            P(),
            P(),
            P(("dp", "seq"), None),
            P(),
            P(),
            P(),
            P(("dp", "seq"), None),
            P(),
            P(("dp", "seq"), None),
            P(),
            P("dp", "seq", None),
        ),
        out_specs=(
            P("dp", "seq", None),
            P("dp", "seq", None),
            P(),
            P(),
            P(("dp", "seq"), None),
            P(),
            P(),
            P(("dp", "seq"), None),
            P(),
            P(),
            P(),
            P(("dp", "seq"), None),
            P(),
            P(("dp", "seq"), None),
            P(),
        ),
        check_vma=False,
    )
```

profile of v0, /device:TPU:0, one launch (start us, length us, event | category | flops | bytes accessed | tf_op | source)
XLA Modules:
  0.0 1422.8 jit_solution(11143816160878280088)
XLA Ops:
  15.6 9.6 all_gather.44
  25.2 7.9 all_gather.45
  35.0 60.7 %all-gather.12.cloned.1.call-done = bf16[2304,2048]{1,0:T(8,128)(2,1)} async-done(((bf16[72,2048]{1,0:T(8,128)(2,1)}), bf16[2304,2048]{1,0:T(8,128)(2,1)}) %all-gather.12.cloned.1.call-update) | async-done | bytes 9437200 | tf_op jit(solution)/shard_map/all_gather | solution.py:96
  103.0 10.0 all-gather.1
  113.0 8.7 all-gather
  121.8 25.7 %conditional.2 = (f32[1,256,16]{1,2,0:T(8,128)}, f32[1,256,16,128]{1,3,2,0:T(8,128)S(1)}, f32[1,256,16]{1,2,0:T(8,128)}) conditional(s32[]{:T(128)} %convert_element_type.145, () %tuple.32, (s32[1024]{0:T(1024)S(1)}, s32[1024]{0:T(1024)S(1)}, s32[]{:T(128)}, s32[1,1024]{1,0:T(1,128)S(1)}, s32[1,256]{1,0:T(1,128)}, ...), branch_computations={%region_2.0_spmd.clone, %region_3.6_spmd.clone} | conditional | flops 7568102400 | bytes 55220252 | solution.py:138
  134.2 13.3 fusion.45
  149.6 25.8 %all-gather.14.cloned.1.call-done = bf16[2048,2048]{1,0:T(8,128)(2,1)} async-done(((bf16[64,2048]{1,0:T(8,128)(2,1)}), bf16[2048,2048]{1,0:T(8,128)(2,1)}) %all-gather.14.cloned.1.call-update) | async-done | bytes 8388624 | tf_op jit(solution)/shard_map/all_gather | solution.py:145
  184.7 187.1 %all-gather.16.cloned.1.call-done = bf16[8192,2048]{1,0:T(8,128)(2,1)} async-done(((bf16[256,2048]{1,0:T(8,128)(2,1)}), bf16[8192,2048]{1,0:T(8,128)(2,1)}) %all-gather.16.cloned.1.call-update) | async-done | bytes 33554448 | tf_op jit(solution)/shard_map/all_gather | solution.py:151
  371.7 21.8 %multiply_convert_fusion = (bf16[256,8192]{1,0:T(8,128)(2,1)}, f32[256,8192]{1,0:T(8,128)}) fusion(f32[8192]{0:T(1024)S(1)} %convert_element_type.159, bf16[256,2048]{1,0:T(8,128)(2,1)} %add_convert_fusion, bf16[8192,2048]{1,0:T(8,128)(2,1)} %all-gather.16.cloned.1.call-done), kind=kOutput, calls=%fused_computation.76 | convolution fusion | flops 8610906112 | bytes 47218688 | tf_op jit(solution)/shard_map/dot_general | solution.py:18
  393.6 173.9 %all-gather.18.cloned.1.call-done = bf16[8192,2048]{1,0:T(8,128)(2,1)} async-done(((bf16[256,2048]{1,0:T(8,128)(2,1)}), bf16[8192,2048]{1,0:T(8,128)(2,1)}) %all-gather.18.cloned.1.call-update) | async-done | bytes 33554448 | tf_op jit(solution)/shard_map/all_gather | solution.py:152
  567.5 21.7 %fusion.114 = (f32[8192]{0:T(1024)}, bf16[256,8192]{1,0:T(8,128)(2,1)}) fusion(f32[256,8192]{1,0:T(8,128)} %get-tuple-element.503, bf16[8192,2048]{1,0:T(8,128)(2,1)} %all-gather.18.cloned.1.call-done, bf16[1,256,2048]{2,1,0:T(8,128)(2,1)} %param.39), kind=kOutput, calls=%fused_computation.157 | convolution fusion | flops 8633966592 | bytes 47218688 | tf_op jit(solution)/shard_map/dot_general | solution.py:18
  589.2 19.1 %multiply_reduce_fusion = (f32[2048]{0:T(1024)}, f32[256]{0:T(256)S(1)}, f32[256]{0:T(256)S(1)}, f32[2048]{0:T(1024)}, f32[256,2048]{1,0:T(8,128)}) fusion(f32[256,2048]{1,0:T(8,128)} %copy-done, f32[256]{0:T(256)S(1)} %add_rsqrt_fusion, f32[256]{0:T(256)S(1)} %broadcast_multiply_fusion.4, f32[2048]{0:T(1024)S(1)} %convert_element_type.156, ...), kind=kOutput, calls=%fused_computation.122 | convolution fusion | flops 8594649088 | bytes 41971712 | tf_op jit(solution)/shard_map/dot_general | solution.py:174
  631.8 27.2 %while.18 = (s32[]{:T(128)}, f32[1,256,16,128]{3,1,2,0:T(8,128)S(1)}, bf16[1,1024,128]{1,2,0:T(8,128)(2,1)}, bf16[1,1024,128]{1,2,0:T(8,128)(2,1)}, s32[2]{0:T(1...) while((s32[]{:T(128)}, ...), condition=%wide.region_14.15_spmd.clone, body=%wide.region_11.14_spmd.clone.sunk | while | flops 5393744896 | bytes 61940196 | solution.py:250
  634.0 20.6 %conditional.5 = (f32[1,256,16,128]{3,1,2,0:T(8,128)S(1)}, bf16[1,512,128]{2,1,0:T(8,128)(2,1)S(1)}, bf16[1,512,128]{2,1,0:T(8,128)(2,1)S(1)}) conditional(s32[]{:T(128)} %convert_element_type.258, f32[1,256,16,128]{3,1,2,0:T(8,128)S(1)} %get-tuple-element.656, (s32[]{:T(128)}, s32[512]{0:T(512)S(1)}, s32[]{:T(128)}, s32[1,1024]{1,0:T(1,128)S(1)}, ...), branch_computations={%region_12.12_spmd, %region_13.13_spmd} | conditional | flops 5393744896 | bytes 60887648 | solution.py:238
  645.8 8.8 fusion.16
  669.5 23.3 %all-to-all-start = ((bf16[1,256,8,4,64]{1,4,2,0,3:T(8,128)(2,1)}), bf16[1,256,8,4,64]{1,4,2,0,3:T(8,128)(2,1)}, u32[]{:S(2)}, u32[]{:S(2)}) async-start(bf16[1,256,8,4,64]{1,4,2,0,3:T(8,128)(2,1)} %copy.90), calls=%async_computation.2 | async-start | bytes 2097152 | tf_op jit(solution)/shard_map/all_to_all | solution.py:277
  694.2 11.0 reduce-scatter.8.cloned.1.call-done
  705.2 29.0 %reduce-scatter.6.cloned.1.call-done = bf16[1,256,128]{1,2,0:T(8,128)(2,1)} async-done(((bf16[1,1024,128]{1,2,0:T(8,128)(2,1)}), bf16[1,256,128]{1,2,0:T(8,128)(2,1)}) %reduce-scatter.6.cloned.1.call-update) | async-done | bytes 65552 | tf_op jit(solution)/shard_map/reduce_scatter | solution.py:254
  740.9 8.1 reshape.624
  753.6 12.9 all-to-all-done.1
  772.0 8.0 reshape.628
  784.7 52.3 %all-to-all-done.2 = bf16[1,256,8,4,256]{4,2,1,0,3:T(8,128)(2,1)} async-done(((bf16[1,256,8,4,256]{4,2,1,0,3:T(8,128)(2,1)}), bf16[1,256,8,4,256]{4,2,1,0,3:T(8,128)(2,1)}, u32[]{:S(2)}, u32[]{:S(2)}) %all-to-all-start.2) | async-done | bytes 4194336 | tf_op jit(solution)/shard_map/all_to_all | solution.py:281
  855.3 65.1 %all-gather.22.cloned.1.call-done = bf16[1,1024,2048]{2,1,0:T(8,128)(2,1)} async-done(((bf16[1,256,2048]{2,1,0:T(8,128)(2,1)}), bf16[1,1024,2048]{2,1,0:T(8,128)(2,1)}) %all-gather.22.cloned.1.call-update) | async-done | bytes 4194320 | tf_op jit(solution)/shard_map/all_gather | solution.py:161
  951.3 24.3 %all-gather.26.cloned.1.call-done = bf16[1024,2048]{1,0:T(8,128)(2,1)} async-done(((bf16[256,2048]{1,0:T(8,128)(2,1)}), bf16[1024,2048]{1,0:T(8,128)(2,1)}) %all-gather.26.cloned.1.call-update) | async-done | bytes 4194320 | tf_op jit(solution)/shard_map/all_gather | solution.py:163
  975.6 13.9 convolution_convert_fusion.1
  989.5 40.5 %all-gather.24.cloned.1.call-done = bf16[1,1024,2048]{2,1,0:T(8,128)(2,1)} async-done(((bf16[1,256,2048]{2,1,0:T(8,128)(2,1)}), bf16[1,1024,2048]{2,1,0:T(8,128)(2,1)}) %all-gather.24.cloned.1.call-update) | async-done | bytes 4194320 | tf_op jit(solution)/shard_map/all_gather | solution.py:164
  1030.0 13.9 convolution_convert_fusion
  1044.0 17.7 %pad_maximum_fusion = bf16[8,648,2048]{2,1,0:T(8,128)(2,1)} fusion(bf16[8,256,2048]{2,1,0:T(8,128)(2,1)} %convolution_convert_fusion, bf16[8,256,2048]{2,1,0:T(8,128)(2,1)} %convolution_convert_fusion.1, bf16[8,72,2048]{2,1,0:T(8,128)(2,1)} %fusion.66, bf16[8,64,2048]{2,1,0:T(8,128)(2,1)} %fusion.69), kind=kLoop, calls=%fused_computation.66 | loop fusion | flops 84934656 | bytes 42467328 | tf_op jit(solution)/shard_map/concatenate | solution.py:298
  1063.0 18.9 %fusion.83 = bf16[1,256,2048]{2,1,0:T(8,128)(2,1)} fusion(f32[256,2048]{1,0:T(8,128)} %copy-done, bf16[256,8192]{1,0:T(8,128)(2,1)} %get-tuple-element.502, bf16[8192,2048]{1,0:T(8,128)(2,1)} %all-gather.18.cloned.1.call-done, f32[2048]{0:T(1024)S(1)} %convert_element_type.161), kind=kOutput, calls=%fused_computation.105 | convolution fusion | flops 8591507456 | bytes 40902656 | tf_op jit(solution)/shard_map/dot_general | solution.py:155
  1092.2 179.8 %reduce-scatter.10.cloned.1.call-done = bf16[648,2048]{1,0:T(8,128)(2,1)} async-done(((bf16[5184,2048]{1,0:T(8,128)(2,1)}), bf16[648,2048]{1,0:T(8,128)(2,1)}) %reduce-scatter.10.cloned.1.call-update) | async-done | bytes 2654224
  1279.7 124.5 %all-reduce.4.cloned.1.call-done = (f32[2048]{0:T(1024)}, f32[2048]{0:T(1024)}, f32[2048]{0:T(1024)}, f32[128]{0:T(128)}, f32[2048]{0:T(1024)}, /*index=5*/f32[2...) async-done(((f32[2048]{0:T(1024)}, f32[2048]{0:T(1024)}, f32[2048]{0:T(1024)}, f32[128]{0:T(128)}, f32[2048]{0:T(1024)}, /*index=5*/f32[2048]{0:T(1024)}, ...) | async-done | bytes 90640 | tf_op jit(solution)/shard_map/psum | solution.py:317
  (180 shorter events, 194.3 us)
Async XLA Ops:
  7.2 27.4 %copy-start.4 = (bf16[1,256,2048]{2,1,0:T(8,128)(2,1)S(1)}, bf16[1,256,2048]{2,1,0:T(8,128)(2,1)}, u32[]{:S(2)}) copy-start(bf16[1,256,2048]{2,1,0:T(8,128)(2,1)} %param.23) | copy-start | bytes 3145732
  7.2 88.5 %all-gather.12.cloned.1.call-start = ((), (), s32[]{:S(2)}) async-start(), calls=%async_computation.7 | async-start | bytes 9732096 | tf_op jit(solution)/shard_map/all_gather | solution.py:96
  7.9 167.5 %all-gather.14.cloned.1.call-start = ((), (), s32[]{:S(2)}) async-start(), calls=%async_computation.8 | async-start | bytes 8650752 | tf_op jit(solution)/shard_map/all_gather | solution.py:145
  8.7 363.1 %all-gather.16.cloned.1.call-start = ((), (), s32[]{:S(2)}) async-start(), calls=%async_computation.9 | async-start | bytes 34603008 | tf_op jit(solution)/shard_map/all_gather | solution.py:151
  9.4 558.0 %all-gather.18.cloned.1.call-start = ((), (), s32[]{:S(2)}) async-start(), calls=%async_computation.10 | async-start | bytes 34603008 | tf_op jit(solution)/shard_map/all_gather | solution.py:152
  10.0 695.2 %reduce-scatter.8.cloned.1.call-start = ((), (), s32[]{:S(2)}) async-start(), calls=%async_computation.12 | async-start | bytes 327680 | tf_op jit(solution)/shard_map/reduce_scatter | solution.py:257
  10.7 91.4 %copy-start.12 = (f32[2048]{0:T(1024)}, f32[2048]{0:T(1024)S(1)}, u32[]{:S(2)}) copy-start(f32[2048]{0:T(1024)S(1)} %convert_element_type.146) | copy-start | bytes 24580
  11.4 90.7 %copy-start.15 = (f32[2048]{0:T(1024)}, f32[2048]{0:T(1024)S(1)}, u32[]{:S(2)}) copy-start(f32[2048]{0:T(1024)S(1)} %convert_element_type.147) | copy-start | bytes 24580
  34.6 67.6 %copy-start.16 = (f32[256]{0:T(256)}, f32[256]{0:T(256)S(1)}, u32[]{:S(2)}) copy-start(f32[256]{0:T(256)S(1)} %broadcast_multiply_fusion.5) | copy-start | bytes 3076
  35.0 67.2 %copy-start.18 = (f32[256]{0:T(256)}, f32[256]{0:T(256)S(1)}, u32[]{:S(2)}) copy-start(f32[256]{0:T(256)S(1)} %add_rsqrt_fusion.1) | copy-start | bytes 3076
  589.2 19.1 %copy-start.1 = (f32[256,2048]{1,0:T(8,128)S(1)}, f32[256,2048]{1,0:T(8,128)}, u32[]{:S(2)}) copy-start(f32[256,2048]{1,0:T(8,128)} %copy-done) | copy-start | bytes 6291460
  589.2 19.1 %copy-start.8 = (bf16[1,256,2048]{2,1,0:T(8,128)(2,1)S(1)}, bf16[1,256,2048]{2,1,0:T(8,128)(2,1)}, u32[]{:S(2)}) copy-start(bf16[1,256,2048]{2,1,0:T(8,128)(2,1)} %param.39) | copy-start | bytes 3145732
  611.8 6.9 copy-start.2
  611.9 6.8 copy-start.6
  631.8 30.2 %copy-start.13 = (f32[2048]{0:T(1024)S(1)}, f32[2048]{0:T(1024)}, u32[]{:S(2)}) copy-start(f32[2048]{0:T(1024)} %copy-done.12) | copy-start | bytes 24580
  659.0 75.1 %reduce-scatter.6.cloned.1.call-start = ((), (), s32[]{:S(2)}) async-start(), calls=%async_computation.11 | async-start | bytes 327680 | tf_op jit(solution)/shard_map/reduce_scatter | solution.py:254
  659.6 185.5 %all-gather.20.cloned.1.call-start = ((), (), s32[]{:S(2)}) async-start(), calls=%async_computation.13 | async-start | bytes 5242880 | tf_op jit(solution)/shard_map/all_gather | solution.py:162
  661.9 258.5 %all-gather.22.cloned.1.call-start = ((), (), s32[]{:S(2)}) async-start(), calls=%async_computation.14 | async-start | bytes 5242880 | tf_op jit(solution)/shard_map/all_gather | solution.py:161
  664.2 311.4 %all-gather.26.cloned.1.call-start = ((), (), s32[]{:S(2)}) async-start(), calls=%async_computation.16 | async-start | bytes 5242880 | tf_op jit(solution)/shard_map/all_gather | solution.py:163
  669.5 67.1 %all-to-all-start = ((bf16[1,256,8,4,64]{1,4,2,0,3:T(8,128)(2,1)}), bf16[1,256,8,4,64]{1,4,2,0,3:T(8,128)(2,1)}, u32[]{:S(2)}, u32[]{:S(2)}) async-start(bf16[1,256,8,4,64]{1,4,2,0,3:T(8,128)(2,1)} %copy.90), calls=%async_computation.2 | async-start | bytes 2097152 | tf_op jit(solution)/shard_map/all_to_all | solution.py:277
  736.7 29.9 %all-to-all-start.1 = ((bf16[1,256,8,4,72]{1,4,2,0,3:T(8,128)(2,1)}), bf16[1,256,8,4,72]{1,4,2,0,3:T(8,128)(2,1)}, u32[]{:S(2)}, u32[]{:S(2)}) async-start(bf16[1,256,8,4,72]{1,4,2,0,3:T(8,128)(2,1)} %copy.93), calls=%async_computation.3 | async-start | bytes 2359296 | tf_op jit(solution)/shard_map/all_to_all | solution.py:280
  766.6 70.4 %all-to-all-start.2 = ((bf16[1,256,8,4,256]{4,2,1,0,3:T(8,128)(2,1)}), bf16[1,256,8,4,256]{4,2,1,0,3:T(8,128)(2,1)}, u32[]{:S(2)}, u32[]{:S(2)}) async-start(bf16[1,256,8,4,256]{4,2,1,0,3:T(8,128)(2,1)} %copy.95), calls=%async_computation.4 | async-start | bytes 8388608 | tf_op jit(solution)/shard_map/all_to_all | solution.py:281
  771.4 258.6 %all-gather.24.cloned.1.call-start = ((), (), s32[]{:S(2)}) async-start(), calls=%async_computation.15 | async-start | bytes 5242880 | tf_op jit(solution)/shard_map/all_gather | solution.py:164
  836.9 102.3 %all-to-all-start.3 = ((bf16[1,256,8,4,256]{4,2,1,0,3:T(8,128)(2,1)}), bf16[1,256,8,4,256]{4,2,1,0,3:T(8,128)(2,1)}, u32[]{:S(2)}, u32[]{:S(2)}) async-start(bf16[1,256,8,4,256]{4,2,1,0,3:T(8,128)(2,1)} %copy.97), calls=%async_computation.5 | async-start | bytes 8388608 | tf_op jit(solution)/shard_map/all_to_all | solution.py:282
  841.8 430.2 %reduce-scatter.10.cloned.1.call-start = ((), (), s32[]{:S(2)}) async-start(), calls=%async_computation.17 | async-start | bytes 23887872
  1061.7 342.6 %all-reduce.4.cloned.1.call-start = ((), (), s32[]{:S(2)}) async-start(), calls=%async_computation.18 | async-start | bytes 181248 | tf_op jit(solution)/shard_map/psum | solution.py:317
  1063.0 18.9 %copy-start.11 = (bf16[1,256,128]{1,2,0:T(8,128)(2,1)S(1)}, bf16[1,256,128]{1,2,0:T(8,128)(2,1)}, u32[]{:S(2)}) copy-start(bf16[1,256,128]{1,2,0:T(8,128)(2,1)} %reduce-scatter.8.cloned.1.call-done) | copy-start | bytes 196612
  1063.0 19.6 %copy-start.7 = (bf16[1,256,16,128]{1,3,2,0:T(8,128)(2,1)S(1)}, bf16[1,256,16,128]{1,3,2,0:T(8,128)(2,1)}, u32[]{:S(2)}) copy-start(bf16[1,256,16,128]{1,3,2,0:T(8,128)(2,1)} %copy.86) | copy-start | bytes 3145732
  1063.0 19.6 %copy-start.14 = (bf16[1,256,128]{1,2,0:T(8,128)(2,1)S(1)}, bf16[1,256,128]{1,2,0:T(8,128)(2,1)}, u32[]{:S(2)}) copy-start(bf16[1,256,128]{1,2,0:T(8,128)(2,1)} %reduce-scatter.6.cloned.1.call-done) | copy-start | bytes 196612
  1063.0 19.6 %copy-start.17 = (f32[256]{0:T(256)S(1)}, f32[256]{0:T(256)}, u32[]{:S(2)}) copy-start(f32[256]{0:T(256)} %copy-done.16) | copy-start | bytes 3076
  1063.0 19.6 %copy-start.19 = (f32[256]{0:T(256)S(1)}, f32[256]{0:T(256)}, u32[]{:S(2)}) copy-start(f32[256]{0:T(256)} %copy-done.18) | copy-start | bytes 3076
  1082.6 7.8 copy-start.3
  (5 other events, 8.9 us)
Sparse Core Ops, SparseCore 0:
  10.9 84.7 all-gather.11
  98.6 76.8 all-gather.13
  178.3 193.3 all-gather.15
  374.5 192.9 all-gather.17
  659.1 45.9 reduce-scatter.7
  708.6 25.5 reduce-scatter.5
  736.0 101.0 all-gather.19
  839.0 81.3 all-gather.21
  922.8 52.7 all-gather.25
  977.3 52.6 all-gather.23
  1061.8 210.1 reduce-scatter.9
  1280.6 123.6 all-reduce.3
where the time goes:
time: 1430 us; the launch traced here: 1420 us
  waiting for transfers between devices  991 us (69%)
  matrix products  187 us (13%)
  local copies, waits for them, and re-layouts  103 us (7%)
  other arithmetic  50.9 us (4%)
  starting transfers between devices  37.7 us (3%)
  blocking collectives  36.3 us (3%)
  between operations  14.8 us (1%)
    all_gather x1, waiting for transfers between devices, shards(): fc_block = lax.all_gather(fc_weight, ('dp', 'seq'), axis=0, tiled=True)  187 us
    unnamed x13, waiting for transfers between devices  184 us
    all_gather x1, waiting for transfers between devices, shards(): proj_block = lax.all_gather(proj_weight, ('dp', 'seq'), axis=0, tiled=True)  174 us
    psum x1, waiting for transfers between devices, shards(): lax.psum((jnp.sum(grad_hidden_one * normed_one, 0), jnp.sum(grad_hidden_o...  125 us
    all_gather x1, waiting for transfers between devices, shards(): lax.all_gather(as_rows(hidden_one), 'seq', axis=1, tiled=True)  65.1 us
    all_gather x1, waiting for transfers between devices, shards(): lax.all_gather(qkv_weight, ('dp', 'seq'), axis=0, tiled=True)  60.7 us
    dot_general x4, matrix products, contract_rows(): lax.dot_general(left, right, (((1,), (1,)), ((), ())), preferred_element_...  56.5 us
    all_to_all x1, waiting for transfers between devices, shards(): lax.all_to_all(owner_columns(grad_pre_all), 'seq', split_axis=3, concat_a...  52.3 us
  transfers between devices with their start and end apart: 16, of which 13 were waited for; matrix products, arithmetic and copies ran while one was open for 15% of the time, Pallas kernels for 0%

commit v1 on v0

v1 whole, which is shorter than its diff:
```python
import jax
import jax.numpy as jnp
from jax import lax
from jax.experimental import pallas as pl
from jax.experimental.pallas import tpu as pltpu
from jax.sharding import PartitionSpec as P

HEADS = 16
HDIM = 128
EPSILON = 1e-05
NEGATIVE = -1e30
BF = jnp.bfloat16
F32 = jnp.float32


def dot_nt(left, right):
    return lax.dot_general(left, right, (((1,), (1,)), ((), ())), preferred_element_type=F32)


def dot_nn(left, right):
    return lax.dot_general(left, right, (((1,), (0,)), ((), ())), preferred_element_type=F32)


def dot_tn(left, right):
    return lax.dot_general(left, right, (((0,), (0,)), ((), ())), preferred_element_type=F32)


def normalize(values):
    center = jnp.mean(values, -1, keepdims=True)
    shifted = values - center
    inverse = lax.rsqrt(jnp.mean(shifted * shifted, -1, keepdims=True) + EPSILON)
    return (shifted * inverse, inverse)


def norm_back(grad_normed, normed, inverse):
    first_mean = jnp.mean(grad_normed, -1, keepdims=True)
    second_mean = jnp.mean(grad_normed * normed, -1, keepdims=True)
    return inverse * (grad_normed - first_mean - normed * second_mean)


def gelu_tanh(values):
    return jax.nn.gelu(values, approximate=True)


FREE = pl.CostEstimate(flops=0, bytes_accessed=0, transcendentals=0)
TILE = 256
ANY = pl.BlockSpec(memory_space=pl.ANY)


def call(kernel, name, out_shape, scratch, inputs):
    return pl.pallas_call(
        kernel,
        name=name,
        out_shape=out_shape,
        in_specs=[ANY] * len(inputs),
        out_specs=jax.tree.map(lambda _: ANY, out_shape),
        scratch_shapes=scratch,
        cost_estimate=FREE,
        compiler_params=pltpu.CompilerParams(vmem_limit_bytes=44 * 1024 * 1024),
    )(*inputs)


def start_rows(pieces, buffer, sems):
    copies, row = [], 0
    for index, piece in enumerate(pieces):
        count = piece.shape[0]
        copy = pltpu.make_async_copy(piece, buffer.at[pl.ds(row, count)], sems.at[index])
        copy.start()
        copies.append((row, count, copy))
        row += count
    return copies


def wait_rows(copies, first, last):
    for row, _, copy in copies:
        if first <= row < last:
            copy.wait()


def join_rows(pieces):
    rows, width = sum(p.shape[0] for p in pieces), pieces[0].shape[1]

    def kernel(*refs):
        out_ref, buffer, in_sem, out_sem = refs[len(pieces) :]
        sent = []
        for index, (row, count, copy) in enumerate(start_rows(refs[: len(pieces)], buffer, in_sem)):
            copy.wait()
            part = pl.ds(row, count)
            sent.append(pltpu.make_async_copy(buffer.at[part], out_ref.at[part], out_sem.at[index]))
            sent[-1].start()
        for copy in sent:
            copy.wait()

    return call(
        kernel,
        "join_rows",
        jax.ShapeDtypeStruct((rows, width), pieces[0].dtype),
        [
            pltpu.VMEM((rows, width), pieces[0].dtype),
            pltpu.SemaphoreType.DMA((len(pieces),)),
            pltpu.SemaphoreType.DMA((len(pieces),)),
        ],
        tuple(pieces),
    )


def row_tile(rows):
    return min(rows, 512)


def slope(values):
    inner = 0.7978845608028654 * (values + 0.044715 * values * values * values)
    curve = jnp.tanh(inner)
    return 0.5 * (1.0 + curve) + 0.5 * values * (1.0 - curve * curve) * 0.7978845608028654 * (
        1.0 + 3 * 0.044715 * values * values
    )


def hidden_forward(pieces, slots, shift):
    rows, width = sum(p.shape[0] for p in pieces), pieces[0].shape[1]
    units = sum(s.shape[0] for s in slots)
    step = row_tile(rows)

    def kernel(*refs):
        piece_refs, slot_refs = refs[: len(pieces)], refs[len(pieces) : len(pieces) + len(slots)]
        shift_hbm, pre_ref, act_ref, x, w, bias, pre_buf, act_buf, x_sem, w_sem, b_sem, out_sem = refs[
            len(pieces) + len(slots) :
        ]
        w_copies = start_rows(slot_refs, w, w_sem)
        x_copies = start_rows(piece_refs, x, x_sem)
        bias_copy = pltpu.make_async_copy(shift_hbm, bias, b_sem)
        bias_copy.start()
        bias_copy.wait()
        wait_rows(x_copies, 0, rows)
        sent = []
        for tile in range(units // TILE):
            slot = tile % 2
            columns = pl.ds(tile * TILE, TILE)
            wait_rows(w_copies, tile * TILE, (tile + 1) * TILE)
            if tile >= 2:
                for copy in sent[tile - 2]:
                    copy.wait()

            @pl.loop(0, rows // step)
            def _(index):
                part = pl.ds(index * step, step)
                pre = dot_nt(x[part], w[columns]) + bias[:, columns]
                pre_buf[slot, part] = pre
                act_buf[slot, part] = gelu_tanh(pre).astype(BF)

            sent.append(
                (
                    pltpu.make_async_copy(pre_buf.at[slot], pre_ref.at[:, columns], out_sem.at[slot, 0]),
                    pltpu.make_async_copy(act_buf.at[slot], act_ref.at[:, columns], out_sem.at[slot, 1]),
                )
            )
            for copy in sent[tile]:
                copy.start()
        for pair in sent[-2:]:
            for copy in pair:
                copy.wait()

    return call(
        kernel,
        "hidden_forward",
        (jax.ShapeDtypeStruct((rows, units), F32), jax.ShapeDtypeStruct((rows, units), BF)),
        [
            pltpu.VMEM((rows, width), BF),
            pltpu.VMEM((units, width), BF),
            pltpu.VMEM((1, units), F32),
            pltpu.VMEM((2, rows, TILE), F32),
            pltpu.VMEM((2, rows, TILE), BF),
            pltpu.SemaphoreType.DMA((len(pieces),)),
            pltpu.SemaphoreType.DMA((len(slots),)),
            pltpu.SemaphoreType.DMA,
            pltpu.SemaphoreType.DMA((2, 2)),
        ],
        (*pieces, *slots, shift.reshape(1, units)),
    )


def hidden_backward(pieces, slots, pre):
    rows, width = sum(p.shape[0] for p in pieces), pieces[0].shape[1]
    units = sum(s.shape[0] for s in slots)
    step = row_tile(rows)

    def kernel(*refs):
        piece_refs, slot_refs = refs[: len(pieces)], refs[len(pieces) : len(pieces) + len(slots)]
        pre_ref, grad_ref, sum_ref, x, w, sums, pre_buf, out_buf, x_sem, w_sem, p_sem, out_sem, s_sem = refs[
            len(pieces) + len(slots) :
        ]
        w_copies = start_rows(slot_refs, w, w_sem)
        x_copies = start_rows(piece_refs, x, x_sem)
        tiles = units // TILE

        def pre_copy(tile):
            return pltpu.make_async_copy(
                pre_ref.at[:, pl.ds(tile * TILE, TILE)], pre_buf.at[tile % 2], p_sem.at[tile % 2]
            )

        pre_copy(0).start()
        wait_rows(x_copies, 0, rows)
        sent = []
        for tile in range(tiles):
            slot = tile % 2
            columns = pl.ds(tile * TILE, TILE)
            wait_rows(w_copies, tile * TILE, (tile + 1) * TILE)
            pre_copy(tile).wait()
            if tile + 1 < tiles:
                pre_copy(tile + 1).start()
            if tile >= 2:
                sent[tile - 2].wait()
            sums[:, columns] = jnp.zeros((1, TILE), F32)

            @pl.loop(0, rows // step)
            def _(index):
                part = pl.ds(index * step, step)
                grad = dot_nt(x[part], w[columns]) * slope(pre_buf[slot, part])
                out_buf[slot, part] = grad.astype(BF)
                sums[:, columns] += jnp.sum(grad, 0, keepdims=True)

            sent.append(pltpu.make_async_copy(out_buf.at[slot], grad_ref.at[:, columns], out_sem.at[slot]))
            sent[tile].start()
        last = pltpu.make_async_copy(sums, sum_ref, s_sem)
        last.start()
        for copy in sent[-2:]:
            copy.wait()
        last.wait()

    grad, sums = call(
        kernel,
        "hidden_backward",
        (jax.ShapeDtypeStruct((rows, units), BF), jax.ShapeDtypeStruct((1, units), F32)),
        [
            pltpu.VMEM((rows, width), BF),
            pltpu.VMEM((units, width), BF),
            pltpu.VMEM((1, units), F32),
            pltpu.VMEM((2, rows, TILE), F32),
            pltpu.VMEM((2, rows, TILE), BF),
            pltpu.SemaphoreType.DMA((len(pieces),)),
            pltpu.SemaphoreType.DMA((len(slots),)),
            pltpu.SemaphoreType.DMA((2,)),
            pltpu.SemaphoreType.DMA((2,)),
            pltpu.SemaphoreType.DMA,
        ],
        (*pieces, *slots, pre),
    )
    return grad, sums.reshape(units)


def hidden_sum(lefts, slots, tok, order, cuts):
    rows = lefts[0].shape[0]
    half = lefts[0].shape[1]
    width = slots[0].shape[1]
    depth = half * len(lefts)
    wide = min(width, 1024)

    def kernel(*refs):
        left_refs, slot_refs = refs[: len(lefts)], refs[len(lefts) : len(lefts) + len(slots)]
        rest = refs[len(lefts) + len(slots) :]
        own_ref, other_refs = rest[0], rest[1 : 1 + len(order) * cuts]
        x, w, own_buf, out_buf, x_sem, w_sem, out_sem = rest[1 + len(order) * cuts :]
        x_copies = []
        for index, left in enumerate(left_refs):
            x_copies.append(pltpu.make_async_copy(left, x.at[index], x_sem.at[index]))
            x_copies[-1].start()
        w_copies = start_rows(slot_refs, w, w_sem)
        for copy in x_copies:
            copy.wait()
        wait_rows(w_copies, 0, depth)

        def product(block, columns):
            part = pl.ds(block * tok, tok)
            total = dot_nn(x[0, part], w[pl.ds(0, half), columns])
            for index in range(1, len(lefts)):
                total = total + dot_nn(x[index, part], w[pl.ds(index * half, half), columns])
            return total

        sent = []
        for count, block in enumerate(order):
            slot = count % 2
            if count >= 2:
                for copy in sent[count - 2]:
                    copy.wait()

            @pl.loop(0, width // wide)
            def _(index):
                columns = pl.ds(pl.multiple_of(index * wide, wide), wide)
                out_buf[slot, :, columns] = product(block, columns).astype(BF)

            size = tok // cuts
            sent.append(
                [
                    pltpu.make_async_copy(
                        out_buf.at[slot, pl.ds(cut * size, size)],
                        other_refs[count * cuts + cut],
                        out_sem.at[slot, cut],
                    )
                    for cut in range(cuts)
                ]
            )
            for copy in sent[count]:
                copy.start()

        @pl.loop(0, width // wide)
        def _(index):
            columns = pl.ds(pl.multiple_of(index * wide, wide), wide)
            own_buf[:, columns] = product(0, columns)

        own_copy = pltpu.make_async_copy(own_buf, own_ref, out_sem.at[2, 0])
        own_copy.start()
        for copies in sent[-2:]:
            for copy in copies:
                copy.wait()
        own_copy.wait()

    return call(
        kernel,
        "hidden_sum",
        tuple(
            [jax.ShapeDtypeStruct((tok, width), F32)]
            + [jax.ShapeDtypeStruct((tok // cuts, width), BF)] * (len(order) * cuts)
        ),
        [
            pltpu.VMEM((len(lefts), rows, half), BF),
            pltpu.VMEM((depth, width), BF),
            pltpu.VMEM((tok, width), F32),
            pltpu.VMEM((2, tok, width), BF),
            pltpu.SemaphoreType.DMA((len(lefts),)),
            pltpu.SemaphoreType.DMA((len(slots),)),
            pltpu.SemaphoreType.DMA((3, cuts)),
        ],
        (*lefts, *slots),
    )


def weight_terms(left, pieces, outs):
    rows, units = left.shape
    width = pieces[0].shape[1]
    size = units // outs
    step = min(rows, 1024)

    def kernel(*refs):
        left_ref, piece_refs = refs[0], refs[1 : 1 + len(pieces)]
        out_refs = refs[1 + len(pieces) : 1 + len(pieces) + outs]
        l, x, out_buf, l_sem, x_sem, out_sem = refs[1 + len(pieces) + outs :]
        l_copy = pltpu.make_async_copy(left_ref, l, l_sem)
        l_copy.start()
        x_copies = start_rows(piece_refs, x, x_sem)
        l_copy.wait()
        wait_rows(x_copies, 0, rows)
        sent = []
        for tile in range(units // TILE):
            slot = tile % 2
            if tile >= 2:
                for copy in sent[tile - 2]:
                    copy.wait()

            columns = pl.ds(tile * TILE, TILE)
            wide = min(width, 1024)

            @pl.loop(0, width // wide)
            def _(index):
                span = pl.ds(pl.multiple_of(index * wide, wide), wide)
                out_buf[slot, :, span] = dot_tn(l[:, columns], x[:, span]).astype(BF)

            copies, row = [], tile * TILE
            while row < (tile + 1) * TILE:
                count = min(size - row % size, TILE)
                copies.append(
                    pltpu.make_async_copy(
                        out_buf.at[slot, pl.ds(row - tile * TILE, count)],
                        out_refs[row // size].at[pl.ds(row % size, count)],
                        out_sem.at[slot, len(copies)],
                    )
                )
                row += count
            for copy in copies:
                copy.start()
            sent.append(copies)
        for copies in sent[-2:]:
            for copy in copies:
                copy.wait()

    return call(
        kernel,
        "weight_terms",
        tuple([jax.ShapeDtypeStruct((size, width), BF)] * outs),
        [
            pltpu.VMEM((rows, units), BF),
            pltpu.VMEM((rows, width), BF),
            pltpu.VMEM((2, TILE, width), BF),
            pltpu.SemaphoreType.DMA,
            pltpu.SemaphoreType.DMA((len(pieces),)),
            pltpu.SemaphoreType.DMA((2, max(1, TILE // size))),
        ],
        (left, *pieces),
    )


def after(value, *needed):
    return lax.optimization_barrier((value, needed))[0]


def add_wide(left, right):
    return left.astype(F32) + right.astype(F32)


def add_low(left, right):
    return add_wide(left, right).astype(BF)


class Links:
    def __init__(self):
        self.seq_n = lax.axis_size("seq")
        self.dp_n = lax.axis_size("dp")
        self.z_n = self.dp_n // 2
        half = self.seq_n // 2
        self.ring = list(range(half)) + list(range(self.seq_n - 1, half - 1, -1))
        self.seq = lax.axis_index("seq")
        dp = lax.axis_index("dp")
        self.z = dp // 2
        self.core = dp % 2
        self.chips = list(range(0, self.z_n, 2)) + list(range(self.z_n - 1, 0, -2))
        self.chip_place = [self.chips.index(z) for z in range(self.z_n)]
        self.chip_pos = jnp.where(self.z % 2 == 0, self.z // 2, self.z_n - 1 - self.z // 2)
        self.place = [self.ring.index(s) for s in range(self.seq_n)]
        self.pos = jnp.where(self.seq < half, self.seq, self.seq_n - 1 + half - self.seq)

    def seq_at(self, rel):
        n, place = self.seq_n, (self.pos + rel) % self.seq_n
        return jnp.where(place < n // 2, place, n - 1 + n // 2 - place)

    def from_rel(self, value, rel):
        n = self.seq_n
        pairs = [(self.ring[(p + rel) % n], self.ring[p]) for p in range(n)]
        return lax.ppermute(value, "seq", pairs)

    def swap_core(self, value):
        pairs = [(i, i ^ 1) for i in range(self.dp_n)]
        return lax.ppermute(value, "dp", pairs)

    def z_next(self, value):
        pairs = [(self.chips[p - 1], self.chips[p]) for p in range(self.z_n)]
        return lax.ppermute(value, "dp", [(2 * i + c, 2 * j + c) for i, j in pairs for c in range(2)])

    def z_back(self, value):
        pairs = [(self.chips[p], self.chips[p - 1]) for p in range(self.z_n)]
        return lax.ppermute(value, "dp", [(2 * i + c, 2 * j + c) for i, j in pairs for c in range(2)])

    def gather_direct(self, value):
        return [value] + [self.from_rel(value, r) for r in range(1, self.seq_n)]

    def gather_near(self, value):
        if self.seq_n != 4:
            return self.gather_direct(value)
        return [value, self.from_rel(value, 1), None, self.from_rel(value, 3)]

    def gather_far(self, blocks):
        if self.seq_n != 4:
            return blocks
        half = blocks[0].shape[0] // 2
        top = self.from_rel(blocks[1][:half], 1)
        low = self.from_rel(blocks[3][half:], 3)
        return [blocks[0], blocks[1], top, low, blocks[3]]

    def exchange(self, parts):
        n = self.seq_n
        got = [parts[0]] + [None] * (n - 1)
        for r in range(1, n):
            got[n - r] = self.from_rel(parts[r], n - r)
        return got

    @property
    def sum_order(self):
        return (2, 1, 3) if self.seq_n == 4 else tuple(range(1, self.seq_n))

    @property
    def sum_cuts(self):
        return 2 if self.seq_n == 4 else 1

    def sum_far(self, parts):
        if self.seq_n != 4:
            return self.exchange(list(parts))[1:]
        far_top, far_low, right_top, right_low, left_top, left_low = parts[1:]
        return [
            self.from_rel(far_top, 3),
            self.from_rel(far_low, 1),
            self.from_rel(right_low, 3),
            self.from_rel(left_top, 1),
        ]

    def sum_near(self, parts, far, *needed):
        if self.seq_n != 4:
            return far
        return [
            self.from_rel(after(add_low(parts[3], far[0]), needed), 3),
            self.from_rel(after(add_low(parts[6], far[1]), needed), 1),
        ]

    def sum_end(self, own, far, near):
        if self.seq_n != 4:
            for member in near:
                own = own + member.astype(F32)
            return own
        half = own.shape[0] // 2
        return jnp.concatenate(
            [
                own[:half] + add_wide(near[0], far[3]),
                own[half:] + add_wide(far[2], near[1]),
            ],
            0,
        )

    def chips_ordered(self, blocks):
        n = self.z_n
        return [
            lax.select_n(self.z, *[blocks[(self.chip_place[z] - self.chip_place[k]) % n] for z in range(n)])
            for k in range(n)
        ]

    def chip_before(self, m):
        n, place = self.z_n, (self.chip_pos - m) % self.z_n
        return jnp.where(place < (n + 1) // 2, 2 * place, 2 * (n - 1 - place) + 1)

    def chip_sum(self, parts, m, came, *needed):
        return self.z_back(after(self.chip_total(parts, m, came).astype(BF), needed))

    def chip_total(self, parts, m, came):
        total = add_wide(*parts[m]) if isinstance(parts[m], tuple) else parts[m].astype(F32)
        return total if came is None else total + came.astype(F32)

    def other_seq(self, value, bit):
        return lax.ppermute(value, "seq", [(i, i ^ bit) for i in range(self.seq_n)])

    def other_dp(self, value, bit):
        return lax.ppermute(value, "dp", [(i, i ^ bit) for i in range(self.dp_n)])


def shards(
    tokens,
    doc_ids,
    pad_mask,
    attn_norm_gain,
    attn_norm_bias,
    qkv_weight,
    query_bias,
    value_bias,
    out_weight,
    out_bias,
    mlp_norm_gain,
    mlp_norm_bias,
    fc_weight,
    fc_bias,
    proj_weight,
    proj_bias,
    cotangent,
):
    links = Links()
    seq_n, dp_n, z_n = links.seq_n, links.dp_n, links.z_n
    tok = tokens.shape[1]
    width = tokens.shape[2]
    scale = HDIM ** (-0.5)
    gain_one = attn_norm_gain.astype(F32)
    shift_one = attn_norm_bias.astype(F32)
    out_shift = out_bias.astype(F32)
    gain_two = mlp_norm_gain.astype(F32)
    shift_two = mlp_norm_bias.astype(F32)
    proj_shift = proj_bias.astype(F32)

    docs = doc_ids[0]
    codes = jnp.where(pad_mask[0] == 1, docs, -1)
    codes = jnp.stack([codes // 128, codes % 128] + [jnp.zeros_like(codes)] * 14).astype(BF)

    units = fc_weight.shape[0]
    split = z_n * units

    block_index = jnp.arange(dp_n)
    owner = 2 * links.chip_before(block_index % z_n) + (links.core ^ (block_index // z_n))
    owner = owner[:, None] == jnp.arange(dp_n)[None, :]
    own_seq = jnp.arange(seq_n) == links.seq
    fc_shift = fc_bias.reshape(dp_n, seq_n, units).astype(F32)
    fc_shift = jnp.sum(jnp.where(own_seq[None, :, None], fc_shift, 0.0), 1)
    fc_shift = jnp.sum(jnp.where(owner[:, :, None], fc_shift[None], 0.0), 1).reshape(-1)
    qkv_rows = qkv_weight.shape[0]
    qkv_shift = jnp.concatenate(
        [query_bias.astype(F32), jnp.zeros((HDIM,), F32), value_bias.astype(F32)]
    ).reshape(dp_n, seq_n, qkv_rows)
    qkv_shift = jnp.sum(jnp.where(own_seq[None, :, None], qkv_shift, 0.0), 1).reshape(-1, 1)

    qkv_chips = [qkv_weight, links.z_next(qkv_weight)]
    grad_low = cotangent.reshape(tok, width)

    def norm_one(member):
        flat = member.reshape(tok, width).astype(F32)
        normed, inverse = normalize(flat)
        return (normed * gain_one + shift_one).astype(BF), normed, inverse

    hidden_one, normed_one, inverse_one = norm_one(tokens)
    ones = links.gather_near(after(hidden_one, qkv_chips[1]))
    qkv_chips[1] = after(qkv_chips[1], hidden_one)
    for _ in range(z_n - 2):
        qkv_chips.append(links.z_next(qkv_chips[-1]))
    fc_chips = [fc_weight, links.z_next(after(fc_weight, qkv_chips))]
    qkv_chips = after(qkv_chips, ones[1], ones[-1], qkv_shift, fc_shift)
    out_full = lax.all_gather(out_weight, ("dp", "seq"), axis=0, tiled=True)

    mine = jnp.stack(links.chips_ordered(qkv_chips), 0)
    other = links.swap_core(mine)

    def both_cores(mine, other):
        first = links.core == 0
        part = jnp.stack([jnp.where(first, mine, other), jnp.where(first, other, mine)], 1)
        return part.reshape(dp_n * qkv_rows, width)

    qkv_part = both_cores(mine, other)
    ones = links.gather_far(ones)

    def columns_of(part, shift, *blocks):
        return [(dot_nt(part, member) + shift).astype(BF) for member in blocks]

    far_place = seq_n // 2
    near_places = [r for r in range(seq_n) if r != far_place]
    near_columns = columns_of(qkv_part, qkv_shift, *ones[:far_place], *ones[1 - far_place :])
    far_rows = ones[far_place : far_place + len(ones) - seq_n + 1]
    far_columns = columns_of(after(qkv_part, near_columns), qkv_shift, jnp.concatenate(far_rows, 0))
    columns = dict(zip(near_places, near_columns)) | {far_place: far_columns[0]}
    got = links.exchange([columns[r] for r in range(seq_n)])

    def assemble(*got):
        got = [member.reshape(dp_n, qkv_rows, tok) for member in got]
        return jnp.stack(
            [
                lax.select_n(links.pos, *[got[(links.place[s] - p) % seq_n] for p in range(seq_n)])
                for s in range(seq_n)
            ],
            1,
        ).reshape(-1, tok)

    qkv = assemble(*got)
    query = qkv[:width].reshape(HEADS, HDIM, tok)
    pairs = links.gather_direct(jnp.concatenate([qkv[width:], codes], 0))
    fc_chips.append(links.z_next(after(fc_chips[1], pairs)))
    grads = links.gather_near(after(grad_low, pairs))

    spot = jnp.arange(tok, dtype=jnp.int32)

    def masked_scores(query, pairs):
        codes_all = [
            (member[2 * HDIM].astype(F32) * 128 + member[2 * HDIM + 1].astype(F32)).astype(jnp.int32)
            for member in pairs
        ]
        allowed = []
        for r in range(seq_n):
            place = links.seq_at(r)
            same = codes_all[r][:, None] == docs[None, :]
            if r == 0:
                allowed.append((same & (spot[:, None] < spot[None, :])) | (spot[:, None] == spot[None, :]))
            else:
                allowed.append(same & (place < links.seq))
        allowed = jnp.concatenate(allowed, 0)[None]
        keys = jnp.concatenate([member[:HDIM] for member in pairs], 1)
        values = jnp.concatenate([member[HDIM : 2 * HDIM] for member in pairs], 1)
        scores = jnp.einsum("dk,hdq->hkq", keys, query, preferred_element_type=F32) * scale
        return allowed, keys, values, jnp.where(allowed, scores, NEGATIVE)

    def attend(query, pairs):
        allowed, keys, values, scores = masked_scores(query, pairs)
        highest = jnp.max(scores, 1, keepdims=True)
        weights = jnp.where(allowed, jnp.exp(scores - highest), 0.0)
        total = jnp.sum(weights, 1, keepdims=True)
        attn = jnp.einsum("dk,hkq->hdq", values, weights.astype(BF), preferred_element_type=F32) / total
        return attn, highest + jnp.log(total), attn.reshape(width, tok).astype(BF).T

    attn, log_total, attn_low = attend(query, pairs)

    def norm_two(attn_low, out_full, tokens):
        flat = tokens.reshape(tok, width).astype(F32)
        middle = flat + dot_nt(attn_low, out_full) + out_shift
        normed, inverse = normalize(middle)
        return middle, normed, inverse, (normed * gain_two + shift_two).astype(BF)

    middle, normed_two, inverse_two, hidden_two = norm_two(attn_low, out_full, tokens)
    twos = links.gather_near(after(hidden_two, grads[1], grads[-1]))
    for _ in range(z_n - 3):
        fc_chips.append(links.z_next(after(fc_chips[-1], hidden_two)))
    proj_chips = [proj_weight, links.z_next(after(proj_weight, fc_chips[2], hidden_two))]

    twos = links.gather_far(after(twos, proj_chips))
    proj_chips.append(links.z_next(after(proj_chips[-1], twos[1], twos[-1])))
    fc_chips = after(fc_chips, twos[1], twos[-1])
    fc_other = links.swap_core(join_rows(fc_chips))
    grads = links.gather_far(after(grads, twos))

    pre_mine, act_mine = hidden_forward(twos, fc_chips, fc_shift[:split])
    ready = act_mine[:8, :HDIM]
    pre_other, act_other = hidden_forward(after(twos, ready, proj_chips), [fc_other], fc_shift[split:])
    for _ in range(z_n - 3):
        proj_chips.append(links.z_next(after(proj_chips[-1], ready)))
    attns = links.gather_near(after(attn_low, grads, ready))
    grads = after(grads, act_other)

    def core_terms(own, came):
        return [(own[m], came[m * units : (m + 1) * units]) for m in range(z_n)]

    (proj_sent,) = weight_terms(act_other, grads, 1)
    proj_came = links.swap_core(proj_sent)
    proj_own = weight_terms(after(act_mine, proj_sent, proj_chips, attns[1], attns[-1]), grads, z_n)
    proj_terms = core_terms(proj_own, proj_came)
    proj_chips = after(proj_chips, proj_own)
    proj_mine = join_rows(proj_chips)
    proj_other = links.swap_core(proj_mine)
    proj_sum = links.chip_sum(proj_terms, z_n - 1, None)
    proj_sum_first = proj_sum
    attns = links.gather_far(after(attns, proj_own))

    grad_mine, bias_mine = hidden_backward(grads, proj_chips, pre_mine)
    grad_other, bias_other = hidden_backward(after(grads, bias_mine, attns), [proj_other], pre_other)
    proj_sum = links.chip_sum(proj_terms, z_n - 2, proj_sum, grad_other)
    fc_bias_sum = jnp.concatenate([bias_mine, bias_other])
    hidden_parts = hidden_sum(
        (after(grad_mine, proj_sum_first), grad_other),
        [*fc_chips, fc_other],
        tok,
        links.sum_order,
        links.sum_cuts,
    )
    hidden_far = links.sum_far(after(hidden_parts, attns))
    (fc_sent,) = weight_terms(after(grad_other, hidden_parts, proj_sum), twos, 1)
    fc_came = links.swap_core(fc_sent)
    fc_own = weight_terms(after(grad_mine, fc_sent, hidden_far), twos, z_n)
    hidden_near = links.sum_near(hidden_parts, hidden_far)
    fc_terms = core_terms(after(fc_own, proj_sum), fc_came)
    for m in range(z_n - 3, 0, -1):
        proj_sum = links.chip_sum(proj_terms, m, proj_sum, hidden_parts)
    fc_sum = links.chip_sum(fc_terms, z_n - 1, None, proj_sum)
    mlp_parts = hidden_sum(
        (after(act_mine, fc_own, proj_sum), act_other), [proj_mine, proj_other], tok, tuple(range(1, seq_n)), 1
    )
    hidden_near = after(hidden_near, mlp_parts, proj_sum)

    def middle_back(parts, far, near, normed_two, inverse_two, grad_low):
        grad_hidden = links.sum_end(parts, far, near)
        grad_out = grad_low.astype(F32)
        grad_middle = grad_out + norm_back(grad_hidden * gain_two, normed_two, inverse_two)
        sums = [
            jnp.sum(grad_middle, 0),
            jnp.sum(grad_hidden * normed_two, 0),
            jnp.sum(grad_hidden, 0),
            jnp.sum(grad_out, 0),
        ]
        low = grad_middle.astype(BF)
        return grad_middle, low, low.T, sums

    grad_middle, grad_middle_low, grad_middle_turned, early = middle_back(hidden_parts[0], hidden_far, hidden_near, normed_two, inverse_two, grad_low
    )

    def to_owners(member, needed=()):
        member = member.reshape(dp_n, seq_n, -1, tok)
        sent = [
            lax.dynamic_index_in_dim(member, links.seq_at(r), 1, False).reshape(-1, tok) for r in range(seq_n)
        ]
        return links.exchange(after(sent, needed))

    mlp_came = [links.from_rel(mlp_parts[r], seq_n - r) for r in range(1, seq_n) if r != far_place]
    out_columns = to_owners(grad_middle_turned, mlp_came)
    proj_grad = links.chip_total(proj_terms, 0, after(proj_sum, grad_middle_low))

    def ordered_parts(columns, rows):
        part = dot_nn(jnp.concatenate(columns, 1), jnp.concatenate(rows, 0))
        part = part.reshape(z_n, 2, -1, width)
        sent = lax.dynamic_index_in_dim(part, 1 - links.core, 1, False).astype(BF)
        return sent, lax.dynamic_index_in_dim(part, links.core, 1, False)

    def ordered_terms(kept, came):
        kept = (kept + came.astype(F32)).astype(BF)
        return [lax.dynamic_index_in_dim(kept, links.chip_before(m), 0, False) for m in range(z_n)]

    def attend_back(out_full, grad_middle_low, query, pairs, attn, log_total):
        grad_attn = lax.dot_general(
            out_full, grad_middle_low, (((0,), (1,)), ((), ())), preferred_element_type=F32
        )
        grad_attn_low = grad_attn.astype(BF).reshape(HEADS, HDIM, tok)
        delta = jnp.sum(grad_attn_low.astype(F32) * attn, 1, keepdims=True)
        allowed, keys, values, scores = masked_scores(query, pairs)
        probs = jnp.where(allowed, jnp.exp(scores - log_total), 0.0)
        grad_probs = jnp.einsum("dk,hdq->hkq", values, grad_attn_low, preferred_element_type=F32)
        grad_scores = (probs * (grad_probs - delta)).astype(BF)
        grad_query = jnp.einsum("dk,hkq->hdq", keys, grad_scores, preferred_element_type=F32) * scale
        grad_keys = jnp.einsum("hkq,hdq->dk", grad_scores, query, preferred_element_type=F32) * scale
        grad_values = jnp.einsum("hkq,hdq->dk", probs.astype(BF), grad_attn_low, preferred_element_type=F32)
        grad_pair = jnp.concatenate([grad_keys, grad_values], 0)
        parts = [grad_pair[:, r * tok : (r + 1) * tok] for r in range(seq_n)]
        grad_query = grad_query.reshape(width, tok)
        return grad_query.astype(BF), jnp.sum(grad_query, 1), [parts[0]] + [part.astype(BF) for part in parts[1:]]

    grad_middle_low = after(grad_middle_low, fc_sum)
    grad_query, query_sum, parts = attend_back(out_full, grad_middle_low, query, pairs, attn, log_total
    )
    fc_sum = links.chip_sum(fc_terms, z_n - 2, fc_sum, grad_middle_low)
    came = links.exchange(parts)
    out_sent, out_kept = ordered_parts(after(out_columns, parts), attns)
    out_came = links.swap_core(out_sent)
    qkv_full = lax.all_gather(after(qkv_weight, got), ("dp", "seq"), axis=0, tiled=True)

    def all_grads(grad_query, came):
        grad_pair = came[0]
        for member in came[1:]:
            grad_pair = grad_pair + member.astype(F32)
        return jnp.concatenate([grad_query, grad_pair.astype(BF)], 0), jnp.sum(grad_pair[HDIM:], 1)

    grad_qkv, value_sum = all_grads(grad_query, after(came, out_sent))
    qkv_columns = to_owners(grad_qkv)
    out_terms = ordered_terms(after(out_kept, grad_qkv, fc_sum), out_came)
    for m in range(z_n - 3, 0, -1):
        fc_sum = links.chip_sum(fc_terms, m, fc_sum, parts)
    def tokens_back(grad_qkv, qkv_full, grad_middle, normed_one, inverse_one):
        grad_hidden = dot_tn(grad_qkv, qkv_full)
        back = grad_middle + norm_back(grad_hidden * gain_one, normed_one, inverse_one)
        return back.astype(BF), [jnp.sum(grad_hidden * normed_one, 0), jnp.sum(grad_hidden, 0)]

    tokens_grad, late = tokens_back(
        after(grad_qkv, out_terms), qkv_full, grad_middle, normed_one, inverse_one
    )
    out_sum = links.chip_sum(out_terms, z_n - 1, None, fc_sum)
    tokens_grad = tokens_grad.reshape(tokens.shape)
    fc_bias_sum = jnp.sum(jnp.where(owner[:, :, None], fc_bias_sum.reshape(dp_n, 1, units), 0.0), 0)
    fc_bias_sum = jnp.where(own_seq[None, :, None], fc_bias_sum[:, None, :], 0.0).reshape(-1)
    sums = jnp.concatenate(early + late + [query_sum, fc_bias_sum, value_sum])
    bit = 1
    while bit < seq_n:
        sums = sums + links.other_seq(sums, bit)
        bit *= 2
    mlp_came.append(links.from_rel(after(mlp_parts[far_place], sums), seq_n - far_place))
    sums = sums + links.other_dp(sums, 1)
    qkv_sent, qkv_kept = ordered_parts(after(qkv_columns, tokens_grad), ones)
    qkv_came = links.swap_core(after(qkv_sent, out_sum))
    for m in range(z_n - 2, 0, -1):
        out_sum = links.chip_sum(out_terms, m, out_sum)
    qkv_terms = ordered_terms(qkv_kept, qkv_came)
    qkv_sum = links.chip_sum(qkv_terms, z_n - 1, None)
    bit = 2
    for m in range(z_n - 2, 0, -1):
        moved = links.other_dp(sums, bit) if bit < dp_n else 0.0
        bit *= 2
        qkv_sum = links.chip_sum(qkv_terms, m, qkv_sum)
        sums = after(sums, qkv_sum) + moved
    while bit < dp_n:
        sums = sums + links.other_dp(sums, bit)
        bit *= 2
    fc_grad = links.chip_total(fc_terms, 0, after(fc_sum, qkv_terms))
    out_grad = links.chip_total(out_terms, 0, after(out_sum, fc_grad))
    mlp = sum(member.astype(F32) for member in [mlp_parts[0], *after(mlp_came, out_grad)])
    block_out = (middle + mlp + proj_shift).astype(BF).reshape(tokens.shape)
    qkv_grad = links.chip_total(qkv_terms, 0, after(qkv_sum, block_out))

    wide = [sums[i * width : (i + 1) * width] for i in range(7)]
    fc_bias_grad = sums[7 * width : 7 * width + fc_bias.shape[0]]
    value_bias_grad = sums[7 * width + fc_bias.shape[0] :]
    return (
        block_out,
        tokens_grad,
        wide[4],
        wide[5],
        qkv_grad,
        wide[6],
        value_bias_grad,
        out_grad,
        wide[0],
        wide[1],
        wide[2],
        fc_grad,
        fc_bias_grad,
        proj_grad,
        wide[3],
    )


def solution(mesh):
    rows = P(("dp", "seq"), None)
    act = P("dp", "seq", None)
    return jax.shard_map(
        shards,
        mesh=mesh,
        in_specs=(
            act,
            P("dp", "seq"),
            P("dp", "seq"),
            P(),
            P(),
            rows,
            P(),
            P(),
            rows,
            P(),
            P(),
            P(),
            rows,
            P(),
            rows,
            P(),
            act,
        ),
        out_specs=(
            act,
            act,
            P(),
            P(),
            rows,
            P(),
            P(),
            rows,
            P(),
            P(),
            P(),
            rows,
            P(),
            rows,
            P(),
        ),
        check_vma=False,
    )
```

time: 1430 us -> 677 us (0.47)
  waiting for transfers between devices: 991 us -> 270 us
  matrix products: 187 us -> 60.5 us
  Pallas kernels: 0 us -> 113 us
  starting transfers between devices: 37.7 us -> 95.2 us
  local copies, waits for them, and re-layouts: 103 us -> 54.7 us
  blocking collectives: 36.3 us -> 0 us
    all_gather x8 -> x2, waiting for transfers between devices: 577 us -> 15 us  [the longest x1 15 us: shards(): out_full = lax.all_gather(out_weight, ('dp', 'seq'), axis=0, tiled=True)]
    ppermute x0 -> x73, waiting for transfers between devices: none -> 254 us  [the longest x40 120 us: from_rel(): return lax.ppermute(value, 'seq', pairs)]
    unnamed x13 -> x2, waiting for transfers between devices: 184 us -> 0.7 us
    dot_general x19 -> x15, matrix products: 187 us -> 60.5 us  [the longest x5 11 us: dot_nt(): lax.dot_general(left, right, (((1,), (1,)), ((), ())), preferred_element_...]
    psum x1 -> x0, waiting for transfers between devices: 125 us -> none  [shards(): lax.psum((jnp.sum(grad_hidden_one * normed_one, 0), jnp.sum(grad_hidden_o...]
    pallas_call x0 -> x12, Pallas kernels: none -> 113 us  [call(): pl.pallas_call(kernel, name=name, out_shape=out_shape, in_specs=[ANY] * l...]
    ppermute x0 -> x73, starting transfers between devices: none -> 95.1 us  [the longest x40 41.2 us: from_rel(): return lax.ppermute(value, 'seq', pairs)]
    all_to_all x4 -> x0, waiting for transfers between devices: 65.2 us -> none  [the longest x1 52.3 us: shards(): lax.all_to_all(owner_columns(grad_pre_all), 'seq', split_axis=3, concat_a...]
  transfers between devices with their start and end apart: 16 -> 75, of which waited for: 13 -> 45; matrix products, arithmetic and copies ran while one was open for 15% -> 21% of each run, Pallas kernels for 0% -> 15%
where the time goes in v1:
time: 677 us; the launch traced here: 671 us
  waiting for transfers between devices  270 us (40%)
  Pallas kernels  113 us (17%)
  starting transfers between devices  95.2 us (14%)
  other arithmetic  62.1 us (9%)
  matrix products  60.5 us (9%)
  local copies, waits for them, and re-layouts  54.7 us (8%)
  between operations  16.5 us (2%)
    ppermute x40, waiting for transfers between devices, from_rel(): return lax.ppermute(value, 'seq', pairs)  120 us
    pallas_call x12, Pallas kernels, call(): pl.pallas_call(kernel, name=name, out_shape=out_shape, in_specs=[ANY] * l...  113 us
    ppermute x12, waiting for transfers between devices, z_back(): lax.ppermute(value, 'dp', [(2 * i + c, 2 * j + c) for i, j in pairs for c...  65.5 us
    ppermute x9, waiting for transfers between devices, z_next(): lax.ppermute(value, 'dp', [(2 * i + c, 2 * j + c) for i, j in pairs for c...  58.9 us
    ppermute x40, starting transfers between devices, from_rel(): return lax.ppermute(value, 'seq', pairs)  41.2 us
    ppermute x9, starting transfers between devices, z_next(): lax.ppermute(value, 'dp', [(2 * i + c, 2 * j + c) for i, j in pairs for c...  37.9 us
    unnamed x295, local copies, waits for them, and re-layouts  31.4 us
    all_gather x1, waiting for transfers between devices, shards(): out_full = lax.all_gather(out_weight, ('dp', 'seq'), axis=0, tiled=True)  15 us
  transfers between devices with their start and end apart: 75, of which 45 were waited for; matrix products, arithmetic and copies ran while one was open for 21% of the time, Pallas kernels for 15%

profile of v1, /device:TPU:0, one launch (start us, length us, event | category | flops | bytes accessed | tf_op | source)
XLA Modules:
  0.0 671.4 jit_solution(9153089562413594901)
XLA Ops:
  23.9 8.8 %collective-permute-done.1 = bf16[72,2048]{1,0:T(8,128)(2,1)S(1)} collective-permute-done((bf16[72,2048]{1,0:T(8,128)(2,1)S(1)}, bf16[72,2048]{1,0:T(8,128)(2,1)S(1)}, u32[]{:S(2)}, u32[]{:S(2)}) %collective-permute-start.1) | collective-permute-done | bytes 294944 | tf_op jit(solution)/shard_map/ppermute | solution.py:445
  77.1 7.3 %collective-permute-done.9 = bf16[576,256]{1,0:T(8,128)(2,1)S(1)} collective-permute-done((bf16[576,256]{1,0:T(8,128)(2,1)S(1)}, bf16[576,256]{1,0:T(8,128)(2,1)S(1)}, u32[]{:S(2)}, u32[]{:S(2)}) %collective-permute-start.9) | collective-permute-done | bytes 294944 | tf_op jit(solution)/shard_map/ppermute | solution.py:437
  122.6 15.0 %all-gather.3.cloned.1.call-done = bf16[2048,2048]{1,0:T(8,128)(2,1)} async-done(((bf16[64,2048]{1,0:T(8,128)(2,1)}), bf16[2048,2048]{1,0:T(8,128)(2,1)}) %all-gather.3.cloned.1.call-update) | async-done | bytes 8388624 | tf_op jit(solution)/shard_map/all_gather | solution.py:606
  137.6 6.3 fusion.107
  148.5 7.9 %collective-permute-start.23 = (bf16[256,2048]{1,0:T(8,128)(2,1)}, bf16[256,2048]{1,0:T(8,128)(2,1)S(1)}, u32[]{:S(2)}, u32[]{:S(2)}) collective-permute-start(bf16[256,2048]{1,0:T(8,128)(2,1)} %collective-permute-done.19.refs_7_.refs_2_.refs_4_), channel_id=1, source_target_pairs={{8,0},{12,4},{0,16},{4,20},{16,24},{20,28},{24,8},{28,12},{9,1},{1... | collective-permute-start | bytes 3145736 | tf_op jit(solution)/shard_map/ppermute | solution.py:445
  156.4 15.5 %collective-permute-done.20.refs_6_.refs_1_ = bf16[256,2048]{1,0:T(8,128)(2,1)} collective-permute-done((bf16[256,2048]{1,0:T(8,128)(2,1)S(1)}, bf16[256,2048]{1,0:T(8,128)(2,1)}, u32[]{:S(2)}, u32[]{:S(2)}) %collective-permute-start.20) | collective-permute-done | bytes 1048608 | tf_op jit(solution)/shard_map/ppermute | solution.py:445
  172.3 21.3 %collective-permute-done.23.refs_8_.refs_3_.refs_5_ = bf16[256,2048]{1,0:T(8,128)(2,1)S(1)} collective-permute-done((bf16[256,2048]{1,0:T(8,128)(2,1)}, bf16[256,2048]{1,0:T(8,128)(2,1)S(1)}, u32[]{:S(2)}, u32[]{:S(2)}) %collective-permute-start.23) | collective-permute-done | bytes 1048608 | tf_op jit(solution)/shard_map/ppermute | solution.py:445
  201.2 6.1 collective-permute-start.26
  221.6 9.8 %hidden_forward.2 = (f32[1024,1024]{1,0:T(8,128)}, bf16[1024,1024]{1,0:T(8,128)(2,1)}) custom-call(bf16[256,2048]{1,0:T(8,128)(2,1)S(1)} %add_convert_fusion.8.refs_0_.refs_1_, bf16[256,2048]{1,0:T(8,128)(2,1)S(1)} %copy-done.2, bf16[128,2048]{1,0:T(8,128)(2,1)} %collective-permute-done.21.refs_2_.refs_3_, ...), custom_call_target="tpu_custom_call" | custom-call | tf_op jit(solution)/shard_map/hidden_forward/pallas_call | solution.py:51
  231.5 10.4 %hidden_forward.3 = (f32[1024,1024]{1,0:T(8,128)}, bf16[1024,1024]{1,0:T(8,128)(2,1)S(1)}) custom-call(bf16[256,2048]{1,0:T(8,128)(2,1)S(1)} %add_convert_fusion.8.refs_0_.refs_1_, bf16[256,2048]{1,0:T(8,128)(2,1)S(1)} %copy-done.2, bf16[128,2048]{1,0:T(8,128)(2,1)} %collective-permute-done.21.refs_2_.refs_3_, ...), custom_call_target="tpu_custom_call" | custom-call | tf_op jit(solution)/shard_map/hidden_forward/pallas_call | solution.py:51
  242.0 9.7 %weight_terms.4 = bf16[1024,2048]{1,0:T(8,128)(2,1)} custom-call(bf16[1024,1024]{1,0:T(8,128)(2,1)S(1)} %get-tuple-element.176.refs_0_.refs_1_, bf16[256,2048]{1,0:T(8,128)(2,1)S(1)} %bitcast.197, bf16[256,2048]{1,0:T(8,128)(2,1)S(1)} %collective-permute-done.14.refs_2_.refs_1_, bf16[128,2048]{1,0:T(8,128)(2,1)S(1)} %collective-permute-done.24.refs_3_.refs_2_, ...), custom_call_target="tpu_custom_call" | custom-call | tf_op jit(solution)/shard_map/weight_terms/pallas_call | solution.py:51
  253.8 6.6 collective-permute-start.28
  260.5 16.9 %collective-permute-done.29 = bf16[256,2048]{0,1:T(8,128)(2,1)S(1)} collective-permute-done((bf16[256,2048]{0,1:T(8,128)(2,1)S(1)}, bf16[256,2048]{0,1:T(8,128)(2,1)S(1)}, u32[]{:S(2)}, u32[]{:S(2)}) %collective-permute-start.29) | collective-permute-done | bytes 1048608 | tf_op jit(solution)/shard_map/ppermute | solution.py:437
  284.5 8.6 %weight_terms.5 = (bf16[256,2048]{1,0:T(8,128)(2,1)S(1)}, bf16[256,2048]{1,0:T(8,128)(2,1)S(1)}, bf16[256,2048]{1,0:T(8,128)(2,1)S(1)}, bf16[256,2048]{1,0:T(8,128)(2,1)S(1)}) custom-call(bf16[1024,1024]{1,0:T(8,128)(2,1)} %get-tuple-element.225.refs_0_, bf16[256,2048]{1,0:T(8,128)(2,1)S(1)} %bitcast.198, ...), custom_call_target="tpu_custom_call" | custom-call | tf_op jit(solution)/shard_map/weight_terms/pallas_call | solution.py:51
  308.3 13.4 %collective-permute-done.31 = bf16[128,2048]{0,1:T(8,128)(2,1)} collective-permute-done((bf16[128,2048]{0,1:T(8,128)(2,1)}, bf16[128,2048]{0,1:T(8,128)(2,1)}, u32[]{:S(2)}, u32[]{:S(2)}) %collective-permute-start.31) | collective-permute-done | bytes 524320 | tf_op jit(solution)/shard_map/ppermute | solution.py:437
  325.0 10.7 %hidden_backward.3 = (bf16[1024,1024]{1,0:T(8,128)(2,1)S(1)}, f32[1,1024]{1,0:T(1,128)S(1)}) custom-call(bf16[256,2048]{1,0:T(8,128)(2,1)S(1)} %bitcast.199, bf16[256,2048]{1,0:T(8,128)(2,1)S(1)} %collective-permute-done.14.refs_2_.refs_1_, bf16[128,2048]{1,0:T(8,128)(2,1)S(1)} %copy-done.15, bf16[128,2048]{1,0:T(8,128)(2,1)S(1)} %copy-done.18, ...), custom_call_target="tpu_custom_call" | custom-call | tf_op jit(solution)/shard_map/hidden_backward/pallas_call | solution.py:51
  344.9 10.7 %hidden_backward.2 = (bf16[1024,1024]{1,0:T(8,128)(2,1)}, f32[1,1024]{1,0:T(1,128)S(1)}) custom-call(bf16[256,2048]{1,0:T(8,128)(2,1)S(1)} %bitcast.200, bf16[256,2048]{1,0:T(8,128)(2,1)S(1)} %collective-permute-done.14.refs_2_.refs_1_, bf16[128,2048]{1,0:T(8,128)(2,1)S(1)} %copy-done.16, bf16[128,2048]{1,0:T(8,128)(2,1)S(1)} %copy-done.19, ...), custom_call_target="tpu_custom_call" | custom-call | tf_op jit(solution)/shard_map/hidden_backward/pallas_call | solution.py:51
  355.7 14.7 %hidden_sum.2 = (f32[256,2048]{1,0:T(8,128)S(1)}, bf16[128,2048]{1,0:T(8,128)(2,1)S(1)}, bf16[128,2048]{1,0:T(8,128)(2,1)S(1)}, bf16[128,2048]{1,0:T(8,128)(2,1)...) custom-call(bf16[1024,1024]{1,0:T(8,128)(2,1)} %get-tuple-element.219.refs_0_, ...), custom_call_target="tpu_custom_call" | custom-call | tf_op jit(solution)/shard_map/hidden_sum/pallas_call | solution.py:51
  370.4 7.1 %collective-permute-done.36 = bf16[256,2048]{1,0:T(8,128)(2,1)} collective-permute-done((bf16[256,2048]{1,0:T(8,128)(2,1)}, bf16[256,2048]{1,0:T(8,128)(2,1)}, u32[]{:S(2)}, u32[]{:S(2)}) %collective-permute-start.36) | collective-permute-done | bytes 1048608 | tf_op jit(solution)/shard_map/ppermute | solution.py:449
  377.6 8.6 %weight_terms.6 = bf16[1024,2048]{1,0:T(8,128)(2,1)} custom-call(bf16[1024,1024]{1,0:T(8,128)(2,1)S(1)} %copy-done.24, bf16[256,2048]{1,0:T(8,128)(2,1)S(1)} %add_convert_fusion.8.refs_0_.refs_1_, bf16[256,2048]{1,0:T(8,128)(2,1)S(1)} %copy-done.3, bf16[128,2048]{1,0:T(8,128)(2,1)} %collective-permute-done.21.refs_2_.refs_3_, ...), custom_call_target="tpu_custom_call" | custom-call | tf_op jit(solution)/shard_map/weight_terms/pallas_call | solution.py:51
  394.0 17.4 %collective-permute-done.38 = bf16[128,2048]{1,0:T(8,128)(2,1)S(1)} collective-permute-done((bf16[128,2048]{1,0:T(8,128)(2,1)S(1)}, bf16[128,2048]{1,0:T(8,128)(2,1)S(1)}, u32[]{:S(2)}, u32[]{:S(2)}) %collective-permute-start.38) | collective-permute-done | bytes 524320 | tf_op jit(solution)/shard_map/ppermute | solution.py:437
  427.3 8.4 %weight_terms.7 = (bf16[256,2048]{1,0:T(8,128)(2,1)S(1)}, bf16[256,2048]{1,0:T(8,128)(2,1)S(1)}, bf16[256,2048]{1,0:T(8,128)(2,1)S(1)}, bf16[256,2048]{1,0:T(8,128)(2,1)S(1)}) custom-call(bf16[1024,1024]{1,0:T(8,128)(2,1)} %get-tuple-element.219.refs_0_, bf16[256,2048]{1,0:T(8,128)(2,1)S(1)} %add_convert_fusion.8.refs_0_.refs_1_, ...), custom_call_target="tpu_custom_call" | custom-call | tf_op jit(solution)/shard_map/weight_terms/pallas_call | solution.py:51
  437.6 7.6 %collective-permute-done.41 = bf16[256,2048]{1,0:T(8,128)(2,1)} collective-permute-done((bf16[256,2048]{1,0:T(8,128)(2,1)S(1)}, bf16[256,2048]{1,0:T(8,128)(2,1)}, u32[]{:S(2)}, u32[]{:S(2)}) %collective-permute-start.41) | collective-permute-done | bytes 1048608 | tf_op jit(solution)/shard_map/ppermute | solution.py:449
  445.3 14.1 %hidden_sum.3 = (f32[256,2048]{1,0:T(8,128)S(1)}, bf16[256,2048]{1,0:T(8,128)(2,1)}, bf16[256,2048]{1,0:T(8,128)(2,1)S(1)}, bf16[256,2048]{1,0:T(8,128)(2,1)}) custom-call(bf16[1024,1024]{1,0:T(8,128)(2,1)S(1)} %copy-done.20, bf16[1024,1024]{1,0:T(8,128)(2,1)S(1)} %copy-done.22, bf16[1024,2048]{1,0:T(8,128)(2,1)} %join_rows.3.refs_2_, ...), custom_call_target="tpu_custom_call" | custom-call | tf_op jit(solution)/shard_map/hidden_sum/pallas_call | solution.py:51
  474.3 10.4 %collective-permute-done.42 = bf16[256,2048]{1,0:T(8,128)(2,1)} collective-permute-done((bf16[256,2048]{1,0:T(8,128)(2,1)}, bf16[256,2048]{1,0:T(8,128)(2,1)}, u32[]{:S(2)}, u32[]{:S(2)}) %collective-permute-start.42) | collective-permute-done | bytes 1048608 | tf_op jit(solution)/shard_map/ppermute | solution.py:437
  491.0 6.7 %fusion.21 = bf16[2048,256]{0,1:T(8,128)(2,1)} fusion(bf16[256,2048]{1,0:T(8,128)(2,1)S(1)} %copy-done.64, bf16[2048,2048]{1,0:T(8,128)(2,1)} %all-gather.3.cloned.1.call-done), kind=kOutput, calls=%fused_computation.28 | convolution fusion | flops 2148007936 | bytes 10485760 | tf_op jit(solution)/shard_map/dot_general | solution.py:780
  501.3 8.3 %fusion = bf16[16,1024,256]{1,2,0:T(8,128)(2,1)S(1)} fusion(f32[16,1024,256]{1,2,0:T(8,128)} %copy-done.49, bf16[16,128,256]{2,1,0:T(8,128)(2,1)S(1)} %bitcast.210, f32[16,256]{1,0:T(8,128)S(1)} %fusion.32, f32[16,256]{1,0:T(8,128)S(1)} %copy-done.117, pred[1024,256]{0,1:T(8,128)(4,1)S(1)} %pad_add_fusion, bf16[128,256]{1,0:T(8,128)(2,1)S(1)} %copy-done.107, ...), kind=kOutput, calls=%fused_computation.1 | convolution fusion | flops 1095761920 | bytes 26771456 | tf_op jit(solution)/shard_map/dk,hdq->hkq/dot_general | solution.py:787
  510.8 7.6 %fusion.33 = f32[128,1024]{1,0:T(8,128)S(1)} fusion(bf16[16,128,256]{2,1,0:T(8,128)(2,1)S(1)} %bitcast.211, f32[16,1024,256]{1,2,0:T(8,128)} %copy-done.49, f32[16,256]{1,0:T(8,128)S(1)} %copy-done.117, pred[1024,256]{0,1:T(8,128)(4,1)S(1)} %pad_add_fusion), kind=kOutput, calls=%fused_computation.74 | convolution fusion | flops 1086324736 | bytes 18628608 | tf_op jit(solution)/shard_map/hkq,hdq->dk/dot_general | solution.py:791
  534.0 13.9 %collective-permute-done.54 = bf16[256,2048]{1,0:T(8,128)(2,1)S(1)} collective-permute-done((bf16[256,2048]{1,0:T(8,128)(2,1)S(1)}, bf16[256,2048]{1,0:T(8,128)(2,1)S(1)}, u32[]{:S(2)}, u32[]{:S(2)}) %collective-permute-start.54) | collective-permute-done | bytes 1048608 | tf_op jit(solution)/shard_map/ppermute | solution.py:449
  550.8 20.8 %collective-permute-done.59 = bf16[256,2048]{1,0:T(8,128)(2,1)S(1)} collective-permute-done((bf16[256,2048]{1,0:T(8,128)(2,1)S(1)}, bf16[256,2048]{1,0:T(8,128)(2,1)S(1)}, u32[]{:S(2)}, u32[]{:S(2)}) %collective-permute-start.59) | collective-permute-done | bytes 1048608 | tf_op jit(solution)/shard_map/ppermute | solution.py:449
  589.8 6.3 fusion.26
  633.0 15.7 %collective-permute-done.58 = bf16[256,2048]{1,0:T(8,128)(2,1)S(1)} collective-permute-done((bf16[256,2048]{1,0:T(8,128)(2,1)S(1)}, bf16[256,2048]{1,0:T(8,128)(2,1)S(1)}, u32[]{:S(2)}, u32[]{:S(2)}) %collective-permute-start.58) | collective-permute-done | bytes 1048608 | tf_op jit(solution)/shard_map/ppermute | solution.py:437
  (566 shorter events, 302.4 us)
Async XLA Ops:
  7.2 130.4 %all-gather.3.cloned.1.call-start = ((), (), s32[]{:S(2)}) async-start(), calls=%async_computation | async-start | bytes 8650752 | tf_op jit(solution)/shard_map/all_gather | solution.py:606
  7.9 581.8 %all-gather.5.cloned.1.call-start = ((), (), s32[]{:S(2)}) async-start(), calls=%async_computation.1 | async-start | bytes 9732096 | tf_op jit(solution)/shard_map/all_gather | solution.py:804
  18.6 26.1 %collective-permute-start.3 = (bf16[256,2048]{1,0:T(8,128)(2,1)S(1)}, bf16[256,2048]{1,0:T(8,128)(2,1)S(1)}, u32[]{:S(2)}, u32[]{:S(2)}) collective-permute-start(bf16[256,2048]{1,0:T(8,128)(2,1)S(1)} %fusion.24), channel_id=1, source_target_pairs={{1,0},{3,1},{2,3},{0,2},{5,4},{7,5},{6,7},{4,6},{9,8},{11,9},{10,1... | collective-permute-start | bytes 3145736 | tf_op jit(solution)/shard_map/ppermute | solution.py:437
  20.2 26.9 %collective-permute-start.4 = (bf16[256,2048]{1,0:T(8,128)(2,1)S(1)}, bf16[256,2048]{1,0:T(8,128)(2,1)}, u32[]{:S(2)}, u32[]{:S(2)}) collective-permute-start(bf16[256,2048]{1,0:T(8,128)(2,1)S(1)} %fusion.24), channel_id=1, source_target_pairs={{2,0},{0,1},{1,3},{3,2},{6,4},{4,5},{5,7},{7,6},{10,8},{8,9},{9,11... | collective-permute-start | bytes 3145736 | tf_op jit(solution)/shard_map/ppermute | solution.py:437
  50.0 57.5 %collective-permute-start.18 = (bf16[256,2048]{1,0:T(8,128)(2,1)S(1)}, bf16[256,2048]{1,0:T(8,128)(2,1)}, u32[]{:S(2)}, u32[]{:S(2)}) collective-permute-start(bf16[256,2048]{1,0:T(8,128)(2,1)S(1)} %copy-done.7), channel_id=1, source_target_pairs={{8,0},{12,4},{0,16},{4,20},{16,24},{20,28},{24,8},{28,12},{9,1},{1... | collective-permute-start | bytes 3145736 | tf_op jit(solution)/shard_map/ppermute | solution.py:445
  104.9 41.6 %collective-permute-start.14 = (bf16[256,2048]{1,0:T(8,128)(2,1)S(1)}, bf16[256,2048]{1,0:T(8,128)(2,1)S(1)}, u32[]{:S(2)}, u32[]{:S(2)}) collective-permute-start(bf16[256,2048]{1,0:T(8,128)(2,1)S(1)} %bitcast.195), channel_id=1, source_target_pairs={{1,0},{3,1},{2,3},{0,2},{5,4},{7,5},{6,7},{4,6},{9,8},{11,9},{10,1... | collective-permute-start | bytes 3145736 | tf_op jit(solution)/shard_map/ppermute | solution.py:437
  107.5 39.0 %collective-permute-start.15 = (bf16[256,2048]{1,0:T(8,128)(2,1)S(1)}, bf16[256,2048]{1,0:T(8,128)(2,1)}, u32[]{:S(2)}, u32[]{:S(2)}) collective-permute-start(bf16[256,2048]{1,0:T(8,128)(2,1)S(1)} %bitcast.196), channel_id=1, source_target_pairs={{2,0},{0,1},{1,3},{3,2},{6,4},{4,5},{5,7},{7,6},{10,8},{8,9},{9,11... | collective-permute-start | bytes 3145736 | tf_op jit(solution)/shard_map/ppermute | solution.py:437
  107.5 37.8 %collective-permute-start.19 = (bf16[256,2048]{1,0:T(8,128)(2,1)}, bf16[256,2048]{1,0:T(8,128)(2,1)}, u32[]{:S(2)}, u32[]{:S(2)}) collective-permute-start(bf16[256,2048]{1,0:T(8,128)(2,1)} %collective-permute-done.18.refs_6_.refs_1_.refs_3_), channel_id=1, source_target_pairs={{8,0},{12,4},{0,16},{4,20},{16,24},{20,28},{24,8},{28,12},{9,1},{1... | collective-permute-start | bytes 3145736 | tf_op jit(solution)/shard_map/ppermute | solution.py:445
  145.9 26.1 %collective-permute-start.20 = (bf16[256,2048]{1,0:T(8,128)(2,1)S(1)}, bf16[256,2048]{1,0:T(8,128)(2,1)}, u32[]{:S(2)}, u32[]{:S(2)}) collective-permute-start(bf16[256,2048]{1,0:T(8,128)(2,1)S(1)} %copy-done.25), channel_id=1, source_target_pairs={{8,0},{12,4},{0,16},{4,20},{16,24},{20,28},{24,8},{28,12},{9,1},{1... | collective-permute-start | bytes 3145736 | tf_op jit(solution)/shard_map/ppermute | solution.py:445
  146.4 25.5 %collective-permute-start.16 = (bf16[256,2048]{1,0:T(8,128)(2,1)S(1)}, bf16[256,2048]{1,0:T(8,128)(2,1)S(1)}, u32[]{:S(2)}, u32[]{:S(2)}) collective-permute-start(bf16[256,2048]{1,0:T(8,128)(2,1)S(1)} %add_convert_fusion.8.refs_0_.refs_1_), channel_id=1, source_target_pairs={{1,0},{3,1},{2,3},{0,2},{5,4},{7,5},{6,7},{4,6},{9,8},{11,9},{10,1... | collective-permute-start | bytes 3145736 | tf_op jit(solution)/shard_map/ppermute | solution.py:437
  148.5 45.2 %collective-permute-start.23 = (bf16[256,2048]{1,0:T(8,128)(2,1)}, bf16[256,2048]{1,0:T(8,128)(2,1)S(1)}, u32[]{:S(2)}, u32[]{:S(2)}) collective-permute-start(bf16[256,2048]{1,0:T(8,128)(2,1)} %collective-permute-done.19.refs_7_.refs_2_.refs_4_), channel_id=1, source_target_pairs={{8,0},{12,4},{0,16},{4,20},{16,24},{20,28},{24,8},{28,12},{9,1},{1... | collective-permute-start | bytes 3145736 | tf_op jit(solution)/shard_map/ppermute | solution.py:445
  197.4 34.2 %collective-permute-start.27 = (bf16[1024,2048]{1,0:T(8,128)(2,1)}, bf16[1024,2048]{1,0:T(8,128)(2,1)}, u32[]{:S(2)}, u32[]{:S(2)}) collective-permute-start(bf16[1024,2048]{1,0:T(8,128)(2,1)} %join_rows.2), channel_id=1, source_target_pairs={{0,4},{4,0},{8,12},{12,8},{16,20},{20,16},{24,28},{28,24},{1,5},{5... | collective-permute-start | bytes 12582920 | tf_op jit(solution)/shard_map/ppermute | solution.py:441
  201.2 30.4 %collective-permute-start.26 = (bf16[256,2048]{1,0:T(8,128)(2,1)}, bf16[256,2048]{1,0:T(8,128)(2,1)}, u32[]{:S(2)}, u32[]{:S(2)}) collective-permute-start(bf16[256,2048]{1,0:T(8,128)(2,1)} %collective-permute-done.20.refs_6_.refs_1_), channel_id=1, source_target_pairs={{8,0},{12,4},{0,16},{4,20},{16,24},{20,28},{24,8},{28,12},{9,1},{1... | collective-permute-start | bytes 3145736 | tf_op jit(solution)/shard_map/ppermute | solution.py:445
  214.6 27.3 %collective-permute-start.24 = (bf16[128,2048]{1,0:T(8,128)(2,1)S(1)}, bf16[128,2048]{1,0:T(8,128)(2,1)S(1)}, u32[]{:S(2)}, u32[]{:S(2)}) collective-permute-start(bf16[128,2048]{1,0:T(8,128)(2,1)S(1)} %slice.205), channel_id=1, source_target_pairs={{1,0},{3,1},{2,3},{0,2},{5,4},{7,5},{6,7},{4,6},{9,8},{11,9},{10,1... | collective-permute-start | bytes 1572872 | tf_op jit(solution)/shard_map/ppermute | solution.py:437
  251.6 47.9 %collective-permute-start.34 = (bf16[1024,2048]{1,0:T(8,128)(2,1)}, bf16[1024,2048]{1,0:T(8,128)(2,1)S(1)}, u32[]{:S(2)}, u32[]{:S(2)}) collective-permute-start(bf16[1024,2048]{1,0:T(8,128)(2,1)} %weight_terms.4), channel_id=1, source_target_pairs={{0,4},{4,0},{8,12},{12,8},{16,20},{20,16},{24,28},{28,24},{1,5},{5... | collective-permute-start | bytes 12582920 | tf_op jit(solution)/shard_map/ppermute | solution.py:441
  251.7 25.6 %collective-permute-start.29 = (bf16[256,2048]{0,1:T(8,128)(2,1)S(1)}, bf16[256,2048]{0,1:T(8,128)(2,1)S(1)}, u32[]{:S(2)}, u32[]{:S(2)}) collective-permute-start(bf16[256,2048]{0,1:T(8,128)(2,1)S(1)} %bitcast.227), channel_id=1, source_target_pairs={{1,0},{3,1},{2,3},{0,2},{5,4},{7,5},{6,7},{4,6},{9,8},{11,9},{10,1... | collective-permute-start | bytes 3145736 | tf_op jit(solution)/shard_map/ppermute | solution.py:437
  253.8 30.7 %collective-permute-start.28 = (bf16[256,2048]{1,0:T(8,128)(2,1)}, bf16[256,2048]{1,0:T(8,128)(2,1)S(1)}, u32[]{:S(2)}, u32[]{:S(2)}) collective-permute-start(bf16[256,2048]{1,0:T(8,128)(2,1)} %collective-permute-done.26.refs_7_.refs_2_), channel_id=1, source_target_pairs={{8,0},{12,4},{0,16},{4,20},{16,24},{20,28},{24,8},{28,12},{9,1},{1... | collective-permute-start | bytes 3145736 | tf_op jit(solution)/shard_map/ppermute | solution.py:445
  301.8 33.8 %collective-permute-start.35 = (bf16[256,2048]{1,0:T(8,128)(2,1)}, bf16[256,2048]{1,0:T(8,128)(2,1)}, u32[]{:S(2)}, u32[]{:S(2)}) collective-permute-start(bf16[256,2048]{1,0:T(8,128)(2,1)} %add_convert_fusion.7), channel_id=1, source_target_pairs={{0,8},{4,12},{16,0},{20,4},{24,16},{28,20},{8,24},{12,28},{1,9},{5... | collective-permute-start | bytes 3145736 | tf_op jit(solution)/shard_map/ppermute | solution.py:449
  339.5 38.0 %collective-permute-start.36 = (bf16[256,2048]{1,0:T(8,128)(2,1)}, bf16[256,2048]{1,0:T(8,128)(2,1)}, u32[]{:S(2)}, u32[]{:S(2)}) collective-permute-start(bf16[256,2048]{1,0:T(8,128)(2,1)} %add_convert_fusion.6), channel_id=1, source_target_pairs={{0,8},{4,12},{16,0},{20,4},{24,16},{28,20},{8,24},{12,28},{1,9},{5... | collective-permute-start | bytes 3145736 | tf_op jit(solution)/shard_map/ppermute | solution.py:449
  386.2 77.7 %collective-permute-start.46 = (bf16[1024,2048]{1,0:T(8,128)(2,1)}, bf16[1024,2048]{1,0:T(8,128)(2,1)S(1)}, u32[]{:S(2)}, u32[]{:S(2)}) collective-permute-start(bf16[1024,2048]{1,0:T(8,128)(2,1)} %weight_terms.6), channel_id=1, source_target_pairs={{0,4},{4,0},{8,12},{12,8},{16,20},{20,16},{24,28},{28,24},{1,5},{5... | collective-permute-start | bytes 12582920 | tf_op jit(solution)/shard_map/ppermute | solution.py:441
  392.0 30.2 %collective-permute-start.39 = (bf16[128,2048]{1,0:T(8,128)(2,1)S(1)}, bf16[128,2048]{1,0:T(8,128)(2,1)S(1)}, u32[]{:S(2)}, u32[]{:S(2)}) collective-permute-start(bf16[128,2048]{1,0:T(8,128)(2,1)S(1)} %get-tuple-element.217), channel_id=1, source_target_pairs={{2,0},{0,1},{1,3},{3,2},{6,4},{4,5},{5,7},{7,6},{10,8},{8,9},{9,11... | collective-permute-start | bytes 1572872 | tf_op jit(solution)/shard_map/ppermute | solution.py:437
  393.2 34.0 %collective-permute-start.40 = (bf16[128,2048]{1,0:T(8,128)(2,1)S(1)}, bf16[128,2048]{1,0:T(8,128)(2,1)}, u32[]{:S(2)}, u32[]{:S(2)}) collective-permute-start(bf16[128,2048]{1,0:T(8,128)(2,1)S(1)} %get-tuple-element.218), channel_id=1, source_target_pairs={{1,0},{3,1},{2,3},{0,2},{5,4},{7,5},{6,7},{4,6},{9,8},{11,9},{10,1... | collective-permute-start | bytes 1572872 | tf_op jit(solution)/shard_map/ppermute | solution.py:437
  412.3 49.1 %collective-permute-start.45 = (bf16[128,2048]{1,0:T(8,128)(2,1)}, bf16[128,2048]{1,0:T(8,128)(2,1)}, u32[]{:S(2)}, u32[]{:S(2)}) collective-permute-start(bf16[128,2048]{1,0:T(8,128)(2,1)} %add_convert_fusion.9), channel_id=1, source_target_pairs={{1,0},{3,1},{2,3},{0,2},{5,4},{7,5},{6,7},{4,6},{9,8},{11,9},{10,1... | collective-permute-start | bytes 1572872 | tf_op jit(solution)/shard_map/ppermute | solution.py:437
  414.8 30.5 %collective-permute-start.41 = (bf16[256,2048]{1,0:T(8,128)(2,1)S(1)}, bf16[256,2048]{1,0:T(8,128)(2,1)}, u32[]{:S(2)}, u32[]{:S(2)}) collective-permute-start(bf16[256,2048]{1,0:T(8,128)(2,1)S(1)} %add_convert_fusion.5), channel_id=1, source_target_pairs={{0,8},{4,12},{16,0},{20,4},{24,16},{28,20},{8,24},{12,28},{1,9},{5... | collective-permute-start | bytes 3145736 | tf_op jit(solution)/shard_map/ppermute | solution.py:449
  422.2 39.2 %collective-permute-start.44 = (bf16[128,2048]{1,0:T(8,128)(2,1)}, bf16[128,2048]{1,0:T(8,128)(2,1)}, u32[]{:S(2)}, u32[]{:S(2)}) collective-permute-start(bf16[128,2048]{1,0:T(8,128)(2,1)} %add_convert_fusion.10), channel_id=1, source_target_pairs={{2,0},{0,1},{1,3},{3,2},{6,4},{4,5},{5,7},{7,6},{10,8},{8,9},{9,11... | collective-permute-start | bytes 1572872 | tf_op jit(solution)/shard_map/ppermute | solution.py:437
  459.3 25.3 %collective-permute-start.42 = (bf16[256,2048]{1,0:T(8,128)(2,1)}, bf16[256,2048]{1,0:T(8,128)(2,1)}, u32[]{:S(2)}, u32[]{:S(2)}) collective-permute-start(bf16[256,2048]{1,0:T(8,128)(2,1)} %get-tuple-element.227), channel_id=1, source_target_pairs={{2,0},{0,1},{1,3},{3,2},{6,4},{4,5},{5,7},{7,6},{10,8},{8,9},{9,11... | collective-permute-start | bytes 3145736 | tf_op jit(solution)/shard_map/ppermute | solution.py:437
  465.4 25.6 %collective-permute-start.47 = (bf16[256,2048]{1,0:T(8,128)(2,1)}, bf16[256,2048]{1,0:T(8,128)(2,1)}, u32[]{:S(2)}, u32[]{:S(2)}) collective-permute-start(bf16[256,2048]{1,0:T(8,128)(2,1)} %add_convert_fusion.4), channel_id=1, source_target_pairs={{0,8},{4,12},{16,0},{20,4},{24,16},{28,20},{8,24},{12,28},{1,9},{5... | collective-permute-start | bytes 3145736 | tf_op jit(solution)/shard_map/ppermute | solution.py:449
  485.8 35.8 %collective-permute-start.51 = (bf16[512,256]{1,0:T(8,128)(2,1)}, bf16[512,256]{1,0:T(8,128)(2,1)}, u32[]{:S(2)}, u32[]{:S(2)}) collective-permute-start(bf16[512,256]{1,0:T(8,128)(2,1)} %bitcast.39), channel_id=1, source_target_pairs={{1,0},{3,1},{2,3},{0,2},{5,4},{7,5},{6,7},{4,6},{9,8},{11,9},{10,1... | collective-permute-start | bytes 786440 | tf_op jit(solution)/shard_map/ppermute | solution.py:437
  486.4 35.6 %collective-permute-start.52 = (bf16[512,256]{1,0:T(8,128)(2,1)}, bf16[512,256]{1,0:T(8,128)(2,1)}, u32[]{:S(2)}, u32[]{:S(2)}) collective-permute-start(bf16[512,256]{1,0:T(8,128)(2,1)} %bitcast.38), channel_id=1, source_target_pairs={{3,0},{2,1},{0,3},{1,2},{7,4},{6,5},{4,7},{5,6},{11,8},{10,9},{8,1... | collective-permute-start | bytes 786440 | tf_op jit(solution)/shard_map/ppermute | solution.py:437
  487.6 34.4 %collective-permute-start.53 = (bf16[512,256]{1,0:T(8,128)(2,1)}, bf16[512,256]{1,0:T(8,128)(2,1)}, u32[]{:S(2)}, u32[]{:S(2)}) collective-permute-start(bf16[512,256]{1,0:T(8,128)(2,1)} %bitcast.37), channel_id=1, source_target_pairs={{2,0},{0,1},{1,3},{3,2},{6,4},{4,5},{5,7},{7,6},{10,8},{8,9},{9,11... | collective-permute-start | bytes 786440 | tf_op jit(solution)/shard_map/ppermute | solution.py:437
  622.9 25.9 %collective-permute-start.58 = (bf16[256,2048]{1,0:T(8,128)(2,1)S(1)}, bf16[256,2048]{1,0:T(8,128)(2,1)S(1)}, u32[]{:S(2)}, u32[]{:S(2)}) collective-permute-start(bf16[256,2048]{1,0:T(8,128)(2,1)S(1)} %copy-done.45), channel_id=1, source_target_pairs={{3,0},{2,1},{0,3},{1,2},{7,4},{6,5},{4,7},{5,6},{11,8},{10,9},{8,1... | collective-permute-start | bytes 3145736 | tf_op jit(solution)/shard_map/ppermute | solution.py:437
  624.3 25.8 %collective-permute-start.70 = (f32[22656]{0:T(1024)S(1)}, f32[22656]{0:T(1024)S(1)}, u32[]{:S(2)}, u32[]{:S(2)}) collective-permute-start(f32[22656]{0:T(1024)S(1)} %add.514), channel_id=1, source_target_pairs={{0,8},{4,12},{8,0},{12,4},{16,24},{20,28},{24,16},{28,20},{1,9},{5... | collective-permute-start | bytes 271880 | tf_op jit(solution)/shard_map/ppermute | solution.py:537
  (181 other events, 2001.0 us)
Sparse Core Ops, SparseCore 0:
  10.9 126.6 all-gather.2
  308.5 119.1 all-gather.4

commit v2 on v1

--- a/solution.py
+++ b/solution.py
@@ -47,7 +47,12 @@
 ANY = pl.BlockSpec(memory_space=pl.ANY)
 
 
-def call(kernel, name, out_shape, scratch, inputs):
+def cost(flops, arrays):
+    moved = sum(leaf.size * jnp.dtype(leaf.dtype).itemsize for leaf in jax.tree.leaves(arrays))
+    return pl.CostEstimate(flops=flops, bytes_accessed=moved, transcendentals=0)
+
+
+def call(kernel, name, out_shape, scratch, inputs, flops=0):
     return pl.pallas_call(
         kernel,
         name=name,
@@ -55,7 +60,7 @@
         in_specs=[ANY] * len(inputs),
         out_specs=jax.tree.map(lambda _: ANY, out_shape),
         scratch_shapes=scratch,
-        cost_estimate=FREE,
+        cost_estimate=cost(flops, (inputs, out_shape)),
         compiler_params=pltpu.CompilerParams(vmem_limit_bytes=44 * 1024 * 1024),
     )(*inputs)
 
@@ -102,6 +107,46 @@
         ],
         tuple(pieces),
     )
+
+
+def add_terms(members, rows, kind=BF):
+    width = members[0][0].shape[1]
+    step = min(rows, 64)
+
+    def kernel(*refs):
+        total = add_wide(refs[0][...], refs[1][...])
+        for ref in refs[2:-1]:
+            total = total + ref[...].astype(F32)
+        refs[-1][...] = total.astype(kind)
+
+    def spec(first):
+        return pl.BlockSpec((step, width), lambda i: (i + first // step, 0))
+
+    return pl.pallas_call(
+        kernel,
+        name="add_terms",
+        grid=(rows // step,),
+        out_shape=jax.ShapeDtypeStruct((rows, width), kind),
+        in_specs=[spec(first) for _, first in members],
+        out_specs=spec(0),
+        cost_estimate=pl.CostEstimate(
+            flops=0, bytes_accessed=2 * rows * width * (len(members) + 1), transcendentals=0
+        ),
+        compiler_params=pltpu.CompilerParams(vmem_limit_bytes=44 * 1024 * 1024),
+    )(*[member for member, _ in members])
+
+
+def gate(value, *needed):
+    def kernel(value_ref, out_ref):
+        out_ref[...] = value_ref[...]
+
+    return pl.pallas_call(
+        kernel,
+        name="gate",
+        out_shape=jax.ShapeDtypeStruct(value.shape, value.dtype),
+        cost_estimate=FREE,
+        compiler_params=pltpu.CompilerParams(vmem_limit_bytes=44 * 1024 * 1024),
+    )(after(value, needed))
 
 
 def row_tile(rows):
@@ -176,6 +221,7 @@
             pltpu.SemaphoreType.DMA((2, 2)),
         ],
         (*pieces, *slots, shift.reshape(1, units)),
+        2 * rows * units * width,
     )
 
 
@@ -244,6 +290,7 @@
             pltpu.SemaphoreType.DMA,
         ],
         (*pieces, *slots, pre),
+        2 * rows * units * width,
     )
     return grad, sums.reshape(units)
 
@@ -331,70 +378,58 @@
             pltpu.SemaphoreType.DMA((3, cuts)),
         ],
         (*lefts, *slots),
-    )
-
-
-def weight_terms(left, pieces, outs):
+        2 * rows * depth * width,
+    )
+
+
+def weight_terms(left, pieces, slots, size):
     rows, units = left.shape
     width = pieces[0].shape[1]
-    size = units // outs
-    step = min(rows, 1024)
-
     def kernel(*refs):
         left_ref, piece_refs = refs[0], refs[1 : 1 + len(pieces)]
-        out_refs = refs[1 + len(pieces) : 1 + len(pieces) + outs]
-        l, x, out_buf, l_sem, x_sem, out_sem = refs[1 + len(pieces) + outs :]
+        out_ref, l, x, out_buf, l_sem, x_sem, out_sem = refs[1 + len(pieces) :]
         l_copy = pltpu.make_async_copy(left_ref, l, l_sem)
         l_copy.start()
         x_copies = start_rows(piece_refs, x, x_sem)
         l_copy.wait()
         wait_rows(x_copies, 0, rows)
         sent = []
+        wide = min(width, 1024)
+        source = slots() if size == TILE else range(units // TILE)
         for tile in range(units // TILE):
             slot = tile % 2
             if tile >= 2:
-                for copy in sent[tile - 2]:
-                    copy.wait()
-
-            columns = pl.ds(tile * TILE, TILE)
-            wide = min(width, 1024)
+                sent[tile - 2].wait()
+            columns = pl.ds(pl.multiple_of(source[tile] * TILE, TILE), TILE)
 
             @pl.loop(0, width // wide)
             def _(index):
                 span = pl.ds(pl.multiple_of(index * wide, wide), wide)
                 out_buf[slot, :, span] = dot_tn(l[:, columns], x[:, span]).astype(BF)
 
-            copies, row = [], tile * TILE
-            while row < (tile + 1) * TILE:
-                count = min(size - row % size, TILE)
-                copies.append(
-                    pltpu.make_async_copy(
-                        out_buf.at[slot, pl.ds(row - tile * TILE, count)],
-                        out_refs[row // size].at[pl.ds(row % size, count)],
-                        out_sem.at[slot, len(copies)],
-                    )
+            sent.append(
+                pltpu.make_async_copy(
+                    out_buf.at[slot], out_ref.at[pl.ds(tile * TILE, TILE)], out_sem.at[slot]
                 )
-                row += count
-            for copy in copies:
-                copy.start()
-            sent.append(copies)
-        for copies in sent[-2:]:
-            for copy in copies:
-                copy.wait()
+            )
+            sent[tile].start()
+        for copy in sent[-2:]:
+            copy.wait()
 
     return call(
         kernel,
         "weight_terms",
-        tuple([jax.ShapeDtypeStruct((size, width), BF)] * outs),
+        jax.ShapeDtypeStruct((units, width), BF),
         [
             pltpu.VMEM((rows, units), BF),
             pltpu.VMEM((rows, width), BF),
             pltpu.VMEM((2, TILE, width), BF),
             pltpu.SemaphoreType.DMA,
             pltpu.SemaphoreType.DMA((len(pieces),)),
-            pltpu.SemaphoreType.DMA((2, max(1, TILE // size))),
+            pltpu.SemaphoreType.DMA((2,)),
         ],
         (left, *pieces),
+        2 * rows * units * width,
     )
 
 
@@ -523,12 +558,49 @@
         n, place = self.z_n, (self.chip_pos - m) % self.z_n
         return jnp.where(place < (n + 1) // 2, 2 * place, 2 * (n - 1 - place) + 1)
 
-    def chip_sum(self, parts, m, came, *needed):
-        return self.z_back(after(self.chip_total(parts, m, came).astype(BF), needed))
-
-    def chip_total(self, parts, m, came):
-        total = add_wide(*parts[m]) if isinstance(parts[m], tuple) else parts[m].astype(F32)
-        return total if came is None else total + came.astype(F32)
+    def other_chip(self, value, bits):
+        pairs = [(2 * z + c, 2 * (z ^ bits) + c) for z in range(self.z_n) for c in range(2)]
+        return lax.ppermute(value, "dp", pairs)
+
+    def term_slots(self):
+        if self.z_n != 4:
+            return list(range(self.z_n))
+        z = lax.axis_index("dp") // 2
+        outer = (z == 0) | (z == 3)
+        return [0, jnp.where(outer, 3, 1), jnp.where(outer, 1, 3), 2]
+
+    def first_term(self, own, came, rows, *needed):
+        own = after(own, needed)
+        if rows % 64 == 0:
+            return add_terms([(own, 2 * rows), (came, 2 * rows)], 2 * rows)
+        return add_low(own[2 * rows :], came[2 * rows :])
+
+    def first_move(self, term, *needed):
+        return self.other_chip(after(term, needed), 1) if self.z_n == 4 else None
+
+    def second_term(self, own, came, first, rows, *needed):
+        own = after(own, needed)
+        if self.z_n != 4:
+            total = add_wide(own, came)
+            moved = total[(self.z_n - 1) * rows :].astype(BF)
+            for m in range(self.z_n - 2, 0, -1):
+                moved = self.z_back(moved)
+                moved = (total[m * rows : (m + 1) * rows] + moved.astype(F32)).astype(BF)
+            return self.z_back(moved)
+        if rows % 64 == 0:
+            return add_terms([(own, rows), (came, rows), (first, rows)], rows)
+        part = slice(rows, 2 * rows)
+        return (add_wide(own[part], came[part]) + first[part].astype(F32)).astype(BF)
+
+    def second_move(self, term, *needed):
+        return self.other_chip(after(term, needed), 2) if self.z_n == 4 else term
+
+    def chip_sum_end(self, own, came, first, second, rows, *needed):
+        if rows % 64 == 0 and first is not None:
+            members = [(after(own, needed), 0), (came, 0), (first, 0), (second, 0)]
+            return add_terms(members, rows, F32)
+        total = add_wide(own[:rows], came[:rows]) + second.astype(F32)
+        return total if first is None else total + first[:rows].astype(F32)
 
     def other_seq(self, value, bit):
         return lax.ppermute(value, "seq", [(i, i ^ bit) for i in range(self.seq_n)])
@@ -673,6 +745,9 @@
         return attn, highest + jnp.log(total), attn.reshape(width, tok).astype(BF).T
 
     attn, log_total, attn_low = attend(query, pairs)
+    for _ in range(z_n - 3):
+        fc_chips.append(links.z_next(after(fc_chips[-1], attn_low)))
+    proj_chips = [proj_weight, links.z_next(after(proj_weight, fc_chips[2], attn_low))]
 
     def norm_two(attn_low, out_full, tokens):
         flat = tokens.reshape(tok, width).astype(F32)
@@ -682,62 +757,59 @@
 
     middle, normed_two, inverse_two, hidden_two = norm_two(attn_low, out_full, tokens)
     twos = links.gather_near(after(hidden_two, grads[1], grads[-1]))
-    for _ in range(z_n - 3):
-        fc_chips.append(links.z_next(after(fc_chips[-1], hidden_two)))
-    proj_chips = [proj_weight, links.z_next(after(proj_weight, fc_chips[2], hidden_two))]
-
-    twos = links.gather_far(after(twos, proj_chips))
-    proj_chips.append(links.z_next(after(proj_chips[-1], twos[1], twos[-1])))
+
+    twos = links.gather_far(twos)
+    qkv_mine = lax.all_gather(after(mine, twos[1], twos[-1]), "seq", axis=0, tiled=True)
+    qkv_mine = qkv_mine.reshape(-1, width)
     fc_chips = after(fc_chips, twos[1], twos[-1])
     fc_other = links.swap_core(join_rows(fc_chips))
     grads = links.gather_far(after(grads, twos))
 
-    pre_mine, act_mine = hidden_forward(twos, fc_chips, fc_shift[:split])
+    proj_chips.append(links.z_next(after(proj_chips[-1], twos)))
+    pre_mine, act_mine = hidden_forward(after(twos, proj_chips[1]), fc_chips, fc_shift[:split])
     ready = act_mine[:8, :HDIM]
-    pre_other, act_other = hidden_forward(after(twos, ready, proj_chips), [fc_other], fc_shift[split:])
+    pre_other, act_other = hidden_forward(after(twos, ready), [fc_other], fc_shift[split:])
+    attns = links.gather_near(after(attn_low, grads, act_other))
+    grads = after(grads, act_other)
+
+    proj_sent = weight_terms(after(act_other, proj_chips[2]), grads, links.term_slots, units)
+    proj_came = links.swap_core(proj_sent)
+    proj_own = weight_terms(after(act_mine, proj_sent), grads, links.term_slots, units)
     for _ in range(z_n - 3):
-        proj_chips.append(links.z_next(after(proj_chips[-1], ready)))
-    attns = links.gather_near(after(attn_low, grads, ready))
-    grads = after(grads, act_other)
-
-    def core_terms(own, came):
-        return [(own[m], came[m * units : (m + 1) * units]) for m in range(z_n)]
-
-    (proj_sent,) = weight_terms(act_other, grads, 1)
-    proj_came = links.swap_core(proj_sent)
-    proj_own = weight_terms(after(act_mine, proj_sent, proj_chips, attns[1], attns[-1]), grads, z_n)
-    proj_terms = core_terms(proj_own, proj_came)
-    proj_chips = after(proj_chips, proj_own)
+        proj_chips.append(links.z_next(after(proj_chips[-1], act_other)))
+    attns = links.gather_far(after(attns, proj_own))
+    proj_term = links.first_term(proj_own, proj_came, units)
+    proj_first = links.first_move(proj_term)
+    proj_chips = after(proj_chips, proj_term, attns[1], attns[-1])
     proj_mine = join_rows(proj_chips)
     proj_other = links.swap_core(proj_mine)
-    proj_sum = links.chip_sum(proj_terms, z_n - 1, None)
-    proj_sum_first = proj_sum
-    attns = links.gather_far(after(attns, proj_own))
 
     grad_mine, bias_mine = hidden_backward(grads, proj_chips, pre_mine)
-    grad_other, bias_other = hidden_backward(after(grads, bias_mine, attns), [proj_other], pre_other)
-    proj_sum = links.chip_sum(proj_terms, z_n - 2, proj_sum, grad_other)
+    grad_other, bias_other = hidden_backward(after(grads, bias_mine), [proj_other], pre_other)
     fc_bias_sum = jnp.concatenate([bias_mine, bias_other])
+    qkv_other = links.swap_core(after(qkv_mine, bias_mine))
     hidden_parts = hidden_sum(
-        (after(grad_mine, proj_sum_first), grad_other),
+        (after(grad_mine, attns), grad_other),
         [*fc_chips, fc_other],
         tok,
         links.sum_order,
         links.sum_cuts,
     )
-    hidden_far = links.sum_far(after(hidden_parts, attns))
-    (fc_sent,) = weight_terms(after(grad_other, hidden_parts, proj_sum), twos, 1)
+    hidden_far = links.sum_far(after(hidden_parts, proj_first) if z_n == 4 else hidden_parts)
+    proj_term = links.second_term(proj_own, proj_came, proj_first, units, hidden_parts)
+    proj_second = links.second_move(proj_term)
+    fc_sent = weight_terms(after(grad_other, hidden_far, proj_second), twos, links.term_slots, units)
     fc_came = links.swap_core(fc_sent)
-    fc_own = weight_terms(after(grad_mine, fc_sent, hidden_far), twos, z_n)
+    fc_own = weight_terms(after(grad_mine, fc_sent, hidden_far), twos, links.term_slots, units)
     hidden_near = links.sum_near(hidden_parts, hidden_far)
-    fc_terms = core_terms(after(fc_own, proj_sum), fc_came)
-    for m in range(z_n - 3, 0, -1):
-        proj_sum = links.chip_sum(proj_terms, m, proj_sum, hidden_parts)
-    fc_sum = links.chip_sum(fc_terms, z_n - 1, None, proj_sum)
+    fc_term = links.first_term(fc_own, fc_came, units)
+    fc_first = links.first_move(fc_term)
     mlp_parts = hidden_sum(
-        (after(act_mine, fc_own, proj_sum), act_other), [proj_mine, proj_other], tok, tuple(range(1, seq_n)), 1
-    )
-    hidden_near = after(hidden_near, mlp_parts, proj_sum)
+        (after(act_mine, fc_term), act_other), [proj_mine, proj_other], tok, tuple(range(1, seq_n)), 1
+    )
+    mlp_came = [links.from_rel(mlp_parts[r], seq_n - r) for r in range(1, seq_n)]
+
+    inverse_two = gate(inverse_two, mlp_parts)
 
     def middle_back(parts, far, near, normed_two, inverse_two, grad_low):
         grad_hidden = links.sum_end(parts, far, near)
@@ -762,9 +834,6 @@
         ]
         return links.exchange(after(sent, needed))
 
-    mlp_came = [links.from_rel(mlp_parts[r], seq_n - r) for r in range(1, seq_n) if r != far_place]
-    out_columns = to_owners(grad_middle_turned, mlp_came)
-    proj_grad = links.chip_total(proj_terms, 0, after(proj_sum, grad_middle_low))
 
     def ordered_parts(columns, rows):
         part = dot_nn(jnp.concatenate(columns, 1), jnp.concatenate(rows, 0))
@@ -773,8 +842,11 @@
         return sent, lax.dynamic_index_in_dim(part, links.core, 1, False)
 
     def ordered_terms(kept, came):
-        kept = (kept + came.astype(F32)).astype(BF)
-        return [lax.dynamic_index_in_dim(kept, links.chip_before(m), 0, False) for m in range(z_n)]
+        order = [links.z ^ k for k in (0, 2, 1, 3)] if z_n == 4 else [links.chip_before(m) for m in range(z_n)]
+        return [
+            jnp.concatenate([lax.dynamic_index_in_dim(member, k, 0, False) for k in order], 0)
+            for member in (kept.astype(BF), came)
+        ]
 
     def attend_back(out_full, grad_middle_low, query, pairs, attn, log_total):
         grad_attn = lax.dot_general(
@@ -794,14 +866,14 @@
         grad_query = grad_query.reshape(width, tok)
         return grad_query.astype(BF), jnp.sum(grad_query, 1), [parts[0]] + [part.astype(BF) for part in parts[1:]]
 
-    grad_middle_low = after(grad_middle_low, fc_sum)
+    log_total = gate(log_total, fc_first, grad_middle_low)
     grad_query, query_sum, parts = attend_back(out_full, grad_middle_low, query, pairs, attn, log_total
     )
-    fc_sum = links.chip_sum(fc_terms, z_n - 2, fc_sum, grad_middle_low)
-    came = links.exchange(parts)
+    came = links.exchange(after(parts, mlp_came))
+    fc_second = links.second_move(links.second_term(fc_own, fc_came, fc_first, units, parts))
+    out_columns = to_owners(grad_middle_turned, came)
     out_sent, out_kept = ordered_parts(after(out_columns, parts), attns)
     out_came = links.swap_core(out_sent)
-    qkv_full = lax.all_gather(after(qkv_weight, got), ("dp", "seq"), axis=0, tiled=True)
 
     def all_grads(grad_query, came):
         grad_pair = came[0]
@@ -809,20 +881,25 @@
             grad_pair = grad_pair + member.astype(F32)
         return jnp.concatenate([grad_query, grad_pair.astype(BF)], 0), jnp.sum(grad_pair[HDIM:], 1)
 
-    grad_qkv, value_sum = all_grads(grad_query, after(came, out_sent))
+    grad_qkv, value_sum = all_grads(grad_query, came)
     qkv_columns = to_owners(grad_qkv)
-    out_terms = ordered_terms(after(out_kept, grad_qkv, fc_sum), out_came)
-    for m in range(z_n - 3, 0, -1):
-        fc_sum = links.chip_sum(fc_terms, m, fc_sum, parts)
-    def tokens_back(grad_qkv, qkv_full, grad_middle, normed_one, inverse_one):
-        grad_hidden = dot_tn(grad_qkv, qkv_full)
+    out_rows = out_weight.shape[0]
+    out_own, out_came = ordered_terms(out_kept, out_came)
+    def tokens_back(grad_qkv, qkv_mine, qkv_other, grad_middle, normed_one, inverse_one):
+        by_core = grad_qkv.reshape(z_n, 2, seq_n, qkv_rows, tok)
+
+        def rows_of(core):
+            rows = lax.dynamic_index_in_dim(by_core, core, 1, False)
+            return rows.transpose(1, 0, 2, 3).reshape(-1, tok)
+
+        grad_hidden = dot_tn(rows_of(links.core), qkv_mine) + dot_tn(rows_of(1 - links.core), qkv_other)
         back = grad_middle + norm_back(grad_hidden * gain_one, normed_one, inverse_one)
         return back.astype(BF), [jnp.sum(grad_hidden * normed_one, 0), jnp.sum(grad_hidden, 0)]
 
     tokens_grad, late = tokens_back(
-        after(grad_qkv, out_terms), qkv_full, grad_middle, normed_one, inverse_one
-    )
-    out_sum = links.chip_sum(out_terms, z_n - 1, None, fc_sum)
+        grad_qkv, qkv_mine, qkv_other, grad_middle, normed_one, inverse_one
+    )
+    out_first = links.first_move(links.first_term(out_own, out_came, out_rows))
     tokens_grad = tokens_grad.reshape(tokens.shape)
     fc_bias_sum = jnp.sum(jnp.where(owner[:, :, None], fc_bias_sum.reshape(dp_n, 1, units), 0.0), 0)
     fc_bias_sum = jnp.where(own_seq[None, :, None], fc_bias_sum[:, None, :], 0.0).reshape(-1)
@@ -831,28 +908,26 @@
     while bit < seq_n:
         sums = sums + links.other_seq(sums, bit)
         bit *= 2
-    mlp_came.append(links.from_rel(after(mlp_parts[far_place], sums), seq_n - far_place))
     sums = sums + links.other_dp(sums, 1)
     qkv_sent, qkv_kept = ordered_parts(after(qkv_columns, tokens_grad), ones)
-    qkv_came = links.swap_core(after(qkv_sent, out_sum))
-    for m in range(z_n - 2, 0, -1):
-        out_sum = links.chip_sum(out_terms, m, out_sum)
-    qkv_terms = ordered_terms(qkv_kept, qkv_came)
-    qkv_sum = links.chip_sum(qkv_terms, z_n - 1, None)
+    qkv_came = links.swap_core(qkv_sent)
+    qkv_own, qkv_came = ordered_terms(qkv_kept, qkv_came)
+    out_second = links.second_move(links.second_term(out_own, out_came, out_first, out_rows))
+    qkv_first = links.first_move(links.first_term(qkv_own, qkv_came, qkv_rows), fc_second)
     bit = 2
-    for m in range(z_n - 2, 0, -1):
-        moved = links.other_dp(sums, bit) if bit < dp_n else 0.0
-        bit *= 2
-        qkv_sum = links.chip_sum(qkv_terms, m, qkv_sum)
-        sums = after(sums, qkv_sum) + moved
+    moved = links.other_dp(sums, bit)
+    qkv_second = links.second_move(links.second_term(qkv_own, qkv_came, qkv_first, qkv_rows))
+    sums = after(sums, qkv_second) + moved
+    bit *= 2
     while bit < dp_n:
         sums = sums + links.other_dp(sums, bit)
         bit *= 2
-    fc_grad = links.chip_total(fc_terms, 0, after(fc_sum, qkv_terms))
-    out_grad = links.chip_total(out_terms, 0, after(out_sum, fc_grad))
-    mlp = sum(member.astype(F32) for member in [mlp_parts[0], *after(mlp_came, out_grad)])
+    proj_grad = links.chip_sum_end(proj_own, proj_came, proj_first, proj_second, units, qkv_own)
+    fc_grad = links.chip_sum_end(fc_own, fc_came, fc_first, fc_second, units, qkv_own)
+    out_grad = links.chip_sum_end(out_own, out_came, out_first, out_second, out_rows)
+    mlp = sum(member.astype(F32) for member in [mlp_parts[0], *after(mlp_came, fc_grad)])
     block_out = (middle + mlp + proj_shift).astype(BF).reshape(tokens.shape)
-    qkv_grad = links.chip_total(qkv_terms, 0, after(qkv_sum, block_out))
+    qkv_grad = links.chip_sum_end(qkv_own, qkv_came, qkv_first, qkv_second, qkv_rows)
 
     wide = [sums[i * width : (i + 1) * width] for i in range(7)]
     fc_bias_grad = sums[7 * width : 7 * width + fc_bias.shape[0]]

time: 677 us -> 651 us (0.962)
  waiting for transfers between devices: 270 us -> 238 us
  Pallas kernels: 113 us -> 139 us
  other arithmetic: 62.1 us -> 37.9 us
  starting transfers between devices: 95.2 us -> 82.7 us
    ppermute x40, waiting for transfers between devices: 120 us -> 82.3 us  [from_rel(): return lax.ppermute(value, 'seq', pairs)]
    pallas_call x0 -> x11, Pallas kernels: none -> 26 us  [the longest x9 26 us: add_terms(): pl.pallas_call(kernel, name='add_terms', grid=(rows // step,), out_shape=...]
    ppermute x9, starting transfers between devices: 37.9 us -> 20.4 us  [z_next(): lax.ppermute(value, 'dp', [(2 * i + c, 2 * j + c) for i, j in pairs for c...]
    ppermute x9, waiting for transfers between devices: 58.9 us -> 75 us  [z_next(): lax.ppermute(value, 'dp', [(2 * i + c, 2 * j + c) for i, j in pairs for c...]
    all_gather x1, waiting for transfers between devices: 15 us -> 0.01 us  [shards(): out_full = lax.all_gather(out_weight, ('dp', 'seq'), axis=0, tiled=True)]
    convert_element_type x12 -> x1, other arithmetic: 15.2 us -> 1.07 us  [second_term(): (add_wide(own[part], came[part]) + first[part].astype(F32)).astype(BF)]
    ppermute x40, starting transfers between devices: 41.2 us -> 50.4 us  [from_rel(): return lax.ppermute(value, 'seq', pairs)]
    unnamed x295 -> x314, local copies, waits for them, and re-layouts: 31.4 us -> 39.2 us
  transfers between devices with their start and end apart: 75 -> 72, of which waited for: 45 -> 40; matrix products, arithmetic and copies ran while one was open for 21% -> 21% of each run, Pallas kernels for 15% -> 19%
where the time goes in v2:
time: 651 us; the launch traced here: 643 us
  waiting for transfers between devices  238 us (37%)
  Pallas kernels  139 us (21%)
  starting transfers between devices  82.7 us (13%)
  matrix products  66.8 us (10%)
  local copies, waits for them, and re-layouts  61.4 us (9%)
  other arithmetic  37.9 us (6%)
  between operations  17.1 us (3%)
    pallas_call x12, Pallas kernels, call(): pl.pallas_call(kernel, name=name, out_shape=out_shape, in_specs=[ANY] * l...  113 us
    ppermute x40, waiting for transfers between devices, from_rel(): return lax.ppermute(value, 'seq', pairs)  82.3 us
    ppermute x9, waiting for transfers between devices, z_next(): lax.ppermute(value, 'dp', [(2 * i + c, 2 * j + c) for i, j in pairs for c...  75 us
    ppermute x8, waiting for transfers between devices, other_chip(): return lax.ppermute(value, 'dp', pairs)  63.6 us
    ppermute x40, starting transfers between devices, from_rel(): return lax.ppermute(value, 'seq', pairs)  50.4 us
    unnamed x314, local copies, waits for them, and re-layouts  39.2 us
    pallas_call x9, Pallas kernels, add_terms(): pl.pallas_call(kernel, name='add_terms', grid=(rows // step,), out_shape=...  26 us
    ppermute x9, starting transfers between devices, z_next(): lax.ppermute(value, 'dp', [(2 * i + c, 2 * j + c) for i, j in pairs for c...  20.4 us
  transfers between devices with their start and end apart: 72, of which 40 were waited for; matrix products, arithmetic and copies ran while one was open for 21% of the time, Pallas kernels for 19%

profile of v2, /device:TPU:0, one launch (start us, length us, event | category | flops | bytes accessed | tf_op | source)
XLA Modules:
  0.0 642.9 jit_solution(6312817990765928895)
XLA Ops:
  23.9 8.8 %collective-permute-done.1 = bf16[72,2048]{1,0:T(8,128)(2,1)} collective-permute-done((bf16[72,2048]{1,0:T(8,128)(2,1)S(1)}, bf16[72,2048]{1,0:T(8,128)(2,1)}, u32[]{:S(2)}, u32[]{:S(2)}) %collective-permute-start.1) | collective-permute-done | bytes 294944 | tf_op jit(solution)/shard_map/ppermute | solution.py:480
  36.3 5.8 collective-permute-done.2
  75.0 6.5 %collective-permute-done.9 = bf16[576,256]{1,0:T(8,128)(2,1)S(1)} collective-permute-done((bf16[576,256]{1,0:T(8,128)(2,1)}, bf16[576,256]{1,0:T(8,128)(2,1)S(1)}, u32[]{:S(2)}, u32[]{:S(2)}) %collective-permute-start.9) | collective-permute-done | bytes 294944 | tf_op jit(solution)/shard_map/ppermute | solution.py:472
  97.0 6.8 %collective-permute-done.12 = bf16[272,256]{1,0:T(8,128)(2,1)S(1)} collective-permute-done((bf16[272,256]{1,0:T(8,128)(2,1)S(1)}, bf16[272,256]{1,0:T(8,128)(2,1)S(1)}, u32[]{:S(2)}, u32[]{:S(2)}) %collective-permute-start.12) | collective-permute-done | bytes 139296 | tf_op jit(solution)/shard_map/ppermute | solution.py:472
  117.8 5.0 bitcast_convert_fusion.3
  122.7 17.1 %collective-permute-done.21.refs_7_.refs_2_.refs_4_ = bf16[256,2048]{1,0:T(8,128)(2,1)} collective-permute-done((bf16[256,2048]{1,0:T(8,128)(2,1)S(1)}, bf16[256,2048]{1,0:T(8,128)(2,1)}, u32[]{:S(2)}, u32[]{:S(2)}) %collective-permute-start.21) | collective-permute-done | bytes 1048608 | tf_op jit(solution)/shard_map/ppermute | solution.py:480
  140.6 6.3 fusion.110
  150.3 13.5 %collective-permute-done.23.refs_8_.refs_3_.refs_5_ = bf16[256,2048]{1,0:T(8,128)(2,1)} collective-permute-done((bf16[256,2048]{1,0:T(8,128)(2,1)}, bf16[256,2048]{1,0:T(8,128)(2,1)}, u32[]{:S(2)}, u32[]{:S(2)}) %collective-permute-start.23) | collective-permute-done | bytes 1048608 | tf_op jit(solution)/shard_map/ppermute | solution.py:480
  163.8 7.1 %collective-permute-done.16.refs_1_.refs_2_ = bf16[256,2048]{1,0:T(8,128)(2,1)S(1)} collective-permute-done((bf16[256,2048]{1,0:T(8,128)(2,1)S(1)}, bf16[256,2048]{1,0:T(8,128)(2,1)S(1)}, u32[]{:S(2)}, u32[]{:S(2)}) %collective-permute-start.16) | collective-permute-done | bytes 1048608 | tf_op jit(solution)/shard_map/ppermute | solution.py:472
  181.4 21.3 %collective-permute-done.22.refs_6_.refs_1_ = bf16[256,2048]{1,0:T(8,128)(2,1)} collective-permute-done((bf16[256,2048]{1,0:T(8,128)(2,1)S(1)}, bf16[256,2048]{1,0:T(8,128)(2,1)}, u32[]{:S(2)}, u32[]{:S(2)}) %collective-permute-start.22) | collective-permute-done | bytes 1048608 | tf_op jit(solution)/shard_map/ppermute | solution.py:480
  210.1 10.4 %hidden_forward.3 = (f32[1024,1024]{1,0:T(8,128)}, bf16[1024,1024]{1,0:T(8,128)(2,1)S(1)}) custom-call(bf16[256,2048]{1,0:T(8,128)(2,1)S(1)} %add_convert_fusion.1.refs_0_.refs_1_, bf16[256,2048]{1,0:T(8,128)(2,1)S(1)} %copy-done.31, bf16[128,2048]{1,0:T(8,128)(2,1)} %collective-permute-done.17.refs_2_.refs_3_, ...), custom_call_target="tpu_custom_call" | custom-call | flops 4294967296 | bytes 14684160 | tf_op jit(solution)/shard_map/hidden_forward/pallas_call | solution.py:56
  222.7 6.9 %collective-permute-done.27.refs_7_.refs_2_ = bf16[256,2048]{1,0:T(8,128)(2,1)S(1)} collective-permute-done((bf16[256,2048]{1,0:T(8,128)(2,1)}, bf16[256,2048]{1,0:T(8,128)(2,1)S(1)}, u32[]{:S(2)}, u32[]{:S(2)}) %collective-permute-start.27) | collective-permute-done | bytes 1048608 | tf_op jit(solution)/shard_map/ppermute | solution.py:480
  229.6 9.0 %weight_terms.4 = bf16[1024,2048]{1,0:T(8,128)(2,1)} custom-call(bf16[1024,1024]{1,0:T(8,128)(2,1)S(1)} %get-tuple-element.166.refs_0_.refs_1_, bf16[256,2048]{1,0:T(8,128)(2,1)S(1)} %bitcast.235, bf16[256,2048]{1,0:T(8,128)(2,1)} %collective-permute-done.14.refs_2_.refs_1_, bf16[128,2048]{1,0:T(8,128)(2,1)S(1)} %collective-permute-done.24.refs_3_.refs_2_, ...), custom_call_target="tpu_custom_call" | custom-call | flops 4294967296 | bytes 10485760 | tf_op jit(solution)/shard_map/weight_terms/pallas_call | solution.py:56
  242.4 9.8 %hidden_forward.2 = (f32[1024,1024]{1,0:T(8,128)}, bf16[1024,1024]{1,0:T(8,128)(2,1)}) custom-call(bf16[256,2048]{1,0:T(8,128)(2,1)S(1)} %add_convert_fusion.1.refs_0_.refs_1_, bf16[256,2048]{1,0:T(8,128)(2,1)S(1)} %copy-done.31, bf16[128,2048]{1,0:T(8,128)(2,1)} %collective-permute-done.17.refs_2_.refs_3_, ...), custom_call_target="tpu_custom_call" | custom-call | flops 4294967296 | bytes 14684160 | tf_op jit(solution)/shard_map/hidden_forward/pallas_call | solution.py:56
  253.8 8.9 %weight_terms.5.refs_0_ = bf16[1024,2048]{1,0:T(8,128)(2,1)} custom-call(bf16[1024,1024]{1,0:T(8,128)(2,1)S(1)} %copy-done.56, bf16[256,2048]{1,0:T(8,128)(2,1)S(1)} %bitcast.236, bf16[256,2048]{1,0:T(8,128)(2,1)} %collective-permute-done.14.refs_2_.refs_1_, bf16[128,2048]{1,0:T(8,128)(2,1)S(1)} %collective-permute-done.24.refs_3_.refs_2_, ...), custom_call_target="tpu_custom_call" | custom-call | flops 4294967296 | bytes 10485760 | tf_op jit(solution)/shard_map/weight_terms/pallas_call | solution.py:56
  290.2 10.6 %hidden_backward.2 = (bf16[1024,1024]{1,0:T(8,128)(2,1)}, f32[1,1024]{1,0:T(1,128)S(1)}) custom-call(bf16[256,2048]{1,0:T(8,128)(2,1)S(1)} %bitcast.237, bf16[256,2048]{1,0:T(8,128)(2,1)} %collective-permute-done.14.refs_2_.refs_1_, bf16[128,2048]{1,0:T(8,128)(2,1)S(1)} %copy-done.47, bf16[128,2048]{1,0:T(8,128)(2,1)S(1)} %copy-done.49, ...), custom_call_target="tpu_custom_call" | custom-call | flops 4294967296 | bytes 14684160 | tf_op jit(solution)/shard_map/hidden_backward/pallas_call | solution.py:56
  300.9 7.8 %collective-permute-done.33 = bf16[128,2048]{0,1:T(8,128)(2,1)S(1)} collective-permute-done((bf16[128,2048]{0,1:T(8,128)(2,1)S(1)}, bf16[128,2048]{0,1:T(8,128)(2,1)S(1)}, u32[]{:S(2)}, u32[]{:S(2)}) %collective-permute-start.33) | collective-permute-done | bytes 524320 | tf_op jit(solution)/shard_map/ppermute | solution.py:472
  310.0 11.1 %hidden_backward.3 = (bf16[1024,1024]{1,0:T(8,128)(2,1)S(1)}, f32[1,1024]{1,0:T(1,128)S(1)}) custom-call(bf16[256,2048]{1,0:T(8,128)(2,1)S(1)} %bitcast.238, bf16[256,2048]{1,0:T(8,128)(2,1)} %collective-permute-done.14.refs_2_.refs_1_, bf16[128,2048]{1,0:T(8,128)(2,1)S(1)} %copy-done.47, bf16[128,2048]{1,0:T(8,128)(2,1)S(1)} %copy-done.50, ...), custom_call_target="tpu_custom_call" | custom-call | flops 4294967296 | bytes 14684160 | tf_op jit(solution)/shard_map/hidden_backward/pallas_call | solution.py:56
  322.4 14.7 %hidden_sum.2 = (f32[256,2048]{1,0:T(8,128)S(1)}, bf16[128,2048]{1,0:T(8,128)(2,1)S(1)}, bf16[128,2048]{1,0:T(8,128)(2,1)S(1)}, bf16[128,2048]{1,0:T(8,128)(2,1)...) custom-call(bf16[1024,1024]{1,0:T(8,128)(2,1)} %get-tuple-element.200.refs_0_, ...), custom_call_target="tpu_custom_call" | custom-call | flops 8589934592 | bytes 17825792 | tf_op jit(solution)/shard_map/hidden_sum/pallas_call | solution.py:56
  351.3 6.7 %collective-permute-done.36 = bf16[128,2048]{1,0:T(8,128)(2,1)S(1)} collective-permute-done((bf16[128,2048]{1,0:T(8,128)(2,1)S(1)}, bf16[128,2048]{1,0:T(8,128)(2,1)S(1)}, u32[]{:S(2)}, u32[]{:S(2)}) %collective-permute-start.36) | collective-permute-done | bytes 524320 | tf_op jit(solution)/shard_map/ppermute | solution.py:472
  360.3 7.3 %collective-permute-done.38 = bf16[128,2048]{1,0:T(8,128)(2,1)S(1)} collective-permute-done((bf16[128,2048]{1,0:T(8,128)(2,1)S(1)}, bf16[128,2048]{1,0:T(8,128)(2,1)S(1)}, u32[]{:S(2)}, u32[]{:S(2)}) %collective-permute-start.38) | collective-permute-done | bytes 524320 | tf_op jit(solution)/shard_map/ppermute | solution.py:472
  370.5 16.3 %collective-permute-done.40.refs_3_ = bf16[256,2048]{1,0:T(8,128)(2,1)} collective-permute-done((bf16[256,2048]{1,0:T(8,128)(2,1)}, bf16[256,2048]{1,0:T(8,128)(2,1)}, u32[]{:S(2)}, u32[]{:S(2)}) %collective-permute-start.40) | collective-permute-done | bytes 1048608 | tf_op jit(solution)/shard_map/ppermute | solution.py:563
  388.4 8.6 %weight_terms.6 = bf16[1024,2048]{1,0:T(8,128)(2,1)} custom-call(bf16[1024,1024]{1,0:T(8,128)(2,1)S(1)} %copy-done.53, bf16[256,2048]{1,0:T(8,128)(2,1)S(1)} %copy-done.12, bf16[256,2048]{1,0:T(8,128)(2,1)S(1)} %copy-done.32, bf16[128,2048]{1,0:T(8,128)(2,1)} %collective-permute-done.17.refs_2_.refs_3_, ...), custom_call_target="tpu_custom_call" | custom-call | flops 4294967296 | bytes 10485760 | tf_op jit(solution)/shard_map/weight_terms/pallas_call | solution.py:56
  416.0 8.8 %weight_terms.7.refs_0_ = bf16[1024,2048]{1,0:T(8,128)(2,1)} custom-call(bf16[1024,1024]{1,0:T(8,128)(2,1)S(1)} %copy-done.51, bf16[256,2048]{1,0:T(8,128)(2,1)S(1)} %copy-done.13, bf16[256,2048]{1,0:T(8,128)(2,1)S(1)} %copy-done.33, bf16[128,2048]{1,0:T(8,128)(2,1)} %collective-permute-done.17.refs_2_.refs_3_, ...), custom_call_target="tpu_custom_call" | custom-call | flops 4294967296 | bytes 10485760 | tf_op jit(solution)/shard_map/weight_terms/pallas_call | solution.py:56
  430.8 6.1 add_terms.11
  436.9 14.0 %hidden_sum.3 = (f32[256,2048]{1,0:T(8,128)S(1)}, bf16[256,2048]{1,0:T(8,128)(2,1)}, bf16[256,2048]{1,0:T(8,128)(2,1)}, bf16[256,2048]{1,0:T(8,128)(2,1)}) custom-call(bf16[1024,1024]{1,0:T(8,128)(2,1)S(1)} %copy-done.57, bf16[1024,1024]{1,0:T(8,128)(2,1)S(1)} %copy-done.55, bf16[1024,2048]{1,0:T(8,128)(2,1)} %join_rows.3.refs_2_, ...), custom_call_target="tpu_custom_call" | custom-call | flops 8589934592 | bytes 17825792 | tf_op jit(solution)/shard_map/hidden_sum/pallas_call | solution.py:56
  459.6 6.7 %fusion.21 = bf16[2048,256]{0,1:T(8,128)(2,1)} fusion(bf16[256,2048]{1,0:T(8,128)(2,1)S(1)} %convert_element_type.374, bf16[2048,2048]{1,0:T(8,128)(2,1)} %all-gather.3.cloned.1.call-done), kind=kOutput, calls=%fused_computation.29 | convolution fusion | flops 2148007936 | bytes 10485760 | tf_op jit(solution)/shard_map/dot_general | solution.py:852
  475.8 29.9 %collective-permute-done.45.refs_2_ = bf16[512,2048]{1,0:T(8,128)(2,1)} collective-permute-done((bf16[512,2048]{1,0:T(8,128)(2,1)}, bf16[512,2048]{1,0:T(8,128)(2,1)}, u32[]{:S(2)}, u32[]{:S(2)}) %collective-permute-start.45) | collective-permute-done | bytes 2097184 | tf_op jit(solution)/shard_map/ppermute | solution.py:563
  505.9 9.2 %fusion.32 = f32[128,1024]{1,0:T(8,128)S(1)} fusion(bf16[16,128,256]{2,1,0:T(8,128)(2,1)} %bitcast.249, f32[16,1024,256]{1,2,0:T(8,128)} %copy-done.67, f32[16,256]{1,0:T(8,128)S(1)} %bitcast.274, pred[1024,256]{0,1:T(8,128)(4,1)S(1)} %copy-done.94), kind=kOutput, calls=%fused_computation.65 | convolution fusion | flops 1086324736 | bytes 18628608 | tf_op jit(solution)/shard_map/hkq,hdq->dk/dot_general | solution.py:863
  515.2 8.3 %fusion = bf16[16,1024,256]{1,2,0:T(8,128)(2,1)S(1)} fusion(f32[16,1024,256]{1,2,0:T(8,128)} %copy-done.67, bf16[16,128,256]{2,1,0:T(8,128)(2,1)S(1)} %bitcast.250, f32[16,256]{1,0:T(8,128)S(1)} %fusion.31, f32[16,256]{1,0:T(8,128)S(1)} %bitcast.275, pred[1024,256]{0,1:T(8,128)(4,1)S(1)} %copy-done.94, bf16[128,256]{1,0:T(8,128)(2,1)S(1)} %copy-done.128, ...), kind=kOutput, calls=%fused_computation.1 | convolution fusion | flops 1095761920 | bytes 26771456 | tf_op jit(solution)/shard_map/dk,hdq->hkq/dot_general | solution.py:859
  541.0 4.6 fusion.29
  608.9 13.0 %collective-permute-done.69.refs_3_ = bf16[64,2048]{1,0:T(8,128)(2,1)S(1)} collective-permute-done((bf16[64,2048]{1,0:T(8,128)(2,1)S(1)}, bf16[64,2048]{1,0:T(8,128)(2,1)S(1)}, u32[]{:S(2)}, u32[]{:S(2)}) %collective-permute-start.69) | collective-permute-done | bytes 262176 | tf_op jit(solution)/shard_map/ppermute | solution.py:563
  (588 shorter events, 298.9 us)
Async XLA Ops:
  7.2 133.4 %all-gather.3.cloned.1.call-start = ((), (), s32[]{:S(2)}) async-start(), calls=%async_computation | async-start | bytes 8650752 | tf_op jit(solution)/shard_map/all_gather | solution.py:678
  7.9 397.8 %all-gather.5.cloned.1.call-start = ((), (), s32[]{:S(2)}) async-start(), calls=%async_computation.1 | async-start | bytes 5898240 | tf_op jit(solution)/shard_map/all_gather | solution.py:762
  18.6 26.0 %collective-permute-start.3 = (bf16[256,2048]{1,0:T(8,128)(2,1)S(1)}, bf16[256,2048]{1,0:T(8,128)(2,1)}, u32[]{:S(2)}, u32[]{:S(2)}) collective-permute-start(bf16[256,2048]{1,0:T(8,128)(2,1)S(1)} %fusion.23), channel_id=1, source_target_pairs={{1,0},{3,1},{2,3},{0,2},{5,4},{7,5},{6,7},{4,6},{9,8},{11,9},{10,1... | collective-permute-start | bytes 3145736 | tf_op jit(solution)/shard_map/ppermute | solution.py:472
  20.2 25.6 %collective-permute-start.4 = (bf16[256,2048]{1,0:T(8,128)(2,1)S(1)}, bf16[256,2048]{1,0:T(8,128)(2,1)S(1)}, u32[]{:S(2)}, u32[]{:S(2)}) collective-permute-start(bf16[256,2048]{1,0:T(8,128)(2,1)S(1)} %fusion.23), channel_id=1, source_target_pairs={{2,0},{0,1},{1,3},{3,2},{6,4},{4,5},{5,7},{7,6},{10,8},{8,9},{9,11... | collective-permute-start | bytes 3145736 | tf_op jit(solution)/shard_map/ppermute | solution.py:472
  49.1 57.3 %collective-permute-start.20 = (bf16[256,2048]{1,0:T(8,128)(2,1)S(1)}, bf16[256,2048]{1,0:T(8,128)(2,1)S(1)}, u32[]{:S(2)}, u32[]{:S(2)}) collective-permute-start(bf16[256,2048]{1,0:T(8,128)(2,1)S(1)} %copy-done.16), channel_id=1, source_target_pairs={{8,0},{12,4},{0,16},{4,20},{16,24},{20,28},{24,8},{28,12},{9,1},{1... | collective-permute-start | bytes 3145736 | tf_op jit(solution)/shard_map/ppermute | solution.py:480
  104.3 43.9 %collective-permute-start.14 = (bf16[256,2048]{1,0:T(8,128)(2,1)S(1)}, bf16[256,2048]{1,0:T(8,128)(2,1)}, u32[]{:S(2)}, u32[]{:S(2)}) collective-permute-start(bf16[256,2048]{1,0:T(8,128)(2,1)S(1)} %bitcast.233), channel_id=1, source_target_pairs={{1,0},{3,1},{2,3},{0,2},{5,4},{7,5},{6,7},{4,6},{9,8},{11,9},{10,1... | collective-permute-start | bytes 3145736 | tf_op jit(solution)/shard_map/ppermute | solution.py:472
  104.8 43.4 %collective-permute-start.15 = (bf16[256,2048]{1,0:T(8,128)(2,1)S(1)}, bf16[256,2048]{1,0:T(8,128)(2,1)}, u32[]{:S(2)}, u32[]{:S(2)}) collective-permute-start(bf16[256,2048]{1,0:T(8,128)(2,1)S(1)} %bitcast.234), channel_id=1, source_target_pairs={{2,0},{0,1},{1,3},{3,2},{6,4},{4,5},{5,7},{7,6},{10,8},{8,9},{9,11... | collective-permute-start | bytes 3145736 | tf_op jit(solution)/shard_map/ppermute | solution.py:472
  106.4 33.5 %collective-permute-start.21 = (bf16[256,2048]{1,0:T(8,128)(2,1)S(1)}, bf16[256,2048]{1,0:T(8,128)(2,1)}, u32[]{:S(2)}, u32[]{:S(2)}) collective-permute-start(bf16[256,2048]{1,0:T(8,128)(2,1)S(1)} %collective-permute-done.20.refs_6_.refs_1_.refs_3_), channel_id=1, source_target_pairs={{8,0},{12,4},{0,16},{4,20},{16,24},{20,28},{24,8},{28,12},{9,1},{1... | collective-permute-start | bytes 3145736 | tf_op jit(solution)/shard_map/ppermute | solution.py:480
  176.9 33.2 %collective-permute-start.26 = (bf16[1024,2048]{1,0:T(8,128)(2,1)}, bf16[1024,2048]{1,0:T(8,128)(2,1)}, u32[]{:S(2)}, u32[]{:S(2)}) collective-permute-start(bf16[1024,2048]{1,0:T(8,128)(2,1)} %join_rows.2), channel_id=1, source_target_pairs={{0,4},{4,0},{8,12},{12,8},{16,20},{20,16},{24,28},{28,24},{1,5},{5... | collective-permute-start | bytes 12582920 | tf_op jit(solution)/shard_map/ppermute | solution.py:476
  177.0 25.7 %collective-permute-start.22 = (bf16[256,2048]{1,0:T(8,128)(2,1)S(1)}, bf16[256,2048]{1,0:T(8,128)(2,1)}, u32[]{:S(2)}, u32[]{:S(2)}) collective-permute-start(bf16[256,2048]{1,0:T(8,128)(2,1)S(1)} %copy-done.14), channel_id=1, source_target_pairs={{8,0},{12,4},{0,16},{4,20},{16,24},{20,28},{24,8},{28,12},{9,1},{1... | collective-permute-start | bytes 3145736 | tf_op jit(solution)/shard_map/ppermute | solution.py:480
  178.3 24.4 %collective-permute-start.17 = (bf16[128,2048]{1,0:T(8,128)(2,1)}, bf16[128,2048]{1,0:T(8,128)(2,1)}, u32[]{:S(2)}, u32[]{:S(2)}) collective-permute-start(bf16[128,2048]{1,0:T(8,128)(2,1)} %slice.234), channel_id=1, source_target_pairs={{1,0},{3,1},{2,3},{0,2},{5,4},{7,5},{6,7},{4,6},{9,8},{11,9},{10,1... | collective-permute-start | bytes 1572872 | tf_op jit(solution)/shard_map/ppermute | solution.py:472
  202.7 26.9 %collective-permute-start.27 = (bf16[256,2048]{1,0:T(8,128)(2,1)}, bf16[256,2048]{1,0:T(8,128)(2,1)S(1)}, u32[]{:S(2)}, u32[]{:S(2)}) collective-permute-start(bf16[256,2048]{1,0:T(8,128)(2,1)} %collective-permute-done.22.refs_6_.refs_1_), channel_id=1, source_target_pairs={{8,0},{12,4},{0,16},{4,20},{16,24},{20,28},{24,8},{28,12},{9,1},{1... | collective-permute-start | bytes 3145736 | tf_op jit(solution)/shard_map/ppermute | solution.py:480
  238.7 27.2 %collective-permute-start.29 = (bf16[1024,2048]{1,0:T(8,128)(2,1)}, bf16[1024,2048]{1,0:T(8,128)(2,1)S(1)}, u32[]{:S(2)}, u32[]{:S(2)}) collective-permute-start(bf16[1024,2048]{1,0:T(8,128)(2,1)} %weight_terms.4), channel_id=1, source_target_pairs={{0,4},{4,0},{8,12},{12,8},{16,20},{20,16},{24,28},{28,24},{1,5},{5... | collective-permute-start | bytes 12582920 | tf_op jit(solution)/shard_map/ppermute | solution.py:476
  238.8 25.8 %collective-permute-start.30 = (bf16[256,2048]{0,1:T(8,128)(2,1)}, bf16[256,2048]{0,1:T(8,128)(2,1)S(1)}, u32[]{:S(2)}, u32[]{:S(2)}) collective-permute-start(bf16[256,2048]{0,1:T(8,128)(2,1)} %bitcast.26), channel_id=1, source_target_pairs={{1,0},{3,1},{2,3},{0,2},{5,4},{7,5},{6,7},{4,6},{9,8},{11,9},{10,1... | collective-permute-start | bytes 3145736 | tf_op jit(solution)/shard_map/ppermute | solution.py:472
  240.5 25.4 %collective-permute-start.31 = (bf16[256,2048]{0,1:T(8,128)(2,1)}, bf16[256,2048]{0,1:T(8,128)(2,1)S(1)}, u32[]{:S(2)}, u32[]{:S(2)}) collective-permute-start(bf16[256,2048]{0,1:T(8,128)(2,1)} %bitcast.26), channel_id=1, source_target_pairs={{2,0},{0,1},{1,3},{3,2},{6,4},{4,5},{5,7},{7,6},{10,8},{8,9},{9,11... | collective-permute-start | bytes 3145736 | tf_op jit(solution)/shard_map/ppermute | solution.py:472
  240.8 34.8 %collective-permute-start.28 = (bf16[256,2048]{1,0:T(8,128)(2,1)S(1)}, bf16[256,2048]{1,0:T(8,128)(2,1)S(1)}, u32[]{:S(2)}, u32[]{:S(2)}) collective-permute-start(bf16[256,2048]{1,0:T(8,128)(2,1)S(1)} %collective-permute-done.27.refs_7_.refs_2_), channel_id=1, source_target_pairs={{8,0},{12,4},{0,16},{4,20},{16,24},{20,28},{24,8},{28,12},{9,1},{1... | collective-permute-start | bytes 3145736 | tf_op jit(solution)/shard_map/ppermute | solution.py:480
  279.4 30.6 %collective-permute-start.32 = (bf16[1024,2048]{1,0:T(8,128)(2,1)}, bf16[1024,2048]{1,0:T(8,128)(2,1)}, u32[]{:S(2)}, u32[]{:S(2)}) collective-permute-start(bf16[1024,2048]{1,0:T(8,128)(2,1)} %join_rows.3.refs_2_), channel_id=1, source_target_pairs={{0,4},{4,0},{8,12},{12,8},{16,20},{20,16},{24,28},{28,24},{1,5},{5... | collective-permute-start | bytes 12582920 | tf_op jit(solution)/shard_map/ppermute | solution.py:476
  279.5 57.7 %collective-permute-start.35 = (bf16[512,2048]{1,0:T(8,128)(2,1)}, bf16[512,2048]{1,0:T(8,128)(2,1)S(1)}, u32[]{:S(2)}, u32[]{:S(2)}) collective-permute-start(bf16[512,2048]{1,0:T(8,128)(2,1)} %copy-done.9), channel_id=1, source_target_pairs={{0,8},{4,12},{8,0},{12,4},{16,24},{20,28},{24,16},{28,20},{1,9},{5... | collective-permute-start | bytes 6291464 | tf_op jit(solution)/shard_map/ppermute | solution.py:563
  284.4 24.3 %collective-permute-start.33 = (bf16[128,2048]{0,1:T(8,128)(2,1)S(1)}, bf16[128,2048]{0,1:T(8,128)(2,1)S(1)}, u32[]{:S(2)}, u32[]{:S(2)}) collective-permute-start(bf16[128,2048]{0,1:T(8,128)(2,1)S(1)} %slice.194), channel_id=1, source_target_pairs={{1,0},{3,1},{2,3},{0,2},{5,4},{7,5},{6,7},{4,6},{9,8},{11,9},{10,1... | collective-permute-start | bytes 1572872 | tf_op jit(solution)/shard_map/ppermute | solution.py:472
  285.1 24.9 %collective-permute-start.34 = (bf16[128,2048]{0,1:T(8,128)(2,1)S(1)}, bf16[128,2048]{0,1:T(8,128)(2,1)S(1)}, u32[]{:S(2)}, u32[]{:S(2)}) collective-permute-start(bf16[128,2048]{0,1:T(8,128)(2,1)S(1)} %slice.195), channel_id=1, source_target_pairs={{2,0},{0,1},{1,3},{3,2},{6,4},{4,5},{5,7},{7,6},{10,8},{8,9},{9,11... | collective-permute-start | bytes 1572872 | tf_op jit(solution)/shard_map/ppermute | solution.py:472
  341.3 45.5 %collective-permute-start.40 = (bf16[256,2048]{1,0:T(8,128)(2,1)}, bf16[256,2048]{1,0:T(8,128)(2,1)}, u32[]{:S(2)}, u32[]{:S(2)}) collective-permute-start(bf16[256,2048]{1,0:T(8,128)(2,1)} %add_terms.10), channel_id=1, source_target_pairs={{0,16},{4,20},{8,24},{12,28},{16,0},{20,4},{24,8},{28,12},{1,17},{... | collective-permute-start | bytes 3145736 | tf_op jit(solution)/shard_map/ppermute | solution.py:563
  397.1 32.1 %collective-permute-start.41 = (bf16[1024,2048]{1,0:T(8,128)(2,1)}, bf16[1024,2048]{1,0:T(8,128)(2,1)}, u32[]{:S(2)}, u32[]{:S(2)}) collective-permute-start(bf16[1024,2048]{1,0:T(8,128)(2,1)} %weight_terms.6), channel_id=1, source_target_pairs={{0,4},{4,0},{8,12},{12,8},{16,20},{20,16},{24,28},{28,24},{1,5},{5... | collective-permute-start | bytes 12582920 | tf_op jit(solution)/shard_map/ppermute | solution.py:476
  405.7 135.1 %collective-permute-start.54 = (bf16[1152,2048]{1,0:T(8,128)(2,1)}, bf16[1152,2048]{1,0:T(8,128)(2,1)}, u32[]{:S(2)}, u32[]{:S(2)}) collective-permute-start(bf16[1152,2048]{1,0:T(8,128)(2,1)} %bitcast.281), channel_id=1, source_target_pairs={{0,4},{4,0},{8,12},{12,8},{16,20},{20,16},{24,28},{28,24},{1,5},{5... | collective-permute-start | bytes 14155784 | tf_op jit(solution)/shard_map/ppermute | solution.py:476
  452.2 72.7 %collective-permute-start.42 = (bf16[256,2048]{1,0:T(8,128)(2,1)}, bf16[256,2048]{1,0:T(8,128)(2,1)}, u32[]{:S(2)}, u32[]{:S(2)}) collective-permute-start(bf16[256,2048]{1,0:T(8,128)(2,1)} %get-tuple-element.203), channel_id=1, source_target_pairs={{2,0},{0,1},{1,3},{3,2},{6,4},{4,5},{5,7},{7,6},{10,8},{8,9},{9,11... | collective-permute-start | bytes 3145736 | tf_op jit(solution)/shard_map/ppermute | solution.py:472
  452.5 72.5 %collective-permute-start.43 = (bf16[256,2048]{1,0:T(8,128)(2,1)}, bf16[256,2048]{1,0:T(8,128)(2,1)}, u32[]{:S(2)}, u32[]{:S(2)}) collective-permute-start(bf16[256,2048]{1,0:T(8,128)(2,1)} %get-tuple-element.204), channel_id=1, source_target_pairs={{3,0},{2,1},{0,3},{1,2},{7,4},{6,5},{4,7},{5,6},{11,8},{10,9},{8,1... | collective-permute-start | bytes 3145736 | tf_op jit(solution)/shard_map/ppermute | solution.py:472
  454.0 71.0 %collective-permute-start.44 = (bf16[256,2048]{1,0:T(8,128)(2,1)}, bf16[256,2048]{1,0:T(8,128)(2,1)}, u32[]{:S(2)}, u32[]{:S(2)}) collective-permute-start(bf16[256,2048]{1,0:T(8,128)(2,1)} %get-tuple-element.205), channel_id=1, source_target_pairs={{1,0},{3,1},{2,3},{0,2},{5,4},{7,5},{6,7},{4,6},{9,8},{11,9},{10,1... | collective-permute-start | bytes 3145736 | tf_op jit(solution)/shard_map/ppermute | solution.py:472
  459.5 46.3 %collective-permute-start.45 = (bf16[512,2048]{1,0:T(8,128)(2,1)}, bf16[512,2048]{1,0:T(8,128)(2,1)}, u32[]{:S(2)}, u32[]{:S(2)}) collective-permute-start(bf16[512,2048]{1,0:T(8,128)(2,1)} %add_terms.11), channel_id=1, source_target_pairs={{0,8},{4,12},{8,0},{12,4},{16,24},{20,28},{24,16},{28,20},{1,9},{5... | collective-permute-start | bytes 6291464 | tf_op jit(solution)/shard_map/ppermute | solution.py:563
  532.3 45.4 %collective-permute-start.55 = (bf16[256,2048]{1,0:T(8,128)(2,1)S(1)}, bf16[256,2048]{1,0:T(8,128)(2,1)S(1)}, u32[]{:S(2)}, u32[]{:S(2)}) collective-permute-start(bf16[256,2048]{1,0:T(8,128)(2,1)S(1)} %add_terms.12), channel_id=1, source_target_pairs={{0,16},{4,20},{8,24},{12,28},{16,0},{20,4},{24,8},{28,12},{1,17},{... | collective-permute-start | bytes 3145736 | tf_op jit(solution)/shard_map/ppermute | solution.py:563
  536.0 32.6 %collective-permute-start.51 = (bf16[576,256]{1,0:T(8,128)(2,1)S(1)}, bf16[576,256]{1,0:T(8,128)(2,1)S(1)}, u32[]{:S(2)}, u32[]{:S(2)}) collective-permute-start(bf16[576,256]{1,0:T(8,128)(2,1)S(1)} %bitcast.267), channel_id=1, source_target_pairs={{1,0},{3,1},{2,3},{0,2},{5,4},{7,5},{6,7},{4,6},{9,8},{11,9},{10,1... | collective-permute-start | bytes 884744 | tf_op jit(solution)/shard_map/ppermute | solution.py:472
  574.4 25.3 %collective-permute-start.68 = (bf16[128,2048]{1,0:T(8,128)(2,1)S(1)}, bf16[128,2048]{1,0:T(8,128)(2,1)S(1)}, u32[]{:S(2)}, u32[]{:S(2)}) collective-permute-start(bf16[128,2048]{1,0:T(8,128)(2,1)S(1)} %add_terms.14), channel_id=1, source_target_pairs={{0,8},{4,12},{8,0},{12,4},{16,24},{20,28},{24,16},{28,20},{1,9},{5... | collective-permute-start | bytes 1572872 | tf_op jit(solution)/shard_map/ppermute | solution.py:563
  577.8 24.4 %collective-permute-start.60 = (bf16[144,2048]{1,0:T(8,128)(2,1)S(1)}, bf16[144,2048]{1,0:T(8,128)(2,1)S(1)}, u32[]{:S(2)}, u32[]{:S(2)}) collective-permute-start(bf16[144,2048]{1,0:T(8,128)(2,1)S(1)} %add_convert_fusion.2), channel_id=1, source_target_pairs={{0,8},{4,12},{8,0},{12,4},{16,24},{20,28},{24,16},{28,20},{1,9},{5... | collective-permute-start | bytes 1769480 | tf_op jit(solution)/shard_map/ppermute | solution.py:563
  589.9 37.2 %collective-permute-start.62 = (f32[22656]{0:T(1024)S(1)}, f32[22656]{0:T(1024)S(1)}, u32[]{:S(2)}, u32[]{:S(2)}) collective-permute-start(f32[22656]{0:T(1024)S(1)} %add.433), channel_id=1, source_target_pairs={{0,8},{4,12},{8,0},{12,4},{16,24},{20,28},{24,16},{28,20},{1,9},{5... | collective-permute-start | bytes 271880 | tf_op jit(solution)/shard_map/ppermute | solution.py:609
  (186 other events, 2098.4 us)
Sparse Core Ops, SparseCore 0:
  10.9 126.9 all-gather.2
  279.6 62.7 all-gather.4

commit v3 on v2

--- a/solution.py
+++ b/solution.py
@@ -52,7 +52,8 @@
     return pl.CostEstimate(flops=flops, bytes_accessed=moved, transcendentals=0)
 
 
-def call(kernel, name, out_shape, scratch, inputs, flops=0):
+def call(kernel, name, out_shape, scratch, inputs, flops=None):
+    estimate = cost(flops or 0, () if flops == 0 else (inputs, out_shape))
     return pl.pallas_call(
         kernel,
         name=name,
@@ -60,7 +61,7 @@
         in_specs=[ANY] * len(inputs),
         out_specs=jax.tree.map(lambda _: ANY, out_shape),
         scratch_shapes=scratch,
-        cost_estimate=cost(flops, (inputs, out_shape)),
+        cost_estimate=estimate,
         compiler_params=pltpu.CompilerParams(vmem_limit_bytes=44 * 1024 * 1024),
     )(*inputs)
 
@@ -295,7 +296,7 @@
     return grad, sums.reshape(units)
 
 
-def hidden_sum(lefts, slots, tok, order, cuts):
+def hidden_sum(lefts, slots, tok, order, cuts, flops):
     rows = lefts[0].shape[0]
     half = lefts[0].shape[1]
     width = slots[0].shape[1]
@@ -378,7 +379,7 @@
             pltpu.SemaphoreType.DMA((3, cuts)),
         ],
         (*lefts, *slots),
-        2 * rows * depth * width,
+        flops,
     )
 
 
@@ -794,6 +795,7 @@
         tok,
         links.sum_order,
         links.sum_cuts,
+        4 * seq_n * tok * split * width,
     )
     hidden_far = links.sum_far(after(hidden_parts, proj_first) if z_n == 4 else hidden_parts)
     proj_term = links.second_term(proj_own, proj_came, proj_first, units, hidden_parts)
@@ -805,7 +807,7 @@
     fc_term = links.first_term(fc_own, fc_came, units)
     fc_first = links.first_move(fc_term)
     mlp_parts = hidden_sum(
-        (after(act_mine, fc_term), act_other), [proj_mine, proj_other], tok, tuple(range(1, seq_n)), 1
+        (after(act_mine, fc_term), act_other), [proj_mine, proj_other], tok, tuple(range(1, seq_n)), 1, 0
     )
     mlp_came = [links.from_rel(mlp_parts[r], seq_n - r) for r in range(1, seq_n)]
 
@@ -871,7 +873,7 @@
     )
     came = links.exchange(after(parts, mlp_came))
     fc_second = links.second_move(links.second_term(fc_own, fc_came, fc_first, units, parts))
-    out_columns = to_owners(grad_middle_turned, came)
+    out_columns = to_owners(grad_middle_turned, mlp_came)
     out_sent, out_kept = ordered_parts(after(out_columns, parts), attns)
     out_came = links.swap_core(out_sent)
 
@@ -904,16 +906,18 @@
     fc_bias_sum = jnp.sum(jnp.where(owner[:, :, None], fc_bias_sum.reshape(dp_n, 1, units), 0.0), 0)
     fc_bias_sum = jnp.where(own_seq[None, :, None], fc_bias_sum[:, None, :], 0.0).reshape(-1)
     sums = jnp.concatenate(early + late + [query_sum, fc_bias_sum, value_sum])
+    qkv_sent, qkv_kept = ordered_parts(after(qkv_columns, tokens_grad), ones)
+    qkv_came = links.swap_core(qkv_sent)
+    qkv_own, qkv_came = ordered_terms(qkv_kept, qkv_came)
+    out_second = links.second_move(links.second_term(out_own, out_came, out_first, out_rows))
+    qkv_term = links.first_term(qkv_own, qkv_came, qkv_rows)
+    qkv_first = links.first_move(qkv_term, fc_second)
+    sums = after(sums, qkv_term)
     bit = 1
     while bit < seq_n:
         sums = sums + links.other_seq(sums, bit)
         bit *= 2
     sums = sums + links.other_dp(sums, 1)
-    qkv_sent, qkv_kept = ordered_parts(after(qkv_columns, tokens_grad), ones)
-    qkv_came = links.swap_core(qkv_sent)
-    qkv_own, qkv_came = ordered_terms(qkv_kept, qkv_came)
-    out_second = links.second_move(links.second_term(out_own, out_came, out_first, out_rows))
-    qkv_first = links.first_move(links.first_term(qkv_own, qkv_came, qkv_rows), fc_second)
     bit = 2
     moved = links.other_dp(sums, bit)
     qkv_second = links.second_move(links.second_term(qkv_own, qkv_came, qkv_first, qkv_rows))
@@ -922,8 +926,8 @@
     while bit < dp_n:
         sums = sums + links.other_dp(sums, bit)
         bit *= 2
-    proj_grad = links.chip_sum_end(proj_own, proj_came, proj_first, proj_second, units, qkv_own)
-    fc_grad = links.chip_sum_end(fc_own, fc_came, fc_first, fc_second, units, qkv_own)
+    proj_grad = links.chip_sum_end(proj_own, proj_came, proj_first, proj_second, units, qkv_first)
+    fc_grad = links.chip_sum_end(fc_own, fc_came, fc_first, fc_second, units, qkv_first)
     out_grad = links.chip_sum_end(out_own, out_came, out_first, out_second, out_rows)
     mlp = sum(member.astype(F32) for member in [mlp_parts[0], *after(mlp_came, fc_grad)])
     block_out = (middle + mlp + proj_shift).astype(BF).reshape(tokens.shape)

time: 651 us -> 631 us (0.969)
  waiting for transfers between devices: 238 us -> 226 us
    ppermute x40, waiting for transfers between devices: 82.3 us -> 109 us  [from_rel(): return lax.ppermute(value, 'seq', pairs)]
    ppermute x8, waiting for transfers between devices: 63.6 us -> 42.6 us  [other_chip(): return lax.ppermute(value, 'dp', pairs)]
    ppermute x9, waiting for transfers between devices: 75 us -> 64.6 us  [z_next(): lax.ppermute(value, 'dp', [(2 * i + c, 2 * j + c) for i, j in pairs for c...]
    unnamed x314 -> x332, local copies, waits for them, and re-layouts: 39.2 us -> 43 us
where the time goes in v3:
time: 631 us; the launch traced here: 623 us
  waiting for transfers between devices  226 us (36%)
  Pallas kernels  138 us (22%)
  starting transfers between devices  79.1 us (13%)
  local copies, waits for them, and re-layouts  64.6 us (10%)
  matrix products  61.3 us (10%)
  other arithmetic  36.3 us (6%)
  between operations  17.1 us (3%)
    pallas_call x12, Pallas kernels, call(): pl.pallas_call(kernel, name=name, out_shape=out_shape, in_specs=[ANY] * l...  114 us
    ppermute x40, waiting for transfers between devices, from_rel(): return lax.ppermute(value, 'seq', pairs)  109 us
    ppermute x9, waiting for transfers between devices, z_next(): lax.ppermute(value, 'dp', [(2 * i + c, 2 * j + c) for i, j in pairs for c...  64.6 us
    ppermute x40, starting transfers between devices, from_rel(): return lax.ppermute(value, 'seq', pairs)  44.9 us
    unnamed x332, local copies, waits for them, and re-layouts  43 us
    ppermute x8, waiting for transfers between devices, other_chip(): return lax.ppermute(value, 'dp', pairs)  42.6 us
    pallas_call x9, Pallas kernels, add_terms(): pl.pallas_call(kernel, name='add_terms', grid=(rows // step,), out_shape=...  24.5 us
    ppermute x9, starting transfers between devices, z_next(): lax.ppermute(value, 'dp', [(2 * i + c, 2 * j + c) for i, j in pairs for c...  20.1 us
  transfers between devices with their start and end apart: 72, of which 40 were waited for; matrix products, arithmetic and copies ran while one was open for 21% of the time, Pallas kernels for 19%

profile of v3, /device:TPU:0, one launch (start us, length us, event | category | flops | bytes accessed | tf_op | source)
XLA Modules:
  0.0 623.3 jit_solution(10323156442615486471)
XLA Ops:
  23.9 8.8 %collective-permute-done.1 = bf16[72,2048]{1,0:T(8,128)(2,1)} collective-permute-done((bf16[72,2048]{1,0:T(8,128)(2,1)S(1)}, bf16[72,2048]{1,0:T(8,128)(2,1)}, u32[]{:S(2)}, u32[]{:S(2)}) %collective-permute-start.1) | collective-permute-done | bytes 294944 | tf_op jit(solution)/shard_map/ppermute | solution.py:481
  36.3 5.8 collective-permute-done.2
  75.6 13.5 %collective-permute-done.9 = bf16[576,256]{1,0:T(8,128)(2,1)S(1)} collective-permute-done((bf16[576,256]{1,0:T(8,128)(2,1)}, bf16[576,256]{1,0:T(8,128)(2,1)S(1)}, u32[]{:S(2)}, u32[]{:S(2)}) %collective-permute-start.9) | collective-permute-done | bytes 294944 | tf_op jit(solution)/shard_map/ppermute | solution.py:473
  89.2 10.4 %collective-permute-done.10 = bf16[576,256]{1,0:T(8,128)(2,1)S(1)} collective-permute-done((bf16[576,256]{1,0:T(8,128)(2,1)}, bf16[576,256]{1,0:T(8,128)(2,1)S(1)}, u32[]{:S(2)}, u32[]{:S(2)}) %collective-permute-start.10) | collective-permute-done | bytes 294944 | tf_op jit(solution)/shard_map/ppermute | solution.py:473
  122.5 5.0 bitcast_convert_fusion.3
  127.5 7.6 %collective-permute-done.21.refs_7_.refs_2_.refs_4_ = bf16[256,2048]{1,0:T(8,128)(2,1)} collective-permute-done((bf16[256,2048]{1,0:T(8,128)(2,1)S(1)}, bf16[256,2048]{1,0:T(8,128)(2,1)}, u32[]{:S(2)}, u32[]{:S(2)}) %collective-permute-start.21) | collective-permute-done | bytes 1048608 | tf_op jit(solution)/shard_map/ppermute | solution.py:481
  136.1 6.3 %fusion.110 = (f32[256]{0:T(256)S(1)}, f32[256,2048]{1,0:T(8,128)S(1)}) fusion(f32[2048]{0:T(1024)S(1)} %copy-done.142, bf16[2048,256]{1,0:T(8,128)(2,1)} %bitcast.24, bf16[2048,2048]{1,0:T(8,128)(2,1)} %all-gather.3.cloned.1.call-done, bf16[1,256,2048]{2,1,0:T(8,128)(2,1)S(1)} %copy-done.66), kind=kOutput, calls=%fused_computation.259 | convolution fusion | flops 2149580544 | bytes 12592128 | tf_op jit(solution)/shard_map/dot_general | solution.py:17
  145.8 10.8 %collective-permute-done.23.refs_8_.refs_3_.refs_5_ = bf16[256,2048]{1,0:T(8,128)(2,1)} collective-permute-done((bf16[256,2048]{1,0:T(8,128)(2,1)}, bf16[256,2048]{1,0:T(8,128)(2,1)}, u32[]{:S(2)}, u32[]{:S(2)}) %collective-permute-start.23) | collective-permute-done | bytes 1048608 | tf_op jit(solution)/shard_map/ppermute | solution.py:481
  156.6 6.6 %collective-permute-done.16.refs_1_.refs_2_ = bf16[256,2048]{1,0:T(8,128)(2,1)S(1)} collective-permute-done((bf16[256,2048]{1,0:T(8,128)(2,1)S(1)}, bf16[256,2048]{1,0:T(8,128)(2,1)S(1)}, u32[]{:S(2)}, u32[]{:S(2)}) %collective-permute-start.16) | collective-permute-done | bytes 1048608 | tf_op jit(solution)/shard_map/ppermute | solution.py:473
  172.4 21.1 %collective-permute-done.22.refs_6_.refs_1_ = bf16[256,2048]{1,0:T(8,128)(2,1)} collective-permute-done((bf16[256,2048]{1,0:T(8,128)(2,1)S(1)}, bf16[256,2048]{1,0:T(8,128)(2,1)}, u32[]{:S(2)}, u32[]{:S(2)}) %collective-permute-start.22) | collective-permute-done | bytes 1048608 | tf_op jit(solution)/shard_map/ppermute | solution.py:481
  199.8 10.4 %hidden_forward.3 = (f32[1024,1024]{1,0:T(8,128)}, bf16[1024,1024]{1,0:T(8,128)(2,1)S(1)}) custom-call(bf16[256,2048]{1,0:T(8,128)(2,1)S(1)} %add_convert_fusion.1.refs_0_.refs_1_, bf16[256,2048]{1,0:T(8,128)(2,1)S(1)} %copy-done.36, bf16[128,2048]{1,0:T(8,128)(2,1)} %collective-permute-done.17.refs_2_.refs_3_, ...), custom_call_target="tpu_custom_call" | custom-call | flops 4294967296 | bytes 14684160 | tf_op jit(solution)/shard_map/hidden_forward/pallas_call | solution.py:57
  210.2 9.1 %collective-permute-done.27.refs_7_.refs_2_ = bf16[256,2048]{1,0:T(8,128)(2,1)S(1)} collective-permute-done((bf16[256,2048]{1,0:T(8,128)(2,1)}, bf16[256,2048]{1,0:T(8,128)(2,1)S(1)}, u32[]{:S(2)}, u32[]{:S(2)}) %collective-permute-start.27) | collective-permute-done | bytes 1048608 | tf_op jit(solution)/shard_map/ppermute | solution.py:481
  219.3 9.7 %weight_terms.4 = bf16[1024,2048]{1,0:T(8,128)(2,1)} custom-call(bf16[1024,1024]{1,0:T(8,128)(2,1)S(1)} %get-tuple-element.167.refs_0_.refs_1_, bf16[256,2048]{1,0:T(8,128)(2,1)S(1)} %bitcast.235, bf16[256,2048]{1,0:T(8,128)(2,1)} %collective-permute-done.14.refs_2_.refs_1_, bf16[128,2048]{1,0:T(8,128)(2,1)S(1)} %collective-permute-done.24.refs_3_.refs_2_, ...), custom_call_target="tpu_custom_call" | custom-call | flops 4294967296 | bytes 10485760 | tf_op jit(solution)/shard_map/weight_terms/pallas_call | solution.py:57
  232.8 9.8 %hidden_forward.2 = (f32[1024,1024]{1,0:T(8,128)}, bf16[1024,1024]{1,0:T(8,128)(2,1)}) custom-call(bf16[256,2048]{1,0:T(8,128)(2,1)S(1)} %add_convert_fusion.1.refs_0_.refs_1_, bf16[256,2048]{1,0:T(8,128)(2,1)S(1)} %copy-done.36, bf16[128,2048]{1,0:T(8,128)(2,1)} %collective-permute-done.17.refs_2_.refs_3_, ...), custom_call_target="tpu_custom_call" | custom-call | flops 4294967296 | bytes 14684160 | tf_op jit(solution)/shard_map/hidden_forward/pallas_call | solution.py:57
  244.3 8.9 %weight_terms.5.refs_0_ = bf16[1024,2048]{1,0:T(8,128)(2,1)} custom-call(bf16[1024,1024]{1,0:T(8,128)(2,1)S(1)} %copy-done.13, bf16[256,2048]{1,0:T(8,128)(2,1)S(1)} %bitcast.236, bf16[256,2048]{1,0:T(8,128)(2,1)} %collective-permute-done.14.refs_2_.refs_1_, bf16[128,2048]{1,0:T(8,128)(2,1)S(1)} %collective-permute-done.24.refs_3_.refs_2_, ...), custom_call_target="tpu_custom_call" | custom-call | flops 4294967296 | bytes 10485760 | tf_op jit(solution)/shard_map/weight_terms/pallas_call | solution.py:57
  281.3 10.6 %hidden_backward.2 = (bf16[1024,1024]{1,0:T(8,128)(2,1)}, f32[1,1024]{1,0:T(1,128)S(1)}) custom-call(bf16[256,2048]{1,0:T(8,128)(2,1)S(1)} %bitcast.237, bf16[256,2048]{1,0:T(8,128)(2,1)} %collective-permute-done.14.refs_2_.refs_1_, bf16[128,2048]{1,0:T(8,128)(2,1)S(1)} %copy-done.52, bf16[128,2048]{1,0:T(8,128)(2,1)S(1)} %copy-done.54, ...), custom_call_target="tpu_custom_call" | custom-call | flops 4294967296 | bytes 14684160 | tf_op jit(solution)/shard_map/hidden_backward/pallas_call | solution.py:57
  292.0 6.3 %collective-permute-done.33 = bf16[128,2048]{0,1:T(8,128)(2,1)S(1)} collective-permute-done((bf16[128,2048]{0,1:T(8,128)(2,1)S(1)}, bf16[128,2048]{0,1:T(8,128)(2,1)S(1)}, u32[]{:S(2)}, u32[]{:S(2)}) %collective-permute-start.33) | collective-permute-done | bytes 524320 | tf_op jit(solution)/shard_map/ppermute | solution.py:473
  302.7 11.0 %hidden_backward.3 = (bf16[1024,1024]{1,0:T(8,128)(2,1)S(1)}, f32[1,1024]{1,0:T(1,128)S(1)}) custom-call(bf16[256,2048]{1,0:T(8,128)(2,1)S(1)} %bitcast.238, bf16[256,2048]{1,0:T(8,128)(2,1)} %collective-permute-done.14.refs_2_.refs_1_, bf16[128,2048]{1,0:T(8,128)(2,1)S(1)} %copy-done.52, bf16[128,2048]{1,0:T(8,128)(2,1)S(1)} %copy-done.55, ...), custom_call_target="tpu_custom_call" | custom-call | flops 4294967296 | bytes 14684160 | tf_op jit(solution)/shard_map/hidden_backward/pallas_call | solution.py:57
  315.0 14.7 %hidden_sum.2 = (f32[256,2048]{1,0:T(8,128)S(1)}, bf16[128,2048]{1,0:T(8,128)(2,1)S(1)}, bf16[128,2048]{1,0:T(8,128)(2,1)S(1)}, bf16[128,2048]{1,0:T(8,128)(2,1)...) custom-call(bf16[1024,1024]{1,0:T(8,128)(2,1)} %get-tuple-element.201.refs_0_, ...), custom_call_target="tpu_custom_call" | custom-call | flops 8589934592 | bytes 17825792 | tf_op jit(solution)/shard_map/hidden_sum/pallas_call | solution.py:57
  343.5 7.0 %collective-permute-done.36 = bf16[128,2048]{1,0:T(8,128)(2,1)S(1)} collective-permute-done((bf16[128,2048]{1,0:T(8,128)(2,1)S(1)}, bf16[128,2048]{1,0:T(8,128)(2,1)S(1)}, u32[]{:S(2)}, u32[]{:S(2)}) %collective-permute-start.36) | collective-permute-done | bytes 524320 | tf_op jit(solution)/shard_map/ppermute | solution.py:473
  351.3 6.5 %collective-permute-done.38 = bf16[128,2048]{1,0:T(8,128)(2,1)S(1)} collective-permute-done((bf16[128,2048]{1,0:T(8,128)(2,1)S(1)}, bf16[128,2048]{1,0:T(8,128)(2,1)S(1)}, u32[]{:S(2)}, u32[]{:S(2)}) %collective-permute-start.38) | collective-permute-done | bytes 524320 | tf_op jit(solution)/shard_map/ppermute | solution.py:473
  359.4 19.6 %collective-permute-done.40.refs_3_ = bf16[256,2048]{1,0:T(8,128)(2,1)} collective-permute-done((bf16[256,2048]{1,0:T(8,128)(2,1)}, bf16[256,2048]{1,0:T(8,128)(2,1)}, u32[]{:S(2)}, u32[]{:S(2)}) %collective-permute-start.40) | collective-permute-done | bytes 1048608 | tf_op jit(solution)/shard_map/ppermute | solution.py:564
  380.7 8.6 %weight_terms.6 = bf16[1024,2048]{1,0:T(8,128)(2,1)} custom-call(bf16[1024,1024]{1,0:T(8,128)(2,1)S(1)} %copy-done.58, bf16[256,2048]{1,0:T(8,128)(2,1)S(1)} %copy-done.17, bf16[256,2048]{1,0:T(8,128)(2,1)S(1)} %copy-done.37, bf16[128,2048]{1,0:T(8,128)(2,1)} %collective-permute-done.17.refs_2_.refs_3_, ...), custom_call_target="tpu_custom_call" | custom-call | flops 4294967296 | bytes 10485760 | tf_op jit(solution)/shard_map/weight_terms/pallas_call | solution.py:57
  407.9 8.7 %weight_terms.7.refs_0_ = bf16[1024,2048]{1,0:T(8,128)(2,1)} custom-call(bf16[1024,1024]{1,0:T(8,128)(2,1)S(1)} %copy-done.56, bf16[256,2048]{1,0:T(8,128)(2,1)S(1)} %copy-done.18, bf16[256,2048]{1,0:T(8,128)(2,1)S(1)} %copy-done.38, bf16[128,2048]{1,0:T(8,128)(2,1)} %collective-permute-done.17.refs_2_.refs_3_, ...), custom_call_target="tpu_custom_call" | custom-call | flops 4294967296 | bytes 10485760 | tf_op jit(solution)/shard_map/weight_terms/pallas_call | solution.py:57
  427.8 14.0 %hidden_sum.3 = (f32[256,2048]{1,0:T(8,128)S(1)}, bf16[256,2048]{1,0:T(8,128)(2,1)}, bf16[256,2048]{1,0:T(8,128)(2,1)}, bf16[256,2048]{1,0:T(8,128)(2,1)}) custom-call(bf16[1024,1024]{1,0:T(8,128)(2,1)S(1)} %copy-done.14, bf16[1024,1024]{1,0:T(8,128)(2,1)S(1)} %copy-done.12, bf16[1024,2048]{1,0:T(8,128)(2,1)} %join_rows.3.refs_2_, ...), custom_call_target="tpu_custom_call" | custom-call | tf_op jit(solution)/shard_map/hidden_sum/pallas_call | solution.py:57
  452.6 6.7 %fusion.21 = bf16[2048,256]{0,1:T(8,128)(2,1)} fusion(bf16[256,2048]{1,0:T(8,128)(2,1)S(1)} %convert_element_type.374, bf16[2048,2048]{1,0:T(8,128)(2,1)} %all-gather.3.cloned.1.call-done), kind=kOutput, calls=%fused_computation.29 | convolution fusion | flops 2148007936 | bytes 10485760 | tf_op jit(solution)/shard_map/dot_general | solution.py:854
  468.9 21.8 %collective-permute-done.43 = bf16[256,2048]{1,0:T(8,128)(2,1)} collective-permute-done((bf16[256,2048]{1,0:T(8,128)(2,1)}, bf16[256,2048]{1,0:T(8,128)(2,1)}, u32[]{:S(2)}, u32[]{:S(2)}) %collective-permute-start.43) | collective-permute-done | bytes 1048608 | tf_op jit(solution)/shard_map/ppermute | solution.py:473
  495.5 8.2 %fusion = bf16[16,1024,256]{1,2,0:T(8,128)(2,1)S(1)} fusion(f32[16,1024,256]{1,2,0:T(8,128)} %copy-done.68, bf16[16,128,256]{2,1,0:T(8,128)(2,1)S(1)} %bitcast.249, f32[16,256]{1,0:T(8,128)S(1)} %fusion.31, f32[16,256]{1,0:T(8,128)S(1)} %bitcast.271, pred[1024,256]{0,1:T(8,128)(4,1)S(1)} %copy-done.92, bf16[128,256]{1,0:T(8,128)(2,1)S(1)} %copy-done.128, ...), kind=kOutput, calls=%fused_computation.1 | convolution fusion | flops 1095761920 | bytes 26771456 | tf_op jit(solution)/shard_map/dk,hdq->hkq/dot_general | solution.py:861
  505.0 7.6 %fusion.32 = f32[128,1024]{1,0:T(8,128)S(1)} fusion(bf16[16,128,256]{2,1,0:T(8,128)(2,1)S(1)} %bitcast.250, f32[16,1024,256]{1,2,0:T(8,128)} %copy-done.68, f32[16,256]{1,0:T(8,128)S(1)} %bitcast.272, pred[1024,256]{0,1:T(8,128)(4,1)S(1)} %copy-done.92), kind=kOutput, calls=%fused_computation.65 | convolution fusion | flops 1086324736 | bytes 18628608 | tf_op jit(solution)/shard_map/hkq,hdq->dk/dot_general | solution.py:865
  547.1 5.5 collective-permute-done.53
  562.1 9.5 %collective-permute-done.68.refs_2_ = bf16[128,2048]{1,0:T(8,128)(2,1)S(1)} collective-permute-done((bf16[128,2048]{1,0:T(8,128)(2,1)S(1)}, bf16[128,2048]{1,0:T(8,128)(2,1)S(1)}, u32[]{:S(2)}, u32[]{:S(2)}) %collective-permute-start.68) | collective-permute-done | bytes 524320 | tf_op jit(solution)/shard_map/ppermute | solution.py:564
  579.1 8.4 %collective-permute-done.69.refs_3_ = bf16[64,2048]{1,0:T(8,128)(2,1)S(1)} collective-permute-done((bf16[64,2048]{1,0:T(8,128)(2,1)S(1)}, bf16[64,2048]{1,0:T(8,128)(2,1)S(1)}, u32[]{:S(2)}, u32[]{:S(2)}) %collective-permute-start.69) | collective-permute-done | bytes 262176 | tf_op jit(solution)/shard_map/ppermute | solution.py:564
  (607 shorter events, 287.5 us)
Async XLA Ops:
  7.2 128.9 %all-gather.3.cloned.1.call-start = ((), (), s32[]{:S(2)}) async-start(), calls=%async_computation | async-start | bytes 8650752 | tf_op jit(solution)/shard_map/all_gather | solution.py:679
  7.9 390.6 %all-gather.5.cloned.1.call-start = ((), (), s32[]{:S(2)}) async-start(), calls=%async_computation.1 | async-start | bytes 5898240 | tf_op jit(solution)/shard_map/all_gather | solution.py:763
  18.6 26.0 %collective-permute-start.3 = (bf16[256,2048]{1,0:T(8,128)(2,1)S(1)}, bf16[256,2048]{1,0:T(8,128)(2,1)}, u32[]{:S(2)}, u32[]{:S(2)}) collective-permute-start(bf16[256,2048]{1,0:T(8,128)(2,1)S(1)} %fusion.23), channel_id=1, source_target_pairs={{1,0},{3,1},{2,3},{0,2},{5,4},{7,5},{6,7},{4,6},{9,8},{11,9},{10,1... | collective-permute-start | bytes 3145736 | tf_op jit(solution)/shard_map/ppermute | solution.py:473
  20.2 25.6 %collective-permute-start.4 = (bf16[256,2048]{1,0:T(8,128)(2,1)S(1)}, bf16[256,2048]{1,0:T(8,128)(2,1)S(1)}, u32[]{:S(2)}, u32[]{:S(2)}) collective-permute-start(bf16[256,2048]{1,0:T(8,128)(2,1)S(1)} %fusion.23), channel_id=1, source_target_pairs={{2,0},{0,1},{1,3},{3,2},{6,4},{4,5},{5,7},{7,6},{10,8},{8,9},{9,11... | collective-permute-start | bytes 3145736 | tf_op jit(solution)/shard_map/ppermute | solution.py:473
  49.6 62.2 %collective-permute-start.20 = (bf16[256,2048]{1,0:T(8,128)(2,1)S(1)}, bf16[256,2048]{1,0:T(8,128)(2,1)S(1)}, u32[]{:S(2)}, u32[]{:S(2)}) collective-permute-start(bf16[256,2048]{1,0:T(8,128)(2,1)S(1)} %copy-done.21), channel_id=1, source_target_pairs={{8,0},{12,4},{0,16},{4,20},{16,24},{20,28},{24,8},{28,12},{9,1},{1... | collective-permute-start | bytes 3145736 | tf_op jit(solution)/shard_map/ppermute | solution.py:481
  72.4 27.2 %collective-permute-start.10 = (bf16[576,256]{1,0:T(8,128)(2,1)}, bf16[576,256]{1,0:T(8,128)(2,1)S(1)}, u32[]{:S(2)}, u32[]{:S(2)}) collective-permute-start(bf16[576,256]{1,0:T(8,128)(2,1)} %fusion.38), channel_id=1, source_target_pairs={{1,0},{3,1},{2,3},{0,2},{5,4},{7,5},{6,7},{4,6},{9,8},{11,9},{10,1... | collective-permute-start | bytes 884744 | tf_op jit(solution)/shard_map/ppermute | solution.py:473
  73.9 25.7 %collective-permute-start.6 = (bf16[576,256]{1,0:T(8,128)(2,1)}, bf16[576,256]{1,0:T(8,128)(2,1)S(1)}, u32[]{:S(2)}, u32[]{:S(2)}) collective-permute-start(bf16[576,256]{1,0:T(8,128)(2,1)} %fusion.37), channel_id=1, source_target_pairs={{2,0},{0,1},{1,3},{3,2},{6,4},{4,5},{5,7},{7,6},{10,8},{8,9},{9,11... | collective-permute-start | bytes 884744 | tf_op jit(solution)/shard_map/ppermute | solution.py:473
  109.8 33.9 %collective-permute-start.14 = (bf16[256,2048]{1,0:T(8,128)(2,1)S(1)}, bf16[256,2048]{1,0:T(8,128)(2,1)}, u32[]{:S(2)}, u32[]{:S(2)}) collective-permute-start(bf16[256,2048]{1,0:T(8,128)(2,1)S(1)} %bitcast.233), channel_id=1, source_target_pairs={{1,0},{3,1},{2,3},{0,2},{5,4},{7,5},{6,7},{4,6},{9,8},{11,9},{10,1... | collective-permute-start | bytes 3145736 | tf_op jit(solution)/shard_map/ppermute | solution.py:473
  111.1 32.6 %collective-permute-start.15 = (bf16[256,2048]{1,0:T(8,128)(2,1)S(1)}, bf16[256,2048]{1,0:T(8,128)(2,1)}, u32[]{:S(2)}, u32[]{:S(2)}) collective-permute-start(bf16[256,2048]{1,0:T(8,128)(2,1)S(1)} %bitcast.234), channel_id=1, source_target_pairs={{2,0},{0,1},{1,3},{3,2},{6,4},{4,5},{5,7},{7,6},{10,8},{8,9},{9,11... | collective-permute-start | bytes 3145736 | tf_op jit(solution)/shard_map/ppermute | solution.py:473
  167.7 32.1 %collective-permute-start.26 = (bf16[1024,2048]{1,0:T(8,128)(2,1)}, bf16[1024,2048]{1,0:T(8,128)(2,1)}, u32[]{:S(2)}, u32[]{:S(2)}) collective-permute-start(bf16[1024,2048]{1,0:T(8,128)(2,1)} %join_rows.2), channel_id=1, source_target_pairs={{0,4},{4,0},{8,12},{12,8},{16,20},{20,16},{24,28},{28,24},{1,5},{5... | collective-permute-start | bytes 12582920 | tf_op jit(solution)/shard_map/ppermute | solution.py:477
  167.8 25.7 %collective-permute-start.22 = (bf16[256,2048]{1,0:T(8,128)(2,1)S(1)}, bf16[256,2048]{1,0:T(8,128)(2,1)}, u32[]{:S(2)}, u32[]{:S(2)}) collective-permute-start(bf16[256,2048]{1,0:T(8,128)(2,1)S(1)} %copy-done.19), channel_id=1, source_target_pairs={{8,0},{12,4},{0,16},{4,20},{16,24},{20,28},{24,8},{28,12},{9,1},{1... | collective-permute-start | bytes 3145736 | tf_op jit(solution)/shard_map/ppermute | solution.py:481
  169.4 24.1 %collective-permute-start.17 = (bf16[128,2048]{1,0:T(8,128)(2,1)}, bf16[128,2048]{1,0:T(8,128)(2,1)}, u32[]{:S(2)}, u32[]{:S(2)}) collective-permute-start(bf16[128,2048]{1,0:T(8,128)(2,1)} %slice.234), channel_id=1, source_target_pairs={{1,0},{3,1},{2,3},{0,2},{5,4},{7,5},{6,7},{4,6},{9,8},{11,9},{10,1... | collective-permute-start | bytes 1572872 | tf_op jit(solution)/shard_map/ppermute | solution.py:473
  193.5 25.8 %collective-permute-start.27 = (bf16[256,2048]{1,0:T(8,128)(2,1)}, bf16[256,2048]{1,0:T(8,128)(2,1)S(1)}, u32[]{:S(2)}, u32[]{:S(2)}) collective-permute-start(bf16[256,2048]{1,0:T(8,128)(2,1)} %collective-permute-done.22.refs_6_.refs_1_), channel_id=1, source_target_pairs={{8,0},{12,4},{0,16},{4,20},{16,24},{20,28},{24,8},{28,12},{9,1},{1... | collective-permute-start | bytes 3145736 | tf_op jit(solution)/shard_map/ppermute | solution.py:481
  229.0 27.9 %collective-permute-start.29 = (bf16[1024,2048]{1,0:T(8,128)(2,1)}, bf16[1024,2048]{1,0:T(8,128)(2,1)S(1)}, u32[]{:S(2)}, u32[]{:S(2)}) collective-permute-start(bf16[1024,2048]{1,0:T(8,128)(2,1)} %weight_terms.4), channel_id=1, source_target_pairs={{0,4},{4,0},{8,12},{12,8},{16,20},{20,16},{24,28},{28,24},{1,5},{5... | collective-permute-start | bytes 12582920 | tf_op jit(solution)/shard_map/ppermute | solution.py:477
  229.1 25.9 %collective-permute-start.30 = (bf16[256,2048]{0,1:T(8,128)(2,1)}, bf16[256,2048]{0,1:T(8,128)(2,1)}, u32[]{:S(2)}, u32[]{:S(2)}) collective-permute-start(bf16[256,2048]{0,1:T(8,128)(2,1)} %bitcast.26), channel_id=1, source_target_pairs={{1,0},{3,1},{2,3},{0,2},{5,4},{7,5},{6,7},{4,6},{9,8},{11,9},{10,1... | collective-permute-start | bytes 3145736 | tf_op jit(solution)/shard_map/ppermute | solution.py:473
  230.4 25.5 %collective-permute-start.31 = (bf16[256,2048]{0,1:T(8,128)(2,1)}, bf16[256,2048]{0,1:T(8,128)(2,1)S(1)}, u32[]{:S(2)}, u32[]{:S(2)}) collective-permute-start(bf16[256,2048]{0,1:T(8,128)(2,1)} %bitcast.26), channel_id=1, source_target_pairs={{2,0},{0,1},{1,3},{3,2},{6,4},{4,5},{5,7},{7,6},{10,8},{8,9},{9,11... | collective-permute-start | bytes 3145736 | tf_op jit(solution)/shard_map/ppermute | solution.py:473
  231.2 35.5 %collective-permute-start.28 = (bf16[256,2048]{1,0:T(8,128)(2,1)S(1)}, bf16[256,2048]{1,0:T(8,128)(2,1)S(1)}, u32[]{:S(2)}, u32[]{:S(2)}) collective-permute-start(bf16[256,2048]{1,0:T(8,128)(2,1)S(1)} %collective-permute-done.27.refs_7_.refs_2_), channel_id=1, source_target_pairs={{8,0},{12,4},{0,16},{4,20},{16,24},{20,28},{24,8},{28,12},{9,1},{1... | collective-permute-start | bytes 3145736 | tf_op jit(solution)/shard_map/ppermute | solution.py:481
  270.4 31.4 %collective-permute-start.32 = (bf16[1024,2048]{1,0:T(8,128)(2,1)}, bf16[1024,2048]{1,0:T(8,128)(2,1)}, u32[]{:S(2)}, u32[]{:S(2)}) collective-permute-start(bf16[1024,2048]{1,0:T(8,128)(2,1)} %join_rows.3.refs_2_), channel_id=1, source_target_pairs={{0,4},{4,0},{8,12},{12,8},{16,20},{20,16},{24,28},{28,24},{1,5},{5... | collective-permute-start | bytes 12582920 | tf_op jit(solution)/shard_map/ppermute | solution.py:477
  270.5 59.3 %collective-permute-start.35 = (bf16[512,2048]{1,0:T(8,128)(2,1)}, bf16[512,2048]{1,0:T(8,128)(2,1)S(1)}, u32[]{:S(2)}, u32[]{:S(2)}) collective-permute-start(bf16[512,2048]{1,0:T(8,128)(2,1)} %copy-done.10), channel_id=1, source_target_pairs={{0,8},{4,12},{8,0},{12,4},{16,24},{20,28},{24,16},{28,20},{1,9},{5... | collective-permute-start | bytes 6291464 | tf_op jit(solution)/shard_map/ppermute | solution.py:564
  277.1 24.7 %collective-permute-start.34 = (bf16[128,2048]{0,1:T(8,128)(2,1)S(1)}, bf16[128,2048]{0,1:T(8,128)(2,1)S(1)}, u32[]{:S(2)}, u32[]{:S(2)}) collective-permute-start(bf16[128,2048]{0,1:T(8,128)(2,1)S(1)} %slice.195), channel_id=1, source_target_pairs={{2,0},{0,1},{1,3},{3,2},{6,4},{4,5},{5,7},{7,6},{10,8},{8,9},{9,11... | collective-permute-start | bytes 1572872 | tf_op jit(solution)/shard_map/ppermute | solution.py:473
  333.9 45.2 %collective-permute-start.40 = (bf16[256,2048]{1,0:T(8,128)(2,1)}, bf16[256,2048]{1,0:T(8,128)(2,1)}, u32[]{:S(2)}, u32[]{:S(2)}) collective-permute-start(bf16[256,2048]{1,0:T(8,128)(2,1)} %add_terms.10), channel_id=1, source_target_pairs={{0,16},{4,20},{8,24},{12,28},{16,0},{20,4},{24,8},{28,12},{1,17},{... | collective-permute-start | bytes 3145736 | tf_op jit(solution)/shard_map/ppermute | solution.py:564
  389.3 31.6 %collective-permute-start.41 = (bf16[1024,2048]{1,0:T(8,128)(2,1)}, bf16[1024,2048]{1,0:T(8,128)(2,1)}, u32[]{:S(2)}, u32[]{:S(2)}) collective-permute-start(bf16[1024,2048]{1,0:T(8,128)(2,1)} %weight_terms.6), channel_id=1, source_target_pairs={{0,4},{4,0},{8,12},{12,8},{16,20},{20,16},{24,28},{28,24},{1,5},{5... | collective-permute-start | bytes 12582920 | tf_op jit(solution)/shard_map/ppermute | solution.py:477
  398.6 131.6 %collective-permute-start.54 = (bf16[1152,2048]{1,0:T(8,128)(2,1)}, bf16[1152,2048]{1,0:T(8,128)(2,1)}, u32[]{:S(2)}, u32[]{:S(2)}) collective-permute-start(bf16[1152,2048]{1,0:T(8,128)(2,1)} %bitcast.278), channel_id=1, source_target_pairs={{0,4},{4,0},{8,12},{12,8},{16,20},{20,16},{24,28},{28,24},{1,5},{5... | collective-permute-start | bytes 14155784 | tf_op jit(solution)/shard_map/ppermute | solution.py:477
  443.2 25.7 %collective-permute-start.42 = (bf16[256,2048]{1,0:T(8,128)(2,1)}, bf16[256,2048]{1,0:T(8,128)(2,1)}, u32[]{:S(2)}, u32[]{:S(2)}) collective-permute-start(bf16[256,2048]{1,0:T(8,128)(2,1)} %get-tuple-element.204), channel_id=1, source_target_pairs={{2,0},{0,1},{1,3},{3,2},{6,4},{4,5},{5,7},{7,6},{10,8},{8,9},{9,11... | collective-permute-start | bytes 3145736 | tf_op jit(solution)/shard_map/ppermute | solution.py:473
  444.9 45.8 %collective-permute-start.43 = (bf16[256,2048]{1,0:T(8,128)(2,1)}, bf16[256,2048]{1,0:T(8,128)(2,1)}, u32[]{:S(2)}, u32[]{:S(2)}) collective-permute-start(bf16[256,2048]{1,0:T(8,128)(2,1)} %get-tuple-element.205), channel_id=1, source_target_pairs={{3,0},{2,1},{0,3},{1,2},{7,4},{6,5},{4,7},{5,6},{11,8},{10,9},{8,1... | collective-permute-start | bytes 3145736 | tf_op jit(solution)/shard_map/ppermute | solution.py:473
  445.2 46.4 %collective-permute-start.44 = (bf16[256,2048]{1,0:T(8,128)(2,1)}, bf16[256,2048]{1,0:T(8,128)(2,1)}, u32[]{:S(2)}, u32[]{:S(2)}) collective-permute-start(bf16[256,2048]{1,0:T(8,128)(2,1)} %get-tuple-element.206), channel_id=1, source_target_pairs={{1,0},{3,1},{2,3},{0,2},{5,4},{7,5},{6,7},{4,6},{9,8},{11,9},{10,1... | collective-permute-start | bytes 3145736 | tf_op jit(solution)/shard_map/ppermute | solution.py:473
  447.4 48.0 %collective-permute-start.45 = (bf16[512,2048]{1,0:T(8,128)(2,1)}, bf16[512,2048]{1,0:T(8,128)(2,1)}, u32[]{:S(2)}, u32[]{:S(2)}) collective-permute-start(bf16[512,2048]{1,0:T(8,128)(2,1)} %copy-done.9), channel_id=1, source_target_pairs={{0,8},{4,12},{8,0},{12,4},{16,24},{20,28},{24,16},{28,20},{1,9},{5... | collective-permute-start | bytes 6291464 | tf_op jit(solution)/shard_map/ppermute | solution.py:564
  491.6 23.8 %collective-permute-start.64 = (bf16[512,256]{1,0:T(8,128)(2,1)}, bf16[512,256]{1,0:T(8,128)(2,1)}, u32[]{:S(2)}, u32[]{:S(2)}) collective-permute-start(bf16[512,256]{1,0:T(8,128)(2,1)} %bitcast.69), channel_id=1, source_target_pairs={{1,0},{3,1},{2,3},{0,2},{5,4},{7,5},{6,7},{4,6},{9,8},{11,9},{10,1... | collective-permute-start | bytes 786440 | tf_op jit(solution)/shard_map/ppermute | solution.py:473
  493.0 23.9 %collective-permute-start.65 = (bf16[512,256]{1,0:T(8,128)(2,1)}, bf16[512,256]{1,0:T(8,128)(2,1)}, u32[]{:S(2)}, u32[]{:S(2)}) collective-permute-start(bf16[512,256]{1,0:T(8,128)(2,1)} %bitcast.68), channel_id=1, source_target_pairs={{3,0},{2,1},{0,3},{1,2},{7,4},{6,5},{4,7},{5,6},{11,8},{10,9},{8,1... | collective-permute-start | bytes 786440 | tf_op jit(solution)/shard_map/ppermute | solution.py:473
  515.3 45.1 %collective-permute-start.56 = (bf16[256,2048]{1,0:T(8,128)(2,1)S(1)}, bf16[256,2048]{1,0:T(8,128)(2,1)S(1)}, u32[]{:S(2)}, u32[]{:S(2)}) collective-permute-start(bf16[256,2048]{1,0:T(8,128)(2,1)S(1)} %add_terms.12), channel_id=1, source_target_pairs={{0,16},{4,20},{8,24},{12,28},{16,0},{20,4},{24,8},{28,12},{1,17},{... | collective-permute-start | bytes 3145736 | tf_op jit(solution)/shard_map/ppermute | solution.py:564
  528.1 28.1 %collective-permute-start.67 = (bf16[4,64,2048]{2,1,0:T(8,128)(2,1)S(1)}, bf16[4,64,2048]{2,1,0:T(8,128)(2,1)S(1)}, u32[]{:S(2)}, u32[]{:S(2)}) collective-permute-start(bf16[4,64,2048]{2,1,0:T(8,128)(2,1)S(1)} %get-tuple-element.263), channel_id=1, source_target_pairs={{0,4},{4,0},{8,12},{12,8},{16,20},{20,16},{24,28},{28,24},{1,5},{5... | collective-permute-start | bytes 3145736 | tf_op jit(solution)/shard_map/ppermute | solution.py:477
  560.4 32.6 %collective-permute-start.57 = (bf16[144,2048]{1,0:T(8,128)(2,1)S(1)}, bf16[144,2048]{1,0:T(8,128)(2,1)S(1)}, u32[]{:S(2)}, u32[]{:S(2)}) collective-permute-start(bf16[144,2048]{1,0:T(8,128)(2,1)S(1)} %add_convert_fusion.2), channel_id=1, source_target_pairs={{0,8},{4,12},{8,0},{12,4},{16,24},{20,28},{24,16},{28,20},{1,9},{5... | collective-permute-start | bytes 1769480 | tf_op jit(solution)/shard_map/ppermute | solution.py:564
  (195 other events, 3004.8 us)
Sparse Core Ops, SparseCore 0:
  10.9 101.4 all-gather.2
  270.6 63.2 all-gather.4

commit v4 on v3

--- a/solution.py
+++ b/solution.py
@@ -868,12 +868,12 @@
         grad_query = grad_query.reshape(width, tok)
         return grad_query.astype(BF), jnp.sum(grad_query, 1), [parts[0]] + [part.astype(BF) for part in parts[1:]]
 
-    log_total = gate(log_total, fc_first, grad_middle_low)
+    grad_middle_low = gate(grad_middle_low, fc_first)
     grad_query, query_sum, parts = attend_back(out_full, grad_middle_low, query, pairs, attn, log_total
     )
     came = links.exchange(after(parts, mlp_came))
     fc_second = links.second_move(links.second_term(fc_own, fc_came, fc_first, units, parts))
-    out_columns = to_owners(grad_middle_turned, mlp_came)
+    out_columns = to_owners(grad_middle_turned, mlp_came[:1])
     out_sent, out_kept = ordered_parts(after(out_columns, parts), attns)
     out_came = links.swap_core(out_sent)
 

time: 631 us -> 623 us (0.987)
  waiting for transfers between devices: 226 us -> 215 us
    ppermute x40, waiting for transfers between devices: 109 us -> 93.1 us  [from_rel(): return lax.ppermute(value, 'seq', pairs)]
    unnamed x332 -> x305, local copies, waits for them, and re-layouts: 43 us -> 38.7 us
  transfers between devices with their start and end apart: 72 -> 72, of which waited for: 40 -> 41; matrix products, arithmetic and copies ran while one was open for 21% -> 22% of each run, Pallas kernels for 19% -> 20%
where the time goes in v4:
time: 623 us; the launch traced here: 615 us
  waiting for transfers between devices  215 us (35%)
  Pallas kernels  140 us (22%)
  starting transfers between devices  79.8 us (13%)
  local copies, waits for them, and re-layouts  61.9 us (10%)
  matrix products  61.2 us (10%)
  other arithmetic  40.8 us (7%)
  between operations  16.9 us (3%)
    pallas_call x12, Pallas kernels, call(): pl.pallas_call(kernel, name=name, out_shape=out_shape, in_specs=[ANY] * l...  114 us
    ppermute x40, waiting for transfers between devices, from_rel(): return lax.ppermute(value, 'seq', pairs)  93.1 us
    ppermute x9, waiting for transfers between devices, z_next(): lax.ppermute(value, 'dp', [(2 * i + c, 2 * j + c) for i, j in pairs for c...  65.3 us
    ppermute x40, starting transfers between devices, from_rel(): return lax.ppermute(value, 'seq', pairs)  50.2 us
    ppermute x8, waiting for transfers between devices, other_chip(): return lax.ppermute(value, 'dp', pairs)  46 us
    unnamed x305, local copies, waits for them, and re-layouts  38.7 us
    pallas_call x9, Pallas kernels, add_terms(): pl.pallas_call(kernel, name='add_terms', grid=(rows // step,), out_shape=...  25.9 us
    ppermute x9, starting transfers between devices, z_next(): lax.ppermute(value, 'dp', [(2 * i + c, 2 * j + c) for i, j in pairs for c...  19 us
  transfers between devices with their start and end apart: 72, of which 41 were waited for; matrix products, arithmetic and copies ran while one was open for 22% of the time, Pallas kernels for 20%

profile of v4, /device:TPU:0, one launch (start us, length us, event | category | flops | bytes accessed | tf_op | source)
XLA Modules:
  0.0 615.3 jit_solution(1270459412067594115)
XLA Ops:
  23.9 8.8 %collective-permute-done.1 = bf16[72,2048]{1,0:T(8,128)(2,1)} collective-permute-done((bf16[72,2048]{1,0:T(8,128)(2,1)S(1)}, bf16[72,2048]{1,0:T(8,128)(2,1)}, u32[]{:S(2)}, u32[]{:S(2)}) %collective-permute-start.1) | collective-permute-done | bytes 294944 | tf_op jit(solution)/shard_map/ppermute | solution.py:481
  36.3 5.8 collective-permute-done.2
  76.2 12.9 %collective-permute-done.9 = bf16[576,256]{1,0:T(8,128)(2,1)S(1)} collective-permute-done((bf16[576,256]{1,0:T(8,128)(2,1)}, bf16[576,256]{1,0:T(8,128)(2,1)S(1)}, u32[]{:S(2)}, u32[]{:S(2)}) %collective-permute-start.9) | collective-permute-done | bytes 294944 | tf_op jit(solution)/shard_map/ppermute | solution.py:473
  89.2 10.4 %collective-permute-done.10 = bf16[576,256]{1,0:T(8,128)(2,1)S(1)} collective-permute-done((bf16[576,256]{1,0:T(8,128)(2,1)}, bf16[576,256]{1,0:T(8,128)(2,1)S(1)}, u32[]{:S(2)}, u32[]{:S(2)}) %collective-permute-start.10) | collective-permute-done | bytes 294944 | tf_op jit(solution)/shard_map/ppermute | solution.py:473
  129.5 7.6 %collective-permute-done.21.refs_7_.refs_2_.refs_4_ = bf16[256,2048]{1,0:T(8,128)(2,1)} collective-permute-done((bf16[256,2048]{1,0:T(8,128)(2,1)S(1)}, bf16[256,2048]{1,0:T(8,128)(2,1)}, u32[]{:S(2)}, u32[]{:S(2)}) %collective-permute-start.21) | collective-permute-done | bytes 1048608 | tf_op jit(solution)/shard_map/ppermute | solution.py:481
  138.1 6.3 %fusion.110 = (f32[256]{0:T(256)S(1)}, f32[256,2048]{1,0:T(8,128)S(1)}) fusion(f32[2048]{0:T(1024)S(1)} %copy-done.129, bf16[2048,256]{1,0:T(8,128)(2,1)} %bitcast.24, bf16[2048,2048]{1,0:T(8,128)(2,1)} %all-gather.3.cloned.1.call-done, bf16[1,256,2048]{2,1,0:T(8,128)(2,1)S(1)} %copy-done.57), kind=kOutput, calls=%fused_computation.258 | convolution fusion | flops 2149580544 | bytes 12592128 | tf_op jit(solution)/shard_map/dot_general | solution.py:17
  147.9 10.7 %collective-permute-done.23.refs_8_.refs_3_.refs_5_ = bf16[256,2048]{1,0:T(8,128)(2,1)} collective-permute-done((bf16[256,2048]{1,0:T(8,128)(2,1)}, bf16[256,2048]{1,0:T(8,128)(2,1)}, u32[]{:S(2)}, u32[]{:S(2)}) %collective-permute-start.23) | collective-permute-done | bytes 1048608 | tf_op jit(solution)/shard_map/ppermute | solution.py:481
  158.6 6.7 %collective-permute-done.16.refs_1_.refs_2_ = bf16[256,2048]{1,0:T(8,128)(2,1)S(1)} collective-permute-done((bf16[256,2048]{1,0:T(8,128)(2,1)S(1)}, bf16[256,2048]{1,0:T(8,128)(2,1)S(1)}, u32[]{:S(2)}, u32[]{:S(2)}) %collective-permute-start.16) | collective-permute-done | bytes 1048608 | tf_op jit(solution)/shard_map/ppermute | solution.py:473
  174.1 21.5 %collective-permute-done.22.refs_6_.refs_1_ = bf16[256,2048]{1,0:T(8,128)(2,1)} collective-permute-done((bf16[256,2048]{1,0:T(8,128)(2,1)S(1)}, bf16[256,2048]{1,0:T(8,128)(2,1)}, u32[]{:S(2)}, u32[]{:S(2)}) %collective-permute-start.22) | collective-permute-done | bytes 1048608 | tf_op jit(solution)/shard_map/ppermute | solution.py:481
  201.5 10.4 %hidden_forward.3 = (f32[1024,1024]{1,0:T(8,128)}, bf16[1024,1024]{1,0:T(8,128)(2,1)S(1)}) custom-call(bf16[256,2048]{1,0:T(8,128)(2,1)S(1)} %add_convert_fusion.1.refs_0_.refs_1_, bf16[256,2048]{1,0:T(8,128)(2,1)S(1)} %copy-done.35, bf16[128,2048]{1,0:T(8,128)(2,1)} %collective-permute-done.17.refs_2_.refs_3_, ...), custom_call_target="tpu_custom_call" | custom-call | flops 4294967296 | bytes 14684160 | tf_op jit(solution)/shard_map/hidden_forward/pallas_call | solution.py:57
  212.0 9.4 %collective-permute-done.27.refs_7_.refs_2_ = bf16[256,2048]{1,0:T(8,128)(2,1)S(1)} collective-permute-done((bf16[256,2048]{1,0:T(8,128)(2,1)}, bf16[256,2048]{1,0:T(8,128)(2,1)S(1)}, u32[]{:S(2)}, u32[]{:S(2)}) %collective-permute-start.27) | collective-permute-done | bytes 1048608 | tf_op jit(solution)/shard_map/ppermute | solution.py:481
  221.5 9.7 %weight_terms.4 = bf16[1024,2048]{1,0:T(8,128)(2,1)} custom-call(bf16[1024,1024]{1,0:T(8,128)(2,1)S(1)} %get-tuple-element.167.refs_0_.refs_1_, bf16[256,2048]{1,0:T(8,128)(2,1)S(1)} %bitcast.232, bf16[256,2048]{1,0:T(8,128)(2,1)} %collective-permute-done.14.refs_2_.refs_1_, bf16[128,2048]{1,0:T(8,128)(2,1)S(1)} %collective-permute-done.24.refs_3_.refs_2_, ...), custom_call_target="tpu_custom_call" | custom-call | flops 4294967296 | bytes 10485760 | tf_op jit(solution)/shard_map/weight_terms/pallas_call | solution.py:57
  234.6 9.8 %hidden_forward.2 = (f32[1024,1024]{1,0:T(8,128)}, bf16[1024,1024]{1,0:T(8,128)(2,1)}) custom-call(bf16[256,2048]{1,0:T(8,128)(2,1)S(1)} %add_convert_fusion.1.refs_0_.refs_1_, bf16[256,2048]{1,0:T(8,128)(2,1)S(1)} %copy-done.35, bf16[128,2048]{1,0:T(8,128)(2,1)} %collective-permute-done.17.refs_2_.refs_3_, ...), custom_call_target="tpu_custom_call" | custom-call | flops 4294967296 | bytes 14684160 | tf_op jit(solution)/shard_map/hidden_forward/pallas_call | solution.py:57
  246.0 8.9 %weight_terms.5.refs_0_ = bf16[1024,2048]{1,0:T(8,128)(2,1)} custom-call(bf16[1024,1024]{1,0:T(8,128)(2,1)S(1)} %copy-done.12, bf16[256,2048]{1,0:T(8,128)(2,1)S(1)} %bitcast.233, bf16[256,2048]{1,0:T(8,128)(2,1)} %collective-permute-done.14.refs_2_.refs_1_, bf16[128,2048]{1,0:T(8,128)(2,1)S(1)} %collective-permute-done.24.refs_3_.refs_2_, ...), custom_call_target="tpu_custom_call" | custom-call | flops 4294967296 | bytes 10485760 | tf_op jit(solution)/shard_map/weight_terms/pallas_call | solution.py:57
  282.2 10.6 %hidden_backward.2 = (bf16[1024,1024]{1,0:T(8,128)(2,1)}, f32[1,1024]{1,0:T(1,128)S(1)}) custom-call(bf16[256,2048]{1,0:T(8,128)(2,1)S(1)} %bitcast.234, bf16[256,2048]{1,0:T(8,128)(2,1)} %collective-permute-done.14.refs_2_.refs_1_, bf16[128,2048]{1,0:T(8,128)(2,1)S(1)} %copy-done.43, bf16[128,2048]{1,0:T(8,128)(2,1)S(1)} %copy-done.45, ...), custom_call_target="tpu_custom_call" | custom-call | flops 4294967296 | bytes 14684160 | tf_op jit(solution)/shard_map/hidden_backward/pallas_call | solution.py:57
  292.8 7.1 %collective-permute-done.33 = bf16[128,2048]{0,1:T(8,128)(2,1)S(1)} collective-permute-done((bf16[128,2048]{0,1:T(8,128)(2,1)S(1)}, bf16[128,2048]{0,1:T(8,128)(2,1)S(1)}, u32[]{:S(2)}, u32[]{:S(2)}) %collective-permute-start.33) | collective-permute-done | bytes 524320 | tf_op jit(solution)/shard_map/ppermute | solution.py:473
  302.1 11.0 %hidden_backward.3 = (bf16[1024,1024]{1,0:T(8,128)(2,1)S(1)}, f32[1,1024]{1,0:T(1,128)S(1)}) custom-call(bf16[256,2048]{1,0:T(8,128)(2,1)S(1)} %bitcast.235, bf16[256,2048]{1,0:T(8,128)(2,1)} %collective-permute-done.14.refs_2_.refs_1_, bf16[128,2048]{1,0:T(8,128)(2,1)S(1)} %copy-done.43, bf16[128,2048]{1,0:T(8,128)(2,1)S(1)} %copy-done.46, ...), custom_call_target="tpu_custom_call" | custom-call | flops 4294967296 | bytes 14684160 | tf_op jit(solution)/shard_map/hidden_backward/pallas_call | solution.py:57
  314.4 14.6 %hidden_sum.2 = (f32[256,2048]{1,0:T(8,128)S(1)}, bf16[128,2048]{1,0:T(8,128)(2,1)}, bf16[128,2048]{1,0:T(8,128)(2,1)}, bf16[128,2048]{1,0:T(8,128)(2,1)S(1)}, b...) custom-call(bf16[1024,1024]{1,0:T(8,128)(2,1)} %get-tuple-element.201.refs_0_, ...), custom_call_target="tpu_custom_call" | custom-call | flops 8589934592 | bytes 17825792 | tf_op jit(solution)/shard_map/hidden_sum/pallas_call | solution.py:57
  340.6 7.5 %collective-permute-done.36 = bf16[128,2048]{1,0:T(8,128)(2,1)} collective-permute-done((bf16[128,2048]{1,0:T(8,128)(2,1)}, bf16[128,2048]{1,0:T(8,128)(2,1)}, u32[]{:S(2)}, u32[]{:S(2)}) %collective-permute-start.36) | collective-permute-done | bytes 524320 | tf_op jit(solution)/shard_map/ppermute | solution.py:473
  350.6 6.8 %collective-permute-done.38 = bf16[128,2048]{1,0:T(8,128)(2,1)} collective-permute-done((bf16[128,2048]{1,0:T(8,128)(2,1)}, bf16[128,2048]{1,0:T(8,128)(2,1)}, u32[]{:S(2)}, u32[]{:S(2)}) %collective-permute-start.38) | collective-permute-done | bytes 524320 | tf_op jit(solution)/shard_map/ppermute | solution.py:473
  359.6 18.8 %collective-permute-done.40.refs_3_ = bf16[256,2048]{1,0:T(8,128)(2,1)} collective-permute-done((bf16[256,2048]{1,0:T(8,128)(2,1)}, bf16[256,2048]{1,0:T(8,128)(2,1)}, u32[]{:S(2)}, u32[]{:S(2)}) %collective-permute-start.40) | collective-permute-done | bytes 1048608 | tf_op jit(solution)/shard_map/ppermute | solution.py:564
  379.9 8.5 %weight_terms.6 = bf16[1024,2048]{1,0:T(8,128)(2,1)} custom-call(bf16[1024,1024]{1,0:T(8,128)(2,1)S(1)} %copy-done.49, bf16[256,2048]{1,0:T(8,128)(2,1)S(1)} %copy-done.16, bf16[256,2048]{1,0:T(8,128)(2,1)S(1)} %copy-done.36, bf16[128,2048]{1,0:T(8,128)(2,1)} %collective-permute-done.17.refs_2_.refs_3_, ...), custom_call_target="tpu_custom_call" | custom-call | flops 4294967296 | bytes 10485760 | tf_op jit(solution)/shard_map/weight_terms/pallas_call | solution.py:57
  407.6 8.7 %weight_terms.7.refs_0_ = bf16[1024,2048]{1,0:T(8,128)(2,1)} custom-call(bf16[1024,1024]{1,0:T(8,128)(2,1)S(1)} %copy-done.47, bf16[256,2048]{1,0:T(8,128)(2,1)S(1)} %copy-done.17, bf16[256,2048]{1,0:T(8,128)(2,1)S(1)} %copy-done.37, bf16[128,2048]{1,0:T(8,128)(2,1)} %collective-permute-done.17.refs_2_.refs_3_, ...), custom_call_target="tpu_custom_call" | custom-call | flops 4294967296 | bytes 10485760 | tf_op jit(solution)/shard_map/weight_terms/pallas_call | solution.py:57
  420.1 6.3 %add_terms.11 = bf16[512,2048]{1,0:T(8,128)(2,1)} custom-call(bf16[1024,2048]{1,0:T(8,128)(2,1)S(1)} %copy-done.3, bf16[1024,2048]{1,0:T(8,128)(2,1)} %collective-permute-done.41.refs_1_), custom_call_target="tpu_custom_call" | custom-call | bytes 6291456 | tf_op jit(solution)/shard_map/add_terms/pallas_call | solution.py:126
  428.7 14.0 %hidden_sum.3 = (f32[256,2048]{1,0:T(8,128)S(1)}, bf16[256,2048]{1,0:T(8,128)(2,1)}, bf16[256,2048]{1,0:T(8,128)(2,1)}, bf16[256,2048]{1,0:T(8,128)(2,1)}) custom-call(bf16[1024,1024]{1,0:T(8,128)(2,1)S(1)} %copy-done.13, bf16[1024,1024]{1,0:T(8,128)(2,1)S(1)} %copy-done.11, bf16[1024,2048]{1,0:T(8,128)(2,1)} %join_rows.3.refs_2_, ...), custom_call_target="tpu_custom_call" | custom-call | tf_op jit(solution)/shard_map/hidden_sum/pallas_call | solution.py:57
  462.1 7.6 %collective-permute-done.42 = bf16[256,2048]{1,0:T(8,128)(2,1)} collective-permute-done((bf16[256,2048]{1,0:T(8,128)(2,1)}, bf16[256,2048]{1,0:T(8,128)(2,1)}, u32[]{:S(2)}, u32[]{:S(2)}) %collective-permute-start.42) | collective-permute-done | bytes 1048608 | tf_op jit(solution)/shard_map/ppermute | solution.py:473
  476.7 6.7 %fusion.21 = bf16[2048,256]{0,1:T(8,128)(2,1)} fusion(bf16[256,2048]{1,0:T(8,128)(2,1)S(1)} %gate.3, bf16[2048,2048]{1,0:T(8,128)(2,1)} %all-gather.3.cloned.1.call-done), kind=kOutput, calls=%fused_computation.29 | convolution fusion | flops 2148007936 | bytes 10485760 | tf_op jit(solution)/shard_map/dot_general | solution.py:854
  487.0 8.2 %fusion = bf16[16,1024,256]{1,2,0:T(8,128)(2,1)S(1)} fusion(f32[16,1024,256]{1,2,0:T(8,128)} %copy-done.59, bf16[16,128,256]{2,1,0:T(8,128)(2,1)S(1)} %bitcast.246, f32[16,256]{1,0:T(8,128)S(1)} %fusion.31, f32[16,256]{1,0:T(8,128)S(1)} %copy-done.126, pred[1024,256]{0,1:T(8,128)(4,1)S(1)} %copy-done.84, bf16[128,256]{1,0:T(8,128)(2,1)S(1)} %copy-done.114, ...), kind=kOutput, calls=%fused_computation.1 | convolution fusion | flops 1095761920 | bytes 26771456 | tf_op jit(solution)/shard_map/dk,hdq->hkq/dot_general | solution.py:861
  495.2 7.5 %fusion.32 = f32[128,1024]{1,0:T(8,128)S(1)} fusion(bf16[16,128,256]{2,1,0:T(8,128)(2,1)S(1)} %bitcast.247, f32[16,1024,256]{1,2,0:T(8,128)} %copy-done.59, f32[16,256]{1,0:T(8,128)S(1)} %copy-done.126, pred[1024,256]{0,1:T(8,128)(4,1)S(1)} %copy-done.84), kind=kOutput, calls=%fused_computation.65 | convolution fusion | flops 1086324736 | bytes 18628608 | tf_op jit(solution)/shard_map/hkq,hdq->dk/dot_general | solution.py:865
  539.8 5.5 collective-permute-done.53
  555.5 10.0 %collective-permute-done.68.refs_2_ = bf16[128,2048]{1,0:T(8,128)(2,1)S(1)} collective-permute-done((bf16[128,2048]{1,0:T(8,128)(2,1)S(1)}, bf16[128,2048]{1,0:T(8,128)(2,1)S(1)}, u32[]{:S(2)}, u32[]{:S(2)}) %collective-permute-start.68) | collective-permute-done | bytes 524320 | tf_op jit(solution)/shard_map/ppermute | solution.py:564
  570.8 9.3 %collective-permute-done.69.refs_3_ = bf16[64,2048]{1,0:T(8,128)(2,1)S(1)} collective-permute-done((bf16[64,2048]{1,0:T(8,128)(2,1)S(1)}, bf16[64,2048]{1,0:T(8,128)(2,1)S(1)}, u32[]{:S(2)}, u32[]{:S(2)}) %collective-permute-start.69) | collective-permute-done | bytes 262176 | tf_op jit(solution)/shard_map/ppermute | solution.py:564
  (579 shorter events, 290.6 us)
Async XLA Ops:
  7.2 130.9 %all-gather.3.cloned.1.call-start = ((), (), s32[]{:S(2)}) async-start(), calls=%async_computation | async-start | bytes 8650752 | tf_op jit(solution)/shard_map/all_gather | solution.py:679
  7.9 389.8 %all-gather.5.cloned.1.call-start = ((), (), s32[]{:S(2)}) async-start(), calls=%async_computation.1 | async-start | bytes 5898240 | tf_op jit(solution)/shard_map/all_gather | solution.py:763
  18.6 26.0 %collective-permute-start.3 = (bf16[256,2048]{1,0:T(8,128)(2,1)S(1)}, bf16[256,2048]{1,0:T(8,128)(2,1)}, u32[]{:S(2)}, u32[]{:S(2)}) collective-permute-start(bf16[256,2048]{1,0:T(8,128)(2,1)S(1)} %fusion.23), channel_id=1, source_target_pairs={{1,0},{3,1},{2,3},{0,2},{5,4},{7,5},{6,7},{4,6},{9,8},{11,9},{10,1... | collective-permute-start | bytes 3145736 | tf_op jit(solution)/shard_map/ppermute | solution.py:473
  20.2 25.6 %collective-permute-start.4 = (bf16[256,2048]{1,0:T(8,128)(2,1)S(1)}, bf16[256,2048]{1,0:T(8,128)(2,1)S(1)}, u32[]{:S(2)}, u32[]{:S(2)}) collective-permute-start(bf16[256,2048]{1,0:T(8,128)(2,1)S(1)} %fusion.23), channel_id=1, source_target_pairs={{2,0},{0,1},{1,3},{3,2},{6,4},{4,5},{5,7},{7,6},{10,8},{8,9},{9,11... | collective-permute-start | bytes 3145736 | tf_op jit(solution)/shard_map/ppermute | solution.py:473
  49.6 64.2 %collective-permute-start.20 = (bf16[256,2048]{1,0:T(8,128)(2,1)S(1)}, bf16[256,2048]{1,0:T(8,128)(2,1)S(1)}, u32[]{:S(2)}, u32[]{:S(2)}) collective-permute-start(bf16[256,2048]{1,0:T(8,128)(2,1)S(1)} %copy-done.20), channel_id=1, source_target_pairs={{8,0},{12,4},{0,16},{4,20},{16,24},{20,28},{24,8},{28,12},{9,1},{1... | collective-permute-start | bytes 3145736 | tf_op jit(solution)/shard_map/ppermute | solution.py:481
  72.4 27.2 %collective-permute-start.10 = (bf16[576,256]{1,0:T(8,128)(2,1)}, bf16[576,256]{1,0:T(8,128)(2,1)S(1)}, u32[]{:S(2)}, u32[]{:S(2)}) collective-permute-start(bf16[576,256]{1,0:T(8,128)(2,1)} %fusion.38), channel_id=1, source_target_pairs={{1,0},{3,1},{2,3},{0,2},{5,4},{7,5},{6,7},{4,6},{9,8},{11,9},{10,1... | collective-permute-start | bytes 884744 | tf_op jit(solution)/shard_map/ppermute | solution.py:473
  73.9 25.7 %collective-permute-start.6 = (bf16[576,256]{1,0:T(8,128)(2,1)}, bf16[576,256]{1,0:T(8,128)(2,1)S(1)}, u32[]{:S(2)}, u32[]{:S(2)}) collective-permute-start(bf16[576,256]{1,0:T(8,128)(2,1)} %fusion.37), channel_id=1, source_target_pairs={{2,0},{0,1},{1,3},{3,2},{6,4},{4,5},{5,7},{7,6},{10,8},{8,9},{9,11... | collective-permute-start | bytes 884744 | tf_op jit(solution)/shard_map/ppermute | solution.py:473
  111.8 34.0 %collective-permute-start.14 = (bf16[256,2048]{1,0:T(8,128)(2,1)S(1)}, bf16[256,2048]{1,0:T(8,128)(2,1)}, u32[]{:S(2)}, u32[]{:S(2)}) collective-permute-start(bf16[256,2048]{1,0:T(8,128)(2,1)S(1)} %bitcast.230), channel_id=1, source_target_pairs={{1,0},{3,1},{2,3},{0,2},{5,4},{7,5},{6,7},{4,6},{9,8},{11,9},{10,1... | collective-permute-start | bytes 3145736 | tf_op jit(solution)/shard_map/ppermute | solution.py:473
  113.1 32.7 %collective-permute-start.15 = (bf16[256,2048]{1,0:T(8,128)(2,1)S(1)}, bf16[256,2048]{1,0:T(8,128)(2,1)}, u32[]{:S(2)}, u32[]{:S(2)}) collective-permute-start(bf16[256,2048]{1,0:T(8,128)(2,1)S(1)} %bitcast.231), channel_id=1, source_target_pairs={{2,0},{0,1},{1,3},{3,2},{6,4},{4,5},{5,7},{7,6},{10,8},{8,9},{9,11... | collective-permute-start | bytes 3145736 | tf_op jit(solution)/shard_map/ppermute | solution.py:473
  169.8 31.7 %collective-permute-start.26 = (bf16[1024,2048]{1,0:T(8,128)(2,1)}, bf16[1024,2048]{1,0:T(8,128)(2,1)}, u32[]{:S(2)}, u32[]{:S(2)}) collective-permute-start(bf16[1024,2048]{1,0:T(8,128)(2,1)} %join_rows.2), channel_id=1, source_target_pairs={{0,4},{4,0},{8,12},{12,8},{16,20},{20,16},{24,28},{28,24},{1,5},{5... | collective-permute-start | bytes 12582920 | tf_op jit(solution)/shard_map/ppermute | solution.py:477
  169.9 25.7 %collective-permute-start.22 = (bf16[256,2048]{1,0:T(8,128)(2,1)S(1)}, bf16[256,2048]{1,0:T(8,128)(2,1)}, u32[]{:S(2)}, u32[]{:S(2)}) collective-permute-start(bf16[256,2048]{1,0:T(8,128)(2,1)S(1)} %copy-done.18), channel_id=1, source_target_pairs={{8,0},{12,4},{0,16},{4,20},{16,24},{20,28},{24,8},{28,12},{9,1},{1... | collective-permute-start | bytes 3145736 | tf_op jit(solution)/shard_map/ppermute | solution.py:481
  171.1 24.5 %collective-permute-start.17 = (bf16[128,2048]{1,0:T(8,128)(2,1)}, bf16[128,2048]{1,0:T(8,128)(2,1)}, u32[]{:S(2)}, u32[]{:S(2)}) collective-permute-start(bf16[128,2048]{1,0:T(8,128)(2,1)} %slice.234), channel_id=1, source_target_pairs={{1,0},{3,1},{2,3},{0,2},{5,4},{7,5},{6,7},{4,6},{9,8},{11,9},{10,1... | collective-permute-start | bytes 1572872 | tf_op jit(solution)/shard_map/ppermute | solution.py:473
  195.6 25.8 %collective-permute-start.27 = (bf16[256,2048]{1,0:T(8,128)(2,1)}, bf16[256,2048]{1,0:T(8,128)(2,1)S(1)}, u32[]{:S(2)}, u32[]{:S(2)}) collective-permute-start(bf16[256,2048]{1,0:T(8,128)(2,1)} %collective-permute-done.22.refs_6_.refs_1_), channel_id=1, source_target_pairs={{8,0},{12,4},{0,16},{4,20},{16,24},{20,28},{24,8},{28,12},{9,1},{1... | collective-permute-start | bytes 3145736 | tf_op jit(solution)/shard_map/ppermute | solution.py:481
  231.2 26.6 %collective-permute-start.29 = (bf16[1024,2048]{1,0:T(8,128)(2,1)}, bf16[1024,2048]{1,0:T(8,128)(2,1)S(1)}, u32[]{:S(2)}, u32[]{:S(2)}) collective-permute-start(bf16[1024,2048]{1,0:T(8,128)(2,1)} %weight_terms.4), channel_id=1, source_target_pairs={{0,4},{4,0},{8,12},{12,8},{16,20},{20,16},{24,28},{28,24},{1,5},{5... | collective-permute-start | bytes 12582920 | tf_op jit(solution)/shard_map/ppermute | solution.py:477
  231.3 25.8 %collective-permute-start.30 = (bf16[256,2048]{0,1:T(8,128)(2,1)}, bf16[256,2048]{0,1:T(8,128)(2,1)S(1)}, u32[]{:S(2)}, u32[]{:S(2)}) collective-permute-start(bf16[256,2048]{0,1:T(8,128)(2,1)} %bitcast.26), channel_id=1, source_target_pairs={{1,0},{3,1},{2,3},{0,2},{5,4},{7,5},{6,7},{4,6},{9,8},{11,9},{10,1... | collective-permute-start | bytes 3145736 | tf_op jit(solution)/shard_map/ppermute | solution.py:473
  232.4 25.4 %collective-permute-start.31 = (bf16[256,2048]{0,1:T(8,128)(2,1)}, bf16[256,2048]{0,1:T(8,128)(2,1)S(1)}, u32[]{:S(2)}, u32[]{:S(2)}) collective-permute-start(bf16[256,2048]{0,1:T(8,128)(2,1)} %bitcast.26), channel_id=1, source_target_pairs={{2,0},{0,1},{1,3},{3,2},{6,4},{4,5},{5,7},{7,6},{10,8},{8,9},{9,11... | collective-permute-start | bytes 3145736 | tf_op jit(solution)/shard_map/ppermute | solution.py:473
  233.3 34.2 %collective-permute-start.28 = (bf16[256,2048]{1,0:T(8,128)(2,1)S(1)}, bf16[256,2048]{1,0:T(8,128)(2,1)S(1)}, u32[]{:S(2)}, u32[]{:S(2)}) collective-permute-start(bf16[256,2048]{1,0:T(8,128)(2,1)S(1)} %collective-permute-done.27.refs_7_.refs_2_), channel_id=1, source_target_pairs={{8,0},{12,4},{0,16},{4,20},{16,24},{20,28},{24,8},{28,12},{9,1},{1... | collective-permute-start | bytes 3145736 | tf_op jit(solution)/shard_map/ppermute | solution.py:481
  271.3 30.0 %collective-permute-start.32 = (bf16[1024,2048]{1,0:T(8,128)(2,1)}, bf16[1024,2048]{1,0:T(8,128)(2,1)}, u32[]{:S(2)}, u32[]{:S(2)}) collective-permute-start(bf16[1024,2048]{1,0:T(8,128)(2,1)} %join_rows.3.refs_2_), channel_id=1, source_target_pairs={{0,4},{4,0},{8,12},{12,8},{16,20},{20,16},{24,28},{28,24},{1,5},{5... | collective-permute-start | bytes 12582920 | tf_op jit(solution)/shard_map/ppermute | solution.py:477
  271.4 57.6 %collective-permute-start.35 = (bf16[512,2048]{1,0:T(8,128)(2,1)}, bf16[512,2048]{1,0:T(8,128)(2,1)S(1)}, u32[]{:S(2)}, u32[]{:S(2)}) collective-permute-start(bf16[512,2048]{1,0:T(8,128)(2,1)} %copy-done.9), channel_id=1, source_target_pairs={{0,8},{4,12},{8,0},{12,4},{16,24},{20,28},{24,16},{28,20},{1,9},{5... | collective-permute-start | bytes 6291464 | tf_op jit(solution)/shard_map/ppermute | solution.py:564
  276.9 24.4 %collective-permute-start.34 = (bf16[128,2048]{0,1:T(8,128)(2,1)S(1)}, bf16[128,2048]{0,1:T(8,128)(2,1)S(1)}, u32[]{:S(2)}, u32[]{:S(2)}) collective-permute-start(bf16[128,2048]{0,1:T(8,128)(2,1)S(1)} %slice.195), channel_id=1, source_target_pairs={{2,0},{0,1},{1,3},{3,2},{6,4},{4,5},{5,7},{7,6},{10,8},{8,9},{9,11... | collective-permute-start | bytes 1572872 | tf_op jit(solution)/shard_map/ppermute | solution.py:473
  332.8 45.6 %collective-permute-start.40 = (bf16[256,2048]{1,0:T(8,128)(2,1)}, bf16[256,2048]{1,0:T(8,128)(2,1)}, u32[]{:S(2)}, u32[]{:S(2)}) collective-permute-start(bf16[256,2048]{1,0:T(8,128)(2,1)} %add_terms.10), channel_id=1, source_target_pairs={{0,16},{4,20},{8,24},{12,28},{16,0},{20,4},{24,8},{28,12},{1,17},{... | collective-permute-start | bytes 3145736 | tf_op jit(solution)/shard_map/ppermute | solution.py:564
  388.5 31.6 %collective-permute-start.41 = (bf16[1024,2048]{1,0:T(8,128)(2,1)}, bf16[1024,2048]{1,0:T(8,128)(2,1)}, u32[]{:S(2)}, u32[]{:S(2)}) collective-permute-start(bf16[1024,2048]{1,0:T(8,128)(2,1)} %weight_terms.6), channel_id=1, source_target_pairs={{0,4},{4,0},{8,12},{12,8},{16,20},{20,16},{24,28},{28,24},{1,5},{5... | collective-permute-start | bytes 12582920 | tf_op jit(solution)/shard_map/ppermute | solution.py:477
  397.8 126.1 %collective-permute-start.54 = (bf16[1152,2048]{1,0:T(8,128)(2,1)}, bf16[1152,2048]{1,0:T(8,128)(2,1)}, u32[]{:S(2)}, u32[]{:S(2)}) collective-permute-start(bf16[1152,2048]{1,0:T(8,128)(2,1)} %bitcast.274), channel_id=1, source_target_pairs={{0,4},{4,0},{8,12},{12,8},{16,20},{20,16},{24,28},{28,24},{1,5},{5... | collective-permute-start | bytes 14155784 | tf_op jit(solution)/shard_map/ppermute | solution.py:477
  426.4 47.5 %collective-permute-start.47 = (bf16[512,2048]{1,0:T(8,128)(2,1)}, bf16[512,2048]{1,0:T(8,128)(2,1)}, u32[]{:S(2)}, u32[]{:S(2)}) collective-permute-start(bf16[512,2048]{1,0:T(8,128)(2,1)} %add_terms.11), channel_id=1, source_target_pairs={{0,8},{4,12},{8,0},{12,4},{16,24},{20,28},{24,16},{28,20},{1,9},{5... | collective-permute-start | bytes 6291464 | tf_op jit(solution)/shard_map/ppermute | solution.py:564
  444.0 25.7 %collective-permute-start.42 = (bf16[256,2048]{1,0:T(8,128)(2,1)}, bf16[256,2048]{1,0:T(8,128)(2,1)}, u32[]{:S(2)}, u32[]{:S(2)}) collective-permute-start(bf16[256,2048]{1,0:T(8,128)(2,1)} %get-tuple-element.204), channel_id=1, source_target_pairs={{2,0},{0,1},{1,3},{3,2},{6,4},{4,5},{5,7},{7,6},{10,8},{8,9},{9,11... | collective-permute-start | bytes 3145736 | tf_op jit(solution)/shard_map/ppermute | solution.py:473
  445.9 58.3 %collective-permute-start.43 = (bf16[256,2048]{1,0:T(8,128)(2,1)}, bf16[256,2048]{1,0:T(8,128)(2,1)}, u32[]{:S(2)}, u32[]{:S(2)}) collective-permute-start(bf16[256,2048]{1,0:T(8,128)(2,1)} %get-tuple-element.205), channel_id=1, source_target_pairs={{3,0},{2,1},{0,3},{1,2},{7,4},{6,5},{4,7},{5,6},{11,8},{10,9},{8,1... | collective-permute-start | bytes 3145736 | tf_op jit(solution)/shard_map/ppermute | solution.py:473
  447.3 60.3 %collective-permute-start.44 = (bf16[256,2048]{1,0:T(8,128)(2,1)}, bf16[256,2048]{1,0:T(8,128)(2,1)}, u32[]{:S(2)}, u32[]{:S(2)}) collective-permute-start(bf16[256,2048]{1,0:T(8,128)(2,1)} %get-tuple-element.206), channel_id=1, source_target_pairs={{1,0},{3,1},{2,3},{0,2},{5,4},{7,5},{6,7},{4,6},{9,8},{11,9},{10,1... | collective-permute-start | bytes 3145736 | tf_op jit(solution)/shard_map/ppermute | solution.py:473
  469.7 37.9 %collective-permute-start.64 = (bf16[512,256]{1,0:T(8,128)(2,1)}, bf16[512,256]{1,0:T(8,128)(2,1)}, u32[]{:S(2)}, u32[]{:S(2)}) collective-permute-start(bf16[512,256]{1,0:T(8,128)(2,1)} %bitcast.69), channel_id=1, source_target_pairs={{1,0},{3,1},{2,3},{0,2},{5,4},{7,5},{6,7},{4,6},{9,8},{11,9},{10,1... | collective-permute-start | bytes 786440 | tf_op jit(solution)/shard_map/ppermute | solution.py:473
  473.9 35.1 %collective-permute-start.65 = (bf16[512,256]{1,0:T(8,128)(2,1)}, bf16[512,256]{1,0:T(8,128)(2,1)}, u32[]{:S(2)}, u32[]{:S(2)}) collective-permute-start(bf16[512,256]{1,0:T(8,128)(2,1)} %bitcast.68), channel_id=1, source_target_pairs={{3,0},{2,1},{0,3},{1,2},{7,4},{6,5},{4,7},{5,6},{11,8},{10,9},{8,1... | collective-permute-start | bytes 786440 | tf_op jit(solution)/shard_map/ppermute | solution.py:473
  507.6 46.8 %collective-permute-start.56 = (bf16[256,2048]{1,0:T(8,128)(2,1)S(1)}, bf16[256,2048]{1,0:T(8,128)(2,1)S(1)}, u32[]{:S(2)}, u32[]{:S(2)}) collective-permute-start(bf16[256,2048]{1,0:T(8,128)(2,1)S(1)} %add_terms.12), channel_id=1, source_target_pairs={{0,16},{4,20},{8,24},{12,28},{16,0},{20,4},{24,8},{28,12},{1,17},{... | collective-permute-start | bytes 3145736 | tf_op jit(solution)/shard_map/ppermute | solution.py:564
  521.8 27.2 %collective-permute-start.67 = (bf16[4,64,2048]{2,1,0:T(8,128)(2,1)S(1)}, bf16[4,64,2048]{2,1,0:T(8,128)(2,1)S(1)}, u32[]{:S(2)}, u32[]{:S(2)}) collective-permute-start(bf16[4,64,2048]{2,1,0:T(8,128)(2,1)S(1)} %get-tuple-element.263), channel_id=1, source_target_pairs={{0,4},{4,0},{8,12},{12,8},{16,20},{20,16},{24,28},{28,24},{1,5},{5... | collective-permute-start | bytes 3145736 | tf_op jit(solution)/shard_map/ppermute | solution.py:477
  554.3 30.4 %collective-permute-start.57 = (bf16[144,2048]{1,0:T(8,128)(2,1)S(1)}, bf16[144,2048]{1,0:T(8,128)(2,1)S(1)}, u32[]{:S(2)}, u32[]{:S(2)}) collective-permute-start(bf16[144,2048]{1,0:T(8,128)(2,1)S(1)} %add_convert_fusion.2), channel_id=1, source_target_pairs={{0,8},{4,12},{8,0},{12,4},{16,24},{20,28},{24,16},{28,20},{1,9},{5... | collective-permute-start | bytes 1769480 | tf_op jit(solution)/shard_map/ppermute | solution.py:564
  (182 other events, 2457.1 us)
Sparse Core Ops, SparseCore 0:
  10.9 101.4 all-gather.2
  271.5 63.0 all-gather.4

commit v5 on v4

--- a/solution.py
+++ b/solution.py
@@ -811,7 +811,7 @@
     )
     mlp_came = [links.from_rel(mlp_parts[r], seq_n - r) for r in range(1, seq_n)]
 
-    inverse_two = gate(inverse_two, mlp_parts)
+    inverse_two = gate(inverse_two, fc_term)
 
     def middle_back(parts, far, near, normed_two, inverse_two, grad_low):
         grad_hidden = links.sum_end(parts, far, near)
@@ -868,7 +868,7 @@
         grad_query = grad_query.reshape(width, tok)
         return grad_query.astype(BF), jnp.sum(grad_query, 1), [parts[0]] + [part.astype(BF) for part in parts[1:]]
 
-    grad_middle_low = gate(grad_middle_low, fc_first)
+    grad_middle_low = gate(grad_middle_low, fc_first, mlp_parts)
     grad_query, query_sum, parts = attend_back(out_full, grad_middle_low, query, pairs, attn, log_total
     )
     came = links.exchange(after(parts, mlp_came))

time: 623 us -> 630 us (1.011)
    ppermute x8, starting transfers between devices: 3.97 us -> 11.5 us  [other_chip(): return lax.ppermute(value, 'dp', pairs)]
    ppermute x40, waiting for transfers between devices: 93.1 us -> 101 us  [from_rel(): return lax.ppermute(value, 'seq', pairs)]
  transfers between devices with their start and end apart: 72 -> 72, of which waited for: 41 -> 38; matrix products, arithmetic and copies ran while one was open for 22% -> 22% of each run, Pallas kernels for 20% -> 20%
where the time goes in v5:
time: 630 us; the launch traced here: 622 us
  waiting for transfers between devices  219 us (35%)
  Pallas kernels  140 us (22%)
  starting transfers between devices  81 us (13%)
  local copies, waits for them, and re-layouts  62.5 us (10%)
  matrix products  61.2 us (10%)
  other arithmetic  40.9 us (6%)
  between operations  16.9 us (3%)
    pallas_call x12, Pallas kernels, call(): pl.pallas_call(kernel, name=name, out_shape=out_shape, in_specs=[ANY] * l...  114 us
    ppermute x40, waiting for transfers between devices, from_rel(): return lax.ppermute(value, 'seq', pairs)  101 us
    ppermute x9, waiting for transfers between devices, z_next(): lax.ppermute(value, 'dp', [(2 * i + c, 2 * j + c) for i, j in pairs for c...  65.3 us
    ppermute x40, starting transfers between devices, from_rel(): return lax.ppermute(value, 'seq', pairs)  47.7 us
    ppermute x8, waiting for transfers between devices, other_chip(): return lax.ppermute(value, 'dp', pairs)  42.3 us
    unnamed x305, local copies, waits for them, and re-layouts  39.3 us
    pallas_call x9, Pallas kernels, add_terms(): pl.pallas_call(kernel, name='add_terms', grid=(rows // step,), out_shape=...  25.8 us
    ppermute x9, starting transfers between devices, z_next(): lax.ppermute(value, 'dp', [(2 * i + c, 2 * j + c) for i, j in pairs for c...  19 us
  transfers between devices with their start and end apart: 72, of which 38 were waited for; matrix products, arithmetic and copies ran while one was open for 22% of the time, Pallas kernels for 20%

profile of v5, /device:TPU:0, one launch (start us, length us, event | category | flops | bytes accessed | tf_op | source)
XLA Modules:
  0.0 621.6 jit_solution(9181954488385422321)
XLA Ops:
  23.9 8.8 %collective-permute-done.1 = bf16[72,2048]{1,0:T(8,128)(2,1)} collective-permute-done((bf16[72,2048]{1,0:T(8,128)(2,1)S(1)}, bf16[72,2048]{1,0:T(8,128)(2,1)}, u32[]{:S(2)}, u32[]{:S(2)}) %collective-permute-start.1) | collective-permute-done | bytes 294944 | tf_op jit(solution)/shard_map/ppermute | solution.py:481
  36.3 5.8 collective-permute-done.2
  76.2 12.9 %collective-permute-done.9 = bf16[576,256]{1,0:T(8,128)(2,1)S(1)} collective-permute-done((bf16[576,256]{1,0:T(8,128)(2,1)}, bf16[576,256]{1,0:T(8,128)(2,1)S(1)}, u32[]{:S(2)}, u32[]{:S(2)}) %collective-permute-start.9) | collective-permute-done | bytes 294944 | tf_op jit(solution)/shard_map/ppermute | solution.py:473
  89.2 10.4 %collective-permute-done.10 = bf16[576,256]{1,0:T(8,128)(2,1)S(1)} collective-permute-done((bf16[576,256]{1,0:T(8,128)(2,1)}, bf16[576,256]{1,0:T(8,128)(2,1)S(1)}, u32[]{:S(2)}, u32[]{:S(2)}) %collective-permute-start.10) | collective-permute-done | bytes 294944 | tf_op jit(solution)/shard_map/ppermute | solution.py:473
  129.5 7.6 %collective-permute-done.21.refs_7_.refs_2_.refs_4_ = bf16[256,2048]{1,0:T(8,128)(2,1)} collective-permute-done((bf16[256,2048]{1,0:T(8,128)(2,1)S(1)}, bf16[256,2048]{1,0:T(8,128)(2,1)}, u32[]{:S(2)}, u32[]{:S(2)}) %collective-permute-start.21) | collective-permute-done | bytes 1048608 | tf_op jit(solution)/shard_map/ppermute | solution.py:481
  138.1 6.3 %fusion.110 = (f32[256]{0:T(256)S(1)}, f32[256,2048]{1,0:T(8,128)S(1)}) fusion(f32[2048]{0:T(1024)S(1)} %copy-done.129, bf16[2048,256]{1,0:T(8,128)(2,1)} %bitcast.24, bf16[2048,2048]{1,0:T(8,128)(2,1)} %all-gather.3.cloned.1.call-done, bf16[1,256,2048]{2,1,0:T(8,128)(2,1)S(1)} %copy-done.57), kind=kOutput, calls=%fused_computation.258 | convolution fusion | flops 2149580544 | bytes 12592128 | tf_op jit(solution)/shard_map/dot_general | solution.py:17
  147.9 10.7 %collective-permute-done.23.refs_8_.refs_3_.refs_5_ = bf16[256,2048]{1,0:T(8,128)(2,1)} collective-permute-done((bf16[256,2048]{1,0:T(8,128)(2,1)}, bf16[256,2048]{1,0:T(8,128)(2,1)}, u32[]{:S(2)}, u32[]{:S(2)}) %collective-permute-start.23) | collective-permute-done | bytes 1048608 | tf_op jit(solution)/shard_map/ppermute | solution.py:481
  158.6 6.7 %collective-permute-done.16.refs_1_.refs_2_ = bf16[256,2048]{1,0:T(8,128)(2,1)S(1)} collective-permute-done((bf16[256,2048]{1,0:T(8,128)(2,1)S(1)}, bf16[256,2048]{1,0:T(8,128)(2,1)S(1)}, u32[]{:S(2)}, u32[]{:S(2)}) %collective-permute-start.16) | collective-permute-done | bytes 1048608 | tf_op jit(solution)/shard_map/ppermute | solution.py:473
  174.1 21.5 %collective-permute-done.22.refs_6_.refs_1_ = bf16[256,2048]{1,0:T(8,128)(2,1)} collective-permute-done((bf16[256,2048]{1,0:T(8,128)(2,1)S(1)}, bf16[256,2048]{1,0:T(8,128)(2,1)}, u32[]{:S(2)}, u32[]{:S(2)}) %collective-permute-start.22) | collective-permute-done | bytes 1048608 | tf_op jit(solution)/shard_map/ppermute | solution.py:481
  201.5 10.4 %hidden_forward.3 = (f32[1024,1024]{1,0:T(8,128)}, bf16[1024,1024]{1,0:T(8,128)(2,1)S(1)}) custom-call(bf16[256,2048]{1,0:T(8,128)(2,1)S(1)} %add_convert_fusion.1.refs_0_.refs_1_, bf16[256,2048]{1,0:T(8,128)(2,1)S(1)} %copy-done.35, bf16[128,2048]{1,0:T(8,128)(2,1)} %collective-permute-done.17.refs_2_.refs_3_, ...), custom_call_target="tpu_custom_call" | custom-call | flops 4294967296 | bytes 14684160 | tf_op jit(solution)/shard_map/hidden_forward/pallas_call | solution.py:57
  212.0 9.4 %collective-permute-done.27.refs_7_.refs_2_ = bf16[256,2048]{1,0:T(8,128)(2,1)S(1)} collective-permute-done((bf16[256,2048]{1,0:T(8,128)(2,1)}, bf16[256,2048]{1,0:T(8,128)(2,1)S(1)}, u32[]{:S(2)}, u32[]{:S(2)}) %collective-permute-start.27) | collective-permute-done | bytes 1048608 | tf_op jit(solution)/shard_map/ppermute | solution.py:481
  221.5 9.7 %weight_terms.4 = bf16[1024,2048]{1,0:T(8,128)(2,1)} custom-call(bf16[1024,1024]{1,0:T(8,128)(2,1)S(1)} %get-tuple-element.167.refs_0_.refs_1_, bf16[256,2048]{1,0:T(8,128)(2,1)S(1)} %bitcast.232, bf16[256,2048]{1,0:T(8,128)(2,1)} %collective-permute-done.14.refs_2_.refs_1_, bf16[128,2048]{1,0:T(8,128)(2,1)S(1)} %collective-permute-done.24.refs_3_.refs_2_, ...), custom_call_target="tpu_custom_call" | custom-call | flops 4294967296 | bytes 10485760 | tf_op jit(solution)/shard_map/weight_terms/pallas_call | solution.py:57
  234.6 9.8 %hidden_forward.2 = (f32[1024,1024]{1,0:T(8,128)}, bf16[1024,1024]{1,0:T(8,128)(2,1)}) custom-call(bf16[256,2048]{1,0:T(8,128)(2,1)S(1)} %add_convert_fusion.1.refs_0_.refs_1_, bf16[256,2048]{1,0:T(8,128)(2,1)S(1)} %copy-done.35, bf16[128,2048]{1,0:T(8,128)(2,1)} %collective-permute-done.17.refs_2_.refs_3_, ...), custom_call_target="tpu_custom_call" | custom-call | flops 4294967296 | bytes 14684160 | tf_op jit(solution)/shard_map/hidden_forward/pallas_call | solution.py:57
  246.0 8.9 %weight_terms.5.refs_0_ = bf16[1024,2048]{1,0:T(8,128)(2,1)} custom-call(bf16[1024,1024]{1,0:T(8,128)(2,1)S(1)} %copy-done.12, bf16[256,2048]{1,0:T(8,128)(2,1)S(1)} %bitcast.233, bf16[256,2048]{1,0:T(8,128)(2,1)} %collective-permute-done.14.refs_2_.refs_1_, bf16[128,2048]{1,0:T(8,128)(2,1)S(1)} %collective-permute-done.24.refs_3_.refs_2_, ...), custom_call_target="tpu_custom_call" | custom-call | flops 4294967296 | bytes 10485760 | tf_op jit(solution)/shard_map/weight_terms/pallas_call | solution.py:57
  282.2 10.7 %hidden_backward.2 = (bf16[1024,1024]{1,0:T(8,128)(2,1)}, f32[1,1024]{1,0:T(1,128)S(1)}) custom-call(bf16[256,2048]{1,0:T(8,128)(2,1)S(1)} %bitcast.234, bf16[256,2048]{1,0:T(8,128)(2,1)} %collective-permute-done.14.refs_2_.refs_1_, bf16[128,2048]{1,0:T(8,128)(2,1)S(1)} %copy-done.43, bf16[128,2048]{1,0:T(8,128)(2,1)S(1)} %copy-done.45, ...), custom_call_target="tpu_custom_call" | custom-call | flops 4294967296 | bytes 14684160 | tf_op jit(solution)/shard_map/hidden_backward/pallas_call | solution.py:57
  292.8 7.1 %collective-permute-done.33 = bf16[128,2048]{0,1:T(8,128)(2,1)S(1)} collective-permute-done((bf16[128,2048]{0,1:T(8,128)(2,1)S(1)}, bf16[128,2048]{0,1:T(8,128)(2,1)S(1)}, u32[]{:S(2)}, u32[]{:S(2)}) %collective-permute-start.33) | collective-permute-done | bytes 524320 | tf_op jit(solution)/shard_map/ppermute | solution.py:473
  302.1 11.0 %hidden_backward.3 = (bf16[1024,1024]{1,0:T(8,128)(2,1)S(1)}, f32[1,1024]{1,0:T(1,128)S(1)}) custom-call(bf16[256,2048]{1,0:T(8,128)(2,1)S(1)} %bitcast.235, bf16[256,2048]{1,0:T(8,128)(2,1)} %collective-permute-done.14.refs_2_.refs_1_, bf16[128,2048]{1,0:T(8,128)(2,1)S(1)} %copy-done.43, bf16[128,2048]{1,0:T(8,128)(2,1)S(1)} %copy-done.46, ...), custom_call_target="tpu_custom_call" | custom-call | flops 4294967296 | bytes 14684160 | tf_op jit(solution)/shard_map/hidden_backward/pallas_call | solution.py:57
  314.4 14.6 %hidden_sum.2 = (f32[256,2048]{1,0:T(8,128)S(1)}, bf16[128,2048]{1,0:T(8,128)(2,1)}, bf16[128,2048]{1,0:T(8,128)(2,1)}, bf16[128,2048]{1,0:T(8,128)(2,1)S(1)}, b...) custom-call(bf16[1024,1024]{1,0:T(8,128)(2,1)} %get-tuple-element.201.refs_0_, ...), custom_call_target="tpu_custom_call" | custom-call | flops 8589934592 | bytes 17825792 | tf_op jit(solution)/shard_map/hidden_sum/pallas_call | solution.py:57
  340.6 7.5 %collective-permute-done.36 = bf16[128,2048]{1,0:T(8,128)(2,1)} collective-permute-done((bf16[128,2048]{1,0:T(8,128)(2,1)}, bf16[128,2048]{1,0:T(8,128)(2,1)}, u32[]{:S(2)}, u32[]{:S(2)}) %collective-permute-start.36) | collective-permute-done | bytes 524320 | tf_op jit(solution)/shard_map/ppermute | solution.py:473
  350.6 6.8 %collective-permute-done.38 = bf16[128,2048]{1,0:T(8,128)(2,1)} collective-permute-done((bf16[128,2048]{1,0:T(8,128)(2,1)}, bf16[128,2048]{1,0:T(8,128)(2,1)}, u32[]{:S(2)}, u32[]{:S(2)}) %collective-permute-start.38) | collective-permute-done | bytes 524320 | tf_op jit(solution)/shard_map/ppermute | solution.py:473
  359.6 18.8 %collective-permute-done.40.refs_3_ = bf16[256,2048]{1,0:T(8,128)(2,1)} collective-permute-done((bf16[256,2048]{1,0:T(8,128)(2,1)}, bf16[256,2048]{1,0:T(8,128)(2,1)}, u32[]{:S(2)}, u32[]{:S(2)}) %collective-permute-start.40) | collective-permute-done | bytes 1048608 | tf_op jit(solution)/shard_map/ppermute | solution.py:564
  380.0 8.6 %weight_terms.6 = bf16[1024,2048]{1,0:T(8,128)(2,1)} custom-call(bf16[1024,1024]{1,0:T(8,128)(2,1)S(1)} %copy-done.49, bf16[256,2048]{1,0:T(8,128)(2,1)S(1)} %copy-done.16, bf16[256,2048]{1,0:T(8,128)(2,1)S(1)} %copy-done.36, bf16[128,2048]{1,0:T(8,128)(2,1)} %collective-permute-done.17.refs_2_.refs_3_, ...), custom_call_target="tpu_custom_call" | custom-call | flops 4294967296 | bytes 10485760 | tf_op jit(solution)/shard_map/weight_terms/pallas_call | solution.py:57
  407.7 8.7 %weight_terms.7.refs_0_ = bf16[1024,2048]{1,0:T(8,128)(2,1)} custom-call(bf16[1024,1024]{1,0:T(8,128)(2,1)S(1)} %copy-done.47, bf16[256,2048]{1,0:T(8,128)(2,1)S(1)} %copy-done.17, bf16[256,2048]{1,0:T(8,128)(2,1)S(1)} %copy-done.37, bf16[128,2048]{1,0:T(8,128)(2,1)} %collective-permute-done.17.refs_2_.refs_3_, ...), custom_call_target="tpu_custom_call" | custom-call | flops 4294967296 | bytes 10485760 | tf_op jit(solution)/shard_map/weight_terms/pallas_call | solution.py:57
  420.2 6.3 %add_terms.11 = bf16[512,2048]{1,0:T(8,128)(2,1)} custom-call(bf16[1024,2048]{1,0:T(8,128)(2,1)S(1)} %copy-done.3, bf16[1024,2048]{1,0:T(8,128)(2,1)} %collective-permute-done.41.refs_1_), custom_call_target="tpu_custom_call" | custom-call | bytes 6291456 | tf_op jit(solution)/shard_map/add_terms/pallas_call | solution.py:126
  434.6 14.0 %hidden_sum.3 = (f32[256,2048]{1,0:T(8,128)S(1)}, bf16[256,2048]{1,0:T(8,128)(2,1)}, bf16[256,2048]{1,0:T(8,128)(2,1)}, bf16[256,2048]{1,0:T(8,128)(2,1)}) custom-call(bf16[1024,1024]{1,0:T(8,128)(2,1)S(1)} %copy-done.13, bf16[1024,1024]{1,0:T(8,128)(2,1)S(1)} %copy-done.11, bf16[1024,2048]{1,0:T(8,128)(2,1)} %join_rows.3.refs_2_, ...), custom_call_target="tpu_custom_call" | custom-call | tf_op jit(solution)/shard_map/hidden_sum/pallas_call | solution.py:57
  462.9 12.8 %collective-permute-done.42 = bf16[256,2048]{1,0:T(8,128)(2,1)} collective-permute-done((bf16[256,2048]{1,0:T(8,128)(2,1)}, bf16[256,2048]{1,0:T(8,128)(2,1)}, u32[]{:S(2)}, u32[]{:S(2)}) %collective-permute-start.42) | collective-permute-done | bytes 1048608 | tf_op jit(solution)/shard_map/ppermute | solution.py:473
  479.9 6.7 %fusion.21 = bf16[2048,256]{0,1:T(8,128)(2,1)} fusion(bf16[256,2048]{1,0:T(8,128)(2,1)S(1)} %gate.3, bf16[2048,2048]{1,0:T(8,128)(2,1)} %all-gather.3.cloned.1.call-done), kind=kOutput, calls=%fused_computation.29 | convolution fusion | flops 2148007936 | bytes 10485760 | tf_op jit(solution)/shard_map/dot_general | solution.py:854
  490.2 8.2 %fusion = bf16[16,1024,256]{1,2,0:T(8,128)(2,1)S(1)} fusion(f32[16,1024,256]{1,2,0:T(8,128)} %copy-done.59, bf16[16,128,256]{2,1,0:T(8,128)(2,1)S(1)} %bitcast.246, f32[16,256]{1,0:T(8,128)S(1)} %fusion.31, f32[16,256]{1,0:T(8,128)S(1)} %copy-done.126, pred[1024,256]{0,1:T(8,128)(4,1)S(1)} %copy-done.84, bf16[128,256]{1,0:T(8,128)(2,1)S(1)} %copy-done.114, ...), kind=kOutput, calls=%fused_computation.1 | convolution fusion | flops 1095761920 | bytes 26771456 | tf_op jit(solution)/shard_map/dk,hdq->hkq/dot_general | solution.py:861
  498.4 7.5 %fusion.32 = f32[128,1024]{1,0:T(8,128)S(1)} fusion(bf16[16,128,256]{2,1,0:T(8,128)(2,1)S(1)} %bitcast.247, f32[16,1024,256]{1,2,0:T(8,128)} %copy-done.59, f32[16,256]{1,0:T(8,128)S(1)} %copy-done.126, pred[1024,256]{0,1:T(8,128)(4,1)S(1)} %copy-done.84), kind=kOutput, calls=%fused_computation.65 | convolution fusion | flops 1086324736 | bytes 18628608 | tf_op jit(solution)/shard_map/hkq,hdq->dk/dot_general | solution.py:865
  560.2 9.6 %collective-permute-done.68.refs_2_ = bf16[128,2048]{1,0:T(8,128)(2,1)S(1)} collective-permute-done((bf16[128,2048]{1,0:T(8,128)(2,1)S(1)}, bf16[128,2048]{1,0:T(8,128)(2,1)S(1)}, u32[]{:S(2)}, u32[]{:S(2)}) %collective-permute-start.68) | collective-permute-done | bytes 524320 | tf_op jit(solution)/shard_map/ppermute | solution.py:564
  574.8 12.3 %collective-permute-done.69.refs_3_ = bf16[64,2048]{1,0:T(8,128)(2,1)S(1)} collective-permute-done((bf16[64,2048]{1,0:T(8,128)(2,1)S(1)}, bf16[64,2048]{1,0:T(8,128)(2,1)S(1)}, u32[]{:S(2)}, u32[]{:S(2)}) %collective-permute-start.69) | collective-permute-done | bytes 262176 | tf_op jit(solution)/shard_map/ppermute | solution.py:564
  606.1 6.4 %collective-permute-done.63 = f32[22656]{0:T(1024)S(1)} collective-permute-done((f32[22656]{0:T(1024)S(1)}, f32[22656]{0:T(1024)S(1)}, u32[]{:S(2)}, u32[]{:S(2)}) %collective-permute-start.63) | collective-permute-done | bytes 90656 | tf_op jit(solution)/shard_map/ppermute | solution.py:610
  (579 shorter events, 288.2 us)
Async XLA Ops:
  7.2 130.9 %all-gather.3.cloned.1.call-start = ((), (), s32[]{:S(2)}) async-start(), calls=%async_computation | async-start | bytes 8650752 | tf_op jit(solution)/shard_map/all_gather | solution.py:679
  7.9 389.9 %all-gather.5.cloned.1.call-start = ((), (), s32[]{:S(2)}) async-start(), calls=%async_computation.1 | async-start | bytes 5898240 | tf_op jit(solution)/shard_map/all_gather | solution.py:763
  18.6 26.0 %collective-permute-start.3 = (bf16[256,2048]{1,0:T(8,128)(2,1)S(1)}, bf16[256,2048]{1,0:T(8,128)(2,1)}, u32[]{:S(2)}, u32[]{:S(2)}) collective-permute-start(bf16[256,2048]{1,0:T(8,128)(2,1)S(1)} %fusion.23), channel_id=1, source_target_pairs={{1,0},{3,1},{2,3},{0,2},{5,4},{7,5},{6,7},{4,6},{9,8},{11,9},{10,1... | collective-permute-start | bytes 3145736 | tf_op jit(solution)/shard_map/ppermute | solution.py:473
  20.2 25.6 %collective-permute-start.4 = (bf16[256,2048]{1,0:T(8,128)(2,1)S(1)}, bf16[256,2048]{1,0:T(8,128)(2,1)S(1)}, u32[]{:S(2)}, u32[]{:S(2)}) collective-permute-start(bf16[256,2048]{1,0:T(8,128)(2,1)S(1)} %fusion.23), channel_id=1, source_target_pairs={{2,0},{0,1},{1,3},{3,2},{6,4},{4,5},{5,7},{7,6},{10,8},{8,9},{9,11... | collective-permute-start | bytes 3145736 | tf_op jit(solution)/shard_map/ppermute | solution.py:473
  49.6 64.2 %collective-permute-start.20 = (bf16[256,2048]{1,0:T(8,128)(2,1)S(1)}, bf16[256,2048]{1,0:T(8,128)(2,1)S(1)}, u32[]{:S(2)}, u32[]{:S(2)}) collective-permute-start(bf16[256,2048]{1,0:T(8,128)(2,1)S(1)} %copy-done.20), channel_id=1, source_target_pairs={{8,0},{12,4},{0,16},{4,20},{16,24},{20,28},{24,8},{28,12},{9,1},{1... | collective-permute-start | bytes 3145736 | tf_op jit(solution)/shard_map/ppermute | solution.py:481
  72.4 27.2 %collective-permute-start.10 = (bf16[576,256]{1,0:T(8,128)(2,1)}, bf16[576,256]{1,0:T(8,128)(2,1)S(1)}, u32[]{:S(2)}, u32[]{:S(2)}) collective-permute-start(bf16[576,256]{1,0:T(8,128)(2,1)} %fusion.38), channel_id=1, source_target_pairs={{1,0},{3,1},{2,3},{0,2},{5,4},{7,5},{6,7},{4,6},{9,8},{11,9},{10,1... | collective-permute-start | bytes 884744 | tf_op jit(solution)/shard_map/ppermute | solution.py:473
  73.9 25.7 %collective-permute-start.6 = (bf16[576,256]{1,0:T(8,128)(2,1)}, bf16[576,256]{1,0:T(8,128)(2,1)S(1)}, u32[]{:S(2)}, u32[]{:S(2)}) collective-permute-start(bf16[576,256]{1,0:T(8,128)(2,1)} %fusion.37), channel_id=1, source_target_pairs={{2,0},{0,1},{1,3},{3,2},{6,4},{4,5},{5,7},{7,6},{10,8},{8,9},{9,11... | collective-permute-start | bytes 884744 | tf_op jit(solution)/shard_map/ppermute | solution.py:473
  111.8 34.0 %collective-permute-start.14 = (bf16[256,2048]{1,0:T(8,128)(2,1)S(1)}, bf16[256,2048]{1,0:T(8,128)(2,1)}, u32[]{:S(2)}, u32[]{:S(2)}) collective-permute-start(bf16[256,2048]{1,0:T(8,128)(2,1)S(1)} %bitcast.230), channel_id=1, source_target_pairs={{1,0},{3,1},{2,3},{0,2},{5,4},{7,5},{6,7},{4,6},{9,8},{11,9},{10,1... | collective-permute-start | bytes 3145736 | tf_op jit(solution)/shard_map/ppermute | solution.py:473
  113.1 32.7 %collective-permute-start.15 = (bf16[256,2048]{1,0:T(8,128)(2,1)S(1)}, bf16[256,2048]{1,0:T(8,128)(2,1)}, u32[]{:S(2)}, u32[]{:S(2)}) collective-permute-start(bf16[256,2048]{1,0:T(8,128)(2,1)S(1)} %bitcast.231), channel_id=1, source_target_pairs={{2,0},{0,1},{1,3},{3,2},{6,4},{4,5},{5,7},{7,6},{10,8},{8,9},{9,11... | collective-permute-start | bytes 3145736 | tf_op jit(solution)/shard_map/ppermute | solution.py:473
  169.8 31.7 %collective-permute-start.26 = (bf16[1024,2048]{1,0:T(8,128)(2,1)}, bf16[1024,2048]{1,0:T(8,128)(2,1)}, u32[]{:S(2)}, u32[]{:S(2)}) collective-permute-start(bf16[1024,2048]{1,0:T(8,128)(2,1)} %join_rows.2), channel_id=1, source_target_pairs={{0,4},{4,0},{8,12},{12,8},{16,20},{20,16},{24,28},{28,24},{1,5},{5... | collective-permute-start | bytes 12582920 | tf_op jit(solution)/shard_map/ppermute | solution.py:477
  169.9 25.7 %collective-permute-start.22 = (bf16[256,2048]{1,0:T(8,128)(2,1)S(1)}, bf16[256,2048]{1,0:T(8,128)(2,1)}, u32[]{:S(2)}, u32[]{:S(2)}) collective-permute-start(bf16[256,2048]{1,0:T(8,128)(2,1)S(1)} %copy-done.18), channel_id=1, source_target_pairs={{8,0},{12,4},{0,16},{4,20},{16,24},{20,28},{24,8},{28,12},{9,1},{1... | collective-permute-start | bytes 3145736 | tf_op jit(solution)/shard_map/ppermute | solution.py:481
  171.1 24.5 %collective-permute-start.17 = (bf16[128,2048]{1,0:T(8,128)(2,1)}, bf16[128,2048]{1,0:T(8,128)(2,1)}, u32[]{:S(2)}, u32[]{:S(2)}) collective-permute-start(bf16[128,2048]{1,0:T(8,128)(2,1)} %slice.234), channel_id=1, source_target_pairs={{1,0},{3,1},{2,3},{0,2},{5,4},{7,5},{6,7},{4,6},{9,8},{11,9},{10,1... | collective-permute-start | bytes 1572872 | tf_op jit(solution)/shard_map/ppermute | solution.py:473
  195.6 25.8 %collective-permute-start.27 = (bf16[256,2048]{1,0:T(8,128)(2,1)}, bf16[256,2048]{1,0:T(8,128)(2,1)S(1)}, u32[]{:S(2)}, u32[]{:S(2)}) collective-permute-start(bf16[256,2048]{1,0:T(8,128)(2,1)} %collective-permute-done.22.refs_6_.refs_1_), channel_id=1, source_target_pairs={{8,0},{12,4},{0,16},{4,20},{16,24},{20,28},{24,8},{28,12},{9,1},{1... | collective-permute-start | bytes 3145736 | tf_op jit(solution)/shard_map/ppermute | solution.py:481
  231.2 26.6 %collective-permute-start.29 = (bf16[1024,2048]{1,0:T(8,128)(2,1)}, bf16[1024,2048]{1,0:T(8,128)(2,1)S(1)}, u32[]{:S(2)}, u32[]{:S(2)}) collective-permute-start(bf16[1024,2048]{1,0:T(8,128)(2,1)} %weight_terms.4), channel_id=1, source_target_pairs={{0,4},{4,0},{8,12},{12,8},{16,20},{20,16},{24,28},{28,24},{1,5},{5... | collective-permute-start | bytes 12582920 | tf_op jit(solution)/shard_map/ppermute | solution.py:477
  231.3 25.8 %collective-permute-start.30 = (bf16[256,2048]{0,1:T(8,128)(2,1)}, bf16[256,2048]{0,1:T(8,128)(2,1)S(1)}, u32[]{:S(2)}, u32[]{:S(2)}) collective-permute-start(bf16[256,2048]{0,1:T(8,128)(2,1)} %bitcast.26), channel_id=1, source_target_pairs={{1,0},{3,1},{2,3},{0,2},{5,4},{7,5},{6,7},{4,6},{9,8},{11,9},{10,1... | collective-permute-start | bytes 3145736 | tf_op jit(solution)/shard_map/ppermute | solution.py:473
  232.4 25.4 %collective-permute-start.31 = (bf16[256,2048]{0,1:T(8,128)(2,1)}, bf16[256,2048]{0,1:T(8,128)(2,1)S(1)}, u32[]{:S(2)}, u32[]{:S(2)}) collective-permute-start(bf16[256,2048]{0,1:T(8,128)(2,1)} %bitcast.26), channel_id=1, source_target_pairs={{2,0},{0,1},{1,3},{3,2},{6,4},{4,5},{5,7},{7,6},{10,8},{8,9},{9,11... | collective-permute-start | bytes 3145736 | tf_op jit(solution)/shard_map/ppermute | solution.py:473
  233.3 34.2 %collective-permute-start.28 = (bf16[256,2048]{1,0:T(8,128)(2,1)S(1)}, bf16[256,2048]{1,0:T(8,128)(2,1)S(1)}, u32[]{:S(2)}, u32[]{:S(2)}) collective-permute-start(bf16[256,2048]{1,0:T(8,128)(2,1)S(1)} %collective-permute-done.27.refs_7_.refs_2_), channel_id=1, source_target_pairs={{8,0},{12,4},{0,16},{4,20},{16,24},{20,28},{24,8},{28,12},{9,1},{1... | collective-permute-start | bytes 3145736 | tf_op jit(solution)/shard_map/ppermute | solution.py:481
  271.3 30.0 %collective-permute-start.32 = (bf16[1024,2048]{1,0:T(8,128)(2,1)}, bf16[1024,2048]{1,0:T(8,128)(2,1)}, u32[]{:S(2)}, u32[]{:S(2)}) collective-permute-start(bf16[1024,2048]{1,0:T(8,128)(2,1)} %join_rows.3.refs_2_), channel_id=1, source_target_pairs={{0,4},{4,0},{8,12},{12,8},{16,20},{20,16},{24,28},{28,24},{1,5},{5... | collective-permute-start | bytes 12582920 | tf_op jit(solution)/shard_map/ppermute | solution.py:477
  271.4 57.6 %collective-permute-start.35 = (bf16[512,2048]{1,0:T(8,128)(2,1)}, bf16[512,2048]{1,0:T(8,128)(2,1)S(1)}, u32[]{:S(2)}, u32[]{:S(2)}) collective-permute-start(bf16[512,2048]{1,0:T(8,128)(2,1)} %copy-done.9), channel_id=1, source_target_pairs={{0,8},{4,12},{8,0},{12,4},{16,24},{20,28},{24,16},{28,20},{1,9},{5... | collective-permute-start | bytes 6291464 | tf_op jit(solution)/shard_map/ppermute | solution.py:564
  276.9 24.4 %collective-permute-start.34 = (bf16[128,2048]{0,1:T(8,128)(2,1)S(1)}, bf16[128,2048]{0,1:T(8,128)(2,1)S(1)}, u32[]{:S(2)}, u32[]{:S(2)}) collective-permute-start(bf16[128,2048]{0,1:T(8,128)(2,1)S(1)} %slice.195), channel_id=1, source_target_pairs={{2,0},{0,1},{1,3},{3,2},{6,4},{4,5},{5,7},{7,6},{10,8},{8,9},{9,11... | collective-permute-start | bytes 1572872 | tf_op jit(solution)/shard_map/ppermute | solution.py:473
  332.8 45.6 %collective-permute-start.40 = (bf16[256,2048]{1,0:T(8,128)(2,1)}, bf16[256,2048]{1,0:T(8,128)(2,1)}, u32[]{:S(2)}, u32[]{:S(2)}) collective-permute-start(bf16[256,2048]{1,0:T(8,128)(2,1)} %add_terms.10), channel_id=1, source_target_pairs={{0,16},{4,20},{8,24},{12,28},{16,0},{20,4},{24,8},{28,12},{1,17},{... | collective-permute-start | bytes 3145736 | tf_op jit(solution)/shard_map/ppermute | solution.py:564
  388.5 31.6 %collective-permute-start.41 = (bf16[1024,2048]{1,0:T(8,128)(2,1)}, bf16[1024,2048]{1,0:T(8,128)(2,1)}, u32[]{:S(2)}, u32[]{:S(2)}) collective-permute-start(bf16[1024,2048]{1,0:T(8,128)(2,1)} %weight_terms.6), channel_id=1, source_target_pairs={{0,4},{4,0},{8,12},{12,8},{16,20},{20,16},{24,28},{28,24},{1,5},{5... | collective-permute-start | bytes 12582920 | tf_op jit(solution)/shard_map/ppermute | solution.py:477
  397.8 130.3 %collective-permute-start.54 = (bf16[1152,2048]{1,0:T(8,128)(2,1)}, bf16[1152,2048]{1,0:T(8,128)(2,1)}, u32[]{:S(2)}, u32[]{:S(2)}) collective-permute-start(bf16[1152,2048]{1,0:T(8,128)(2,1)} %bitcast.274), channel_id=1, source_target_pairs={{0,4},{4,0},{8,12},{12,8},{16,20},{20,16},{24,28},{28,24},{1,5},{5... | collective-permute-start | bytes 14155784 | tf_op jit(solution)/shard_map/ppermute | solution.py:477
  426.5 51.9 %collective-permute-start.47 = (bf16[512,2048]{1,0:T(8,128)(2,1)}, bf16[512,2048]{1,0:T(8,128)(2,1)}, u32[]{:S(2)}, u32[]{:S(2)}) collective-permute-start(bf16[512,2048]{1,0:T(8,128)(2,1)} %add_terms.11), channel_id=1, source_target_pairs={{0,8},{4,12},{8,0},{12,4},{16,24},{20,28},{24,16},{28,20},{1,9},{5... | collective-permute-start | bytes 6291464 | tf_op jit(solution)/shard_map/ppermute | solution.py:564
  449.9 25.7 %collective-permute-start.42 = (bf16[256,2048]{1,0:T(8,128)(2,1)}, bf16[256,2048]{1,0:T(8,128)(2,1)}, u32[]{:S(2)}, u32[]{:S(2)}) collective-permute-start(bf16[256,2048]{1,0:T(8,128)(2,1)} %get-tuple-element.204), channel_id=1, source_target_pairs={{2,0},{0,1},{1,3},{3,2},{6,4},{4,5},{5,7},{7,6},{10,8},{8,9},{9,11... | collective-permute-start | bytes 3145736 | tf_op jit(solution)/shard_map/ppermute | solution.py:473
  451.8 55.5 %collective-permute-start.43 = (bf16[256,2048]{1,0:T(8,128)(2,1)}, bf16[256,2048]{1,0:T(8,128)(2,1)}, u32[]{:S(2)}, u32[]{:S(2)}) collective-permute-start(bf16[256,2048]{1,0:T(8,128)(2,1)} %get-tuple-element.205), channel_id=1, source_target_pairs={{3,0},{2,1},{0,3},{1,2},{7,4},{6,5},{4,7},{5,6},{11,8},{10,9},{8,1... | collective-permute-start | bytes 3145736 | tf_op jit(solution)/shard_map/ppermute | solution.py:473
  453.2 57.7 %collective-permute-start.44 = (bf16[256,2048]{1,0:T(8,128)(2,1)}, bf16[256,2048]{1,0:T(8,128)(2,1)}, u32[]{:S(2)}, u32[]{:S(2)}) collective-permute-start(bf16[256,2048]{1,0:T(8,128)(2,1)} %get-tuple-element.206), channel_id=1, source_target_pairs={{1,0},{3,1},{2,3},{0,2},{5,4},{7,5},{6,7},{4,6},{9,8},{11,9},{10,1... | collective-permute-start | bytes 3145736 | tf_op jit(solution)/shard_map/ppermute | solution.py:473
  475.7 36.3 %collective-permute-start.64 = (bf16[512,256]{1,0:T(8,128)(2,1)}, bf16[512,256]{1,0:T(8,128)(2,1)}, u32[]{:S(2)}, u32[]{:S(2)}) collective-permute-start(bf16[512,256]{1,0:T(8,128)(2,1)} %bitcast.69), channel_id=1, source_target_pairs={{1,0},{3,1},{2,3},{0,2},{5,4},{7,5},{6,7},{4,6},{9,8},{11,9},{10,1... | collective-permute-start | bytes 786440 | tf_op jit(solution)/shard_map/ppermute | solution.py:473
  478.3 34.6 %collective-permute-start.65 = (bf16[512,256]{1,0:T(8,128)(2,1)}, bf16[512,256]{1,0:T(8,128)(2,1)}, u32[]{:S(2)}, u32[]{:S(2)}) collective-permute-start(bf16[512,256]{1,0:T(8,128)(2,1)} %bitcast.68), channel_id=1, source_target_pairs={{3,0},{2,1},{0,3},{1,2},{7,4},{6,5},{4,7},{5,6},{11,8},{10,9},{8,1... | collective-permute-start | bytes 786440 | tf_op jit(solution)/shard_map/ppermute | solution.py:473
  510.9 46.4 %collective-permute-start.56 = (bf16[256,2048]{1,0:T(8,128)(2,1)S(1)}, bf16[256,2048]{1,0:T(8,128)(2,1)S(1)}, u32[]{:S(2)}, u32[]{:S(2)}) collective-permute-start(bf16[256,2048]{1,0:T(8,128)(2,1)S(1)} %add_terms.12), channel_id=1, source_target_pairs={{0,16},{4,20},{8,24},{12,28},{16,0},{20,4},{24,8},{28,12},{1,17},{... | collective-permute-start | bytes 3145736 | tf_op jit(solution)/shard_map/ppermute | solution.py:564
  526.1 27.9 %collective-permute-start.67 = (bf16[4,64,2048]{2,1,0:T(8,128)(2,1)S(1)}, bf16[4,64,2048]{2,1,0:T(8,128)(2,1)S(1)}, u32[]{:S(2)}, u32[]{:S(2)}) collective-permute-start(bf16[4,64,2048]{2,1,0:T(8,128)(2,1)S(1)} %get-tuple-element.263), channel_id=1, source_target_pairs={{0,4},{4,0},{8,12},{12,8},{16,20},{20,16},{24,28},{28,24},{1,5},{5... | collective-permute-start | bytes 3145736 | tf_op jit(solution)/shard_map/ppermute | solution.py:477
  557.3 31.5 %collective-permute-start.57 = (bf16[144,2048]{1,0:T(8,128)(2,1)S(1)}, bf16[144,2048]{1,0:T(8,128)(2,1)S(1)}, u32[]{:S(2)}, u32[]{:S(2)}) collective-permute-start(bf16[144,2048]{1,0:T(8,128)(2,1)S(1)} %add_convert_fusion.2), channel_id=1, source_target_pairs={{0,8},{4,12},{8,0},{12,4},{16,24},{20,28},{24,16},{28,20},{1,9},{5... | collective-permute-start | bytes 1769480 | tf_op jit(solution)/shard_map/ppermute | solution.py:564
  (182 other events, 2475.5 us)
Sparse Core Ops, SparseCore 0:
  10.9 101.4 all-gather.2
  271.5 63.0 all-gather.4
